TPU v7x, 32 devices: a whole 2x2x4 slice. The times are simulated.
32 devices in a mesh: seed: 4 (over z), dp: 8 (over y, x, core).
Axes of the slice: x: 2, y: 2, z: 4, core: 2. Of those that a mesh axis runs over, the one named last changes fastest.
Arguments:
- states: float32 [4, 17, 32768], P('seed', None, 'dp'), may hold values from -6 to 6
- actions: float32 [4, 6, 32768], P('seed', None, 'dp'), may hold values from -0.95 to 0.95
- rewards: float32 [4, 32768], P('seed', 'dp'), may hold values from -24 to 24
- next_states: float32 [4, 17, 32768], P('seed', None, 'dp'), may hold values from -6 to 6
- dones: int32 [4, 32768], P('seed', 'dp'), may hold values 0 or 1
- noise_now: float32 [4, 6, 32768], P('seed', None, 'dp'), may hold values from -4 to 4
- noise_next: float32 [4, 6, 32768], P('seed', None, 'dp'), may hold values from -4 to 4
- probs: float32 [4, 32768], P('seed', 'dp'), may hold values from 1e-06 to 4.8e-05
- valid_counts: int32 [4, 8], P('seed', 'dp'), may hold values from 1 to 4096, as said below
- owners: int32 [4, 32768], P('seed', 'dp'), may hold values from 0 to 7, as said below
- slots: int32 [4, 32768], P('seed', 'dp'), may hold values from 0 to 4095, as said below
- old_priorities: float32 [4, 32768], P('seed', 'dp'), may hold values from 0.01 to 2
- actor_w1: float32 [4, 256, 17], P('seed'), may hold values from -1.5 to 1.5
- actor_b1: float32 [4, 256], P('seed'), may hold values from -1.5 to 1.5
- actor_w2: float32 [4, 256, 256], P('seed'), may hold values from -0.375 to 0.375
- actor_b2: float32 [4, 256], P('seed'), may hold values from -1.5 to 1.5
- actor_w3: float32 [4, 12, 256], P('seed'), may hold values from -0.375 to 0.375
- actor_b3: float32 [4, 12], P('seed'), may hold values from -1.5 to 1.5
- critic_w1: float32 [4, 2, 256, 23], P('seed'), may hold values from -1.25 to 1.25
- critic_b1: float32 [4, 2, 256], P('seed'), may hold values from -1.5 to 1.5
- critic_w2: float32 [4, 2, 256, 256], P('seed'), may hold values from -0.375 to 0.375
- critic_b2: float32 [4, 2, 256], P('seed'), may hold values from -1.5 to 1.5
- critic_w3: float32 [4, 2, 256], P('seed'), may hold values from -0.375 to 0.375
- critic_b3: float32 [4, 2], P('seed'), may hold values from -2 to 2
- target_w1: float32 [4, 2, 256, 23], P('seed'), may hold values from -1.25 to 1.25
- target_b1: float32 [4, 2, 256], P('seed'), may hold values from -1.5 to 1.5
- target_w2: float32 [4, 2, 256, 256], P('seed'), may hold values from -0.375 to 0.375
- target_b2: float32 [4, 2, 256], P('seed'), may hold values from -1.5 to 1.5
- target_w3: float32 [4, 2, 256], P('seed'), may hold values from -0.375 to 0.375
- target_b3: float32 [4, 2], P('seed'), may hold values from -2 to 2
- log_alpha: float32 [4], P('seed'), may hold values from -2.5 to -0.5
Outputs:
- grad_actor_w1: float32 [4, 256, 17], P('seed', 'dp')
- grad_actor_b1: float32 [4, 256], P('seed', 'dp')
- grad_actor_w2: float32 [4, 256, 256], P('seed', 'dp')
- grad_actor_b2: float32 [4, 256], P('seed', 'dp')
- grad_actor_w3: float32 [4, 12, 256], P('seed', None, 'dp')
- grad_actor_b3: float32 [4, 12], P('seed')
- grad_critic_w1: float32 [4, 2, 256, 23], P('seed', None, 'dp')
- grad_critic_b1: float32 [4, 2, 256], P('seed', None, 'dp')
- grad_critic_w2: float32 [4, 2, 256, 256], P('seed', None, 'dp')
- grad_critic_b2: float32 [4, 2, 256], P('seed', None, 'dp')
- grad_critic_w3: float32 [4, 2, 256], P('seed', None, 'dp')
- grad_critic_b3: float32 [4, 2], P('seed')
- grad_log_alpha: float32 [4], P('seed')
- new_priorities: float32 [4, 32768], P('seed', 'dp')
- max_priority: float32 [], replicated
Inputs may be any that keep to these rules, and one draw needn't show every extreme that they name: `valid_counts`: some device of each agent has all 4096 rows valid. `owners`: the 4096 rows of each device name every owner exactly 512 times. Within one agent, rows that name the same owner hold distinct slots, and every slot of every owner is named.
All inputs are finite; a program needn't handle non-finite values. No bound on the sum of `dones` on one device may be relied on, other than what follows from the above.
Results may differ from a plain program's by a relative error of at most 0.0001.
Values sent between devices are 32-bit elements; how exact they have to be, the bound alone decides.
No kernel may reach another device: no remote copies, remote signals or barrier semaphores. Data moves between devices by JAX's collectives and lax.ppermute only.
A program may use at most 128 MiB of HBM per device.

v0:
```python
import math

import jax
import jax.numpy as jnp
from jax import lax
from jax.sharding import PartitionSpec as P

HIGH = lax.Precision.HIGHEST
GAMMA = 0.99
STD_LO = -5.0
STD_HI = 2.0
ENTROPY_AIM = -6.0
SOFT_TEMP = 0.1
BETA = 0.4
PRIO_EXP = 0.6
PRIO_EPS = 0.001
HALF_LOG_TAU = 0.5 * math.log(2.0 * math.pi)
LOG_TWO = math.log(2.0)


def dense(weight, inputs, bias):
    return jnp.dot(weight, inputs, precision=HIGH) + bias[:, None]


def actor_head(params, observe):
    w_one, b_one, w_two, b_two, w_out, b_out = params
    hidden = jax.nn.silu(dense(w_one, observe, b_one))
    hidden = jax.nn.silu(dense(w_two, hidden, b_two))
    result = dense(w_out, hidden, b_out)
    half = result.shape[0] // 2
    log_std = STD_LO + 0.5 * (STD_HI - STD_LO) * (jnp.tanh(result[half:]) + 1.0)
    return (result[:half], log_std)


def squash(means, log_std, noise):
    pre = means + jnp.exp(log_std) * noise
    action = jnp.tanh(pre)
    log_jac = 2.0 * (LOG_TWO - pre - jax.nn.softplus(-2.0 * pre))
    logp = jnp.sum(-0.5 * noise * noise - log_std - HALF_LOG_TAU - log_jac, axis=0)
    return (action, logp)


def critic_value(params, index, observe, action):
    w_one, b_one, w_two, b_two, w_out, b_out = params
    joined = jnp.concatenate([observe, action], axis=0)
    hidden = jax.nn.silu(dense(w_one[index], joined, b_one[index]))
    hidden = jax.nn.silu(dense(w_two[index], hidden, b_two[index]))
    return jnp.dot(w_out[index], hidden, precision=HIGH) + b_out[index]


def soft_min(first, second):
    return -SOFT_TEMP * jnp.logaddexp(-first / SOFT_TEMP, -second / SOFT_TEMP)


def place_rows(payload, keys, targets):
    rows = keys.shape[0]
    block = math.gcd(rows, 512)
    count = rows // block
    value_blocks = jnp.transpose(payload.reshape(payload.shape[0], count, block), (1, 0, 2))
    key_blocks = keys.reshape(count, block)

    def step(total, parts):
        values, found = parts
        picks = (found[:, None] == targets[None, :]).astype(jnp.float32)
        return (total + jnp.dot(values, picks, precision=HIGH), None)

    start = jnp.zeros((payload.shape[0], targets.shape[0]), jnp.float32)
    total, _ = lax.scan(step, start, (value_blocks, key_blocks))
    return total


def shards(
    states,
    actions,
    rewards,
    next_states,
    dones,
    noise_now,
    noise_next,
    probs,
    valid_counts,
    owners,
    slots,
    old_priorities,
    actor_w1,
    actor_b1,
    actor_w2,
    actor_b2,
    actor_w3,
    actor_b3,
    critic_w1,
    critic_b1,
    critic_w2,
    critic_b2,
    critic_w3,
    critic_b3,
    target_w1,
    target_b1,
    target_w2,
    target_b2,
    target_w3,
    target_b3,
    log_alpha,
):
    actor_p = (actor_w1[0], actor_b1[0], actor_w2[0], actor_b2[0], actor_w3[0], actor_b3[0])
    critic_p = (critic_w1[0], critic_b1[0], critic_w2[0], critic_b2[0], critic_w3[0], critic_b3[0])
    target_p = (target_w1[0], target_b1[0], target_w2[0], target_b2[0], target_w3[0], target_b3[0])
    observe = states[0]
    action = actions[0]
    observe_next = next_states[0]
    rows = observe.shape[1]
    valid = lax.iota(jnp.int32, rows) < valid_counts[0, 0]
    mask = valid.astype(jnp.float32)
    chance = probs[0]
    least = lax.pmin(jnp.min(jnp.where(valid, chance, 1.0)), "dp")
    total = lax.psum(jnp.sum(mask), "dp")
    critic_coef = mask * (least / chance) ** BETA / total
    actor_coef = mask / total
    temper = log_alpha[0]
    alpha = jnp.exp(temper)
    next_mean, next_std = actor_head(actor_p, observe_next)
    next_action, next_logp = squash(next_mean, next_std, noise_next[0])
    target_q = soft_min(
        critic_value(target_p, 0, observe_next, next_action),
        critic_value(target_p, 1, observe_next, next_action),
    )
    target = rewards[0] + GAMMA * (1.0 - dones[0].astype(jnp.float32)) * (
        target_q - alpha * next_logp
    )

    def critic_loss(params):
        first = critic_value(params, 0, observe, action)
        second = critic_value(params, 1, observe, action)
        loss = jnp.sum(critic_coef * 0.5 * ((first - target) ** 2 + (second - target) ** 2))
        return (loss, 0.5 * (first + second) - target)

    loss_q, critic_back, delta = jax.vjp(critic_loss, critic_p, has_aux=True)
    critic_grad = critic_back(jnp.ones_like(loss_q))[0]

    def actor_loss(params):
        means, log_std = actor_head(params, observe)
        fresh, logp = squash(means, log_std, noise_now[0])
        value = soft_min(
            critic_value(critic_p, 0, observe, fresh), critic_value(critic_p, 1, observe, fresh)
        )
        return (jnp.sum(actor_coef * (alpha * logp - value)), logp)

    loss_pi, actor_back, logp_now = jax.vjp(actor_loss, actor_p, has_aux=True)
    actor_grad = actor_back(jnp.ones_like(loss_pi))[0]

    def alpha_loss(value):
        return -jnp.sum(actor_coef * value * (logp_now + ENTROPY_AIM))

    loss_a, alpha_back = jax.vjp(alpha_loss, temper)
    alpha_grad = alpha_back(jnp.ones_like(loss_a))[0]
    critic_one = critic_grad[0][None]
    critic_two = critic_grad[1][None]
    critic_three = critic_grad[2][None]
    critic_four = critic_grad[3][None]
    critic_five = critic_grad[4][None]
    actor_one = actor_grad[0][None]
    actor_two = actor_grad[1][None]
    actor_three = actor_grad[2][None]
    actor_four = actor_grad[3][None]
    actor_five = actor_grad[4][None]
    critic_sums = (
        lax.psum_scatter(critic_one, "dp", scatter_dimension=2, tiled=True),
        lax.psum_scatter(critic_two, "dp", scatter_dimension=2, tiled=True),
        lax.psum_scatter(critic_three, "dp", scatter_dimension=2, tiled=True),
        lax.psum_scatter(critic_four, "dp", scatter_dimension=2, tiled=True),
        lax.psum_scatter(critic_five, "dp", scatter_dimension=2, tiled=True),
    )
    actor_sums = (
        lax.psum_scatter(actor_one, "dp", scatter_dimension=1, tiled=True),
        lax.psum_scatter(actor_two, "dp", scatter_dimension=1, tiled=True),
        lax.psum_scatter(actor_three, "dp", scatter_dimension=1, tiled=True),
        lax.psum_scatter(actor_four, "dp", scatter_dimension=1, tiled=True),
        lax.psum_scatter(actor_five, "dp", scatter_dimension=2, tiled=True),
    )
    actor_bias, critic_bias, alpha_sum = lax.psum((actor_grad[5], critic_grad[5], alpha_grad), "dp")
    actor_scale = jnp.float32(1.0)
    critic_scale = jnp.float32(1.0)
    priority = (jnp.abs(delta) + PRIO_EPS) ** PRIO_EXP
    peers = lax.axis_size("dp")
    share = rows // peers
    owner = owners[0]
    owner_hits = (owner[None, :] == lax.iota(jnp.int32, peers)[:, None]).astype(jnp.int32)
    rank = jnp.sum(owner_hits * (jnp.cumsum(owner_hits, axis=1) - 1), axis=0)
    destination = jnp.where(valid, owner * share + rank, -1)
    payload = jnp.stack([priority, (slots[0] + 1).astype(jnp.float32)])
    outgoing = place_rows(payload, destination, lax.iota(jnp.int32, peers * share))
    incoming = lax.all_to_all(
        outgoing.reshape(2, peers, share), "dp", split_axis=1, concat_axis=1, tiled=True
    )
    flat = incoming.reshape(2, peers * share)
    table = old_priorities[0]
    received = jnp.stack([flat[0], jnp.ones_like(flat[0])])
    landing = place_rows(received, flat[1], lax.iota(jnp.float32, table.shape[0]) + 1.0)
    new_table = table * (1.0 - landing[1]) + landing[0]
    top = lax.pmax(jnp.max(jnp.where(valid, priority, 0.0)), ("seed", "dp"))
    return (
        actor_sums[0] * actor_scale,
        actor_sums[1] * actor_scale,
        actor_sums[2] * actor_scale,
        actor_sums[3] * actor_scale,
        actor_sums[4] * actor_scale,
        (actor_bias * actor_scale)[None],
        critic_sums[0] * critic_scale,
        critic_sums[1] * critic_scale,
        critic_sums[2] * critic_scale,
        critic_sums[3] * critic_scale,
        critic_sums[4] * critic_scale,
        (critic_bias * critic_scale)[None],
        jnp.reshape(alpha_sum * actor_scale, (1,)),
        new_table[None],
        top,
    )


def solution(mesh):
    placed = (
        P("seed", None, "dp"),
        P("seed", None, "dp"),
        P("seed", "dp"),
        P("seed", None, "dp"),
        P("seed", "dp"),
        P("seed", None, "dp"),
        P("seed", None, "dp"),
        P("seed", "dp"),
        P("seed", "dp"),
        P("seed", "dp"),
        P("seed", "dp"),
        P("seed", "dp"),
        P("seed", None, None),
        P("seed", None),
        P("seed", None, None),
        P("seed", None),
        P("seed", None, None),
        P("seed", None),
        P("seed", None, None, None),
        P("seed", None, None),
        P("seed", None, None, None),
        P("seed", None, None),
        P("seed", None, None),
        P("seed", None),
        P("seed", None, None, None),
        P("seed", None, None),
        P("seed", None, None, None),
        P("seed", None, None),
        P("seed", None, None),
        P("seed", None),
        P("seed"),
    )
    return jax.shard_map(
        shards,
        mesh=mesh,
        in_specs=placed,
        out_specs=(
            P("seed", "dp", None),
            P("seed", "dp"),
            P("seed", "dp", None),
            P("seed", "dp"),
            P("seed", None, "dp"),
            P("seed", None),
            P("seed", None, "dp", None),
            P("seed", None, "dp"),
            P("seed", None, "dp", None),
            P("seed", None, "dp"),
            P("seed", None, "dp"),
            P("seed", None),
            P("seed"),
            P("seed", "dp"),
            P(),
        ),
        check_vma=False,
    )
```

profile of v0, /device:TPU:0, one launch (start us, length us, event | category | flops | bytes accessed | tf_op | source)
XLA Modules:
  0.0 557.5 jit_solution(7934676909340217647)
XLA Ops:
  14.1 15.8 %psum.28 = f32[]{:T(128)} all-reduce(f32[]{:T(128)} %convert_reduce_fusion), channel_id=1, replica_groups=mesh['seed'=4,'dp'=8] {'dp'}, use_global_device_ids=true, to_apply=%region_1.2 | all-reduce | flops 1 | bytes 8 | tf_op jit(solution)/shard_map/psum | solution.py:116
  35.2 5.1 fusion.33
  47.6 5.1 fusion.31
  59.6 5.1 fusion.29
  71.9 7.8 %convolution_bitcast_fusion.5 = f32[256,4096]{1,0:T(8,128)S(1)} fusion(f32[256,4096]{1,0:T(8,128)} %copy-done.45, f32[256]{0:T(256)S(1)} %bitcast.437, f32[4096]{0:T(1024)S(1)} %get-tuple-element.190, f32[1,2,256,256]{3,2,1,0:T(8,128)S(1)} %copy-done.37), kind=kOutput, calls=%fused_computation.54 | convolution fusion | flops 3231711232 | bytes 8668160 | tf_op jit(solution)/shard_map/transpose(jvp())/dot_general | solution.py:22
  83.5 5.6 convolution_bitcast_fusion.4
  98.8 6.8 %fusion.284 = (f32[256]{0:T(256)S(1)}, f32[256,4096]{1,0:T(8,128)}) fusion(f32[256,4096]{1,0:T(8,128)S(1)} %copy-done.3, f32[256,4096]{1,0:T(8,128)S(1)} %get-tuple-element.209, f32[1,256,256]{2,1,0:T(8,128)S(1)} %copy-done), kind=kOutput, calls=%fused_computation.387 | convolution fusion | flops 3231710976 | bytes 12846080 | tf_op jit(solution)/shard_map/transpose(jvp())/dot_general | solution.py:22
  121.9 7.0 %fusion.27 = f32[256,4096]{1,0:T(8,128)S(1)} fusion(f32[256]{0:T(256)S(1)} %bitcast.452, f32[256,4096]{1,0:T(8,128)} %fusion.28, f32[1,2,256,256]{3,2,1,0:T(8,128)S(1)} %copy-done.37), kind=kOutput, calls=%fused_computation.48 | convolution fusion | flops 3226468352 | bytes 8651776 | tf_op jit(solution)/shard_map/jvp()/dot_general | solution.py:22
  132.6 5.1 fusion.20
  141.5 5.3 fusion.26
  153.8 5.3 fusion.24
  165.8 5.6 fusion.22
  181.5 32.4 %while.22 = (s32[]{:T(128)}, f32[2,4096]{1,0:T(2,128)}, f32[8,2,512]{2,1,0:T(2,128)S(1)}, s32[8,512]{1,0:T(8,128)S(1)}, s32[]{:T(128)}, /*index=5*/s32[]{:T(128)}) while((s32[]{:T(128)}, f32[2,4096]{1,0:T(2,128)}, f32[8,2,512]{2,1,0:T(2,128)S(1)}, s32[8,512]{1,0:T(8,128)S(1)}, s32[]{:T(128)}, /*index=5*/s32[]{:T(128)}) %tuple.86), condition=%wide.region_33.34_spmd.clone, body=%wide.region_32.33_spmd.clone.sunk | while | flops 52445184 | bytes 75863 | solution.py:68
  218.7 15.1 %pmin.7 = f32[]{:T(128)} all-reduce(f32[]{:T(128)} %select_reduce_fusion.2), channel_id=1, replica_groups=mesh['seed'=4,'dp'=8] {'dp'}, use_global_device_ids=true, to_apply=%region_12.13 | all-reduce | flops 1 | bytes 8 | tf_op jit(solution)/shard_map/pmin | solution.py:115
  237.1 5.9 %fusion.136 = f32[1,256]{1,0:T(1,128)S(1)} fusion(f32[4096,1]{0,1:T(1,128)S(1)} %bitcast.400, f32[256,4096]{1,0:T(8,128)} %copy-done.13), kind=kOutput, calls=%fused_computation.184 | convolution fusion | flops 16777216 | bytes 4211712 | tf_op jit(solution)/shard_map/transpose(jvp())/dot_general | solution.py:48
  247.4 5.7 %fusion.265 = (f32[256]{0:T(256)S(1)}, f32[256]{0:T(256)S(1)}) fusion(f32[256,4096]{1,0:T(8,128)} %copy-done.15, f32[256]{0:T(256)S(1)} %bitcast.442, f32[4096]{0:T(1024)S(1)} %get-tuple-element.189, f32[256,4096]{1,0:T(8,128)} %copy-done.13, f32[256]{0:T(256)S(1)} %bitcast.438, f32[4096]{0:T(1024)S(1)} %get-tuple-element.175), kind=kLoop, calls=%fused_computation.373 | loop fusion | flops 23068160 | bytes 8425472 | tf_op jit(solution)/shard_map/transpose(jvp())/reduce_sum | solution.py:22
  254.0 10.9 %fusion.287 = (f32[256]{0:T(256)S(1)}, f32[256,4096]{1,0:T(8,128)}) fusion(f32[256,4096]{1,0:T(8,128)} %fusion.28, f32[1,2,256,256]{3,2,1,0:T(8,128)S(1)} %copy-done.37, f32[256,4096]{1,0:T(8,128)} %copy-done.13, f32[4096]{0:T(1024)S(1)} %get-tuple-element.175, f32[256]{0:T(256)S(1)} %bitcast.439), kind=kOutput, calls=%fused_computation.390 | convolution fusion | flops 3242196736 | bytes 12863488 | tf_op jit(solution)/shard_map/transpose(jvp())/dot_general | solution.py:22
  265.0 8.5 %fusion.286 = (f32[256]{0:T(256)S(1)}, f32[256,4096]{1,0:T(8,128)}) fusion(f32[256,4096]{1,0:T(8,128)S(1)} %copy-done.8, f32[1,2,256,256]{3,2,1,0:T(8,128)S(1)} %copy-done.37, f32[256,4096]{1,0:T(8,128)S(1)} %copy-done.17, f32[4096]{0:T(1024)S(1)} %get-tuple-element.189, f32[256]{0:T(256)S(1)} %bitcast.443), kind=kOutput, calls=%fused_computation.389 | convolution fusion | flops 3242196736 | bytes 12863488 | tf_op jit(solution)/shard_map/transpose(jvp())/dot_general | solution.py:22
  274.4 5.9 %convolution_bitcast_fusion.11 = f32[256,12]{1,0:T(8,128)} fusion(f32[256,4096]{1,0:T(8,128)} %copy-done.43, f32[6,4096]{1,0:T(8,128)S(1)} %get-tuple-element.178, f32[6,4096]{1,0:T(8,128)S(1)} %get-tuple-element.179), kind=kOutput, calls=%fused_computation.181 | convolution fusion | flops 155238400 | bytes 4403200 | tf_op jit(solution)/shard_map/transpose(jvp())/dot_general | solution.py:22
  280.3 5.8 %fusion.194 = f32[256,17]{1,0:T(8,128)} fusion(f32[256,4096]{1,0:T(8,128)} %get-tuple-element.207, f32[1,17,4096]{2,0,1:T(1,128)S(1)} %copy-done.18), kind=kOutput, calls=%fused_computation.264 | convolution fusion | flops 213909504 | bytes 4490240 | tf_op jit(solution)/shard_map/transpose(jvp())/dot_general | solution.py:22
  286.7 5.7 %convolution_bitcast_fusion.13 = f32[1,256,23]{1,2,0:T(8,128)S(1)} fusion(f32[256,4096]{1,0:T(8,128)} %get-tuple-element.213, f32[6,4096]{1,0:T(8,128)S(1)} %bitcast.389, f32[17,4096]{1,0:T(8,128)S(1)} %bitcast.383), kind=kOutput, calls=%fused_computation.183 | convolution fusion | flops 289501184 | bytes 4594688 | tf_op jit(solution)/shard_map/transpose(jvp())/dot_general | solution.py:22
  296.9 8.5 %convolution_bitcast_fusion.10 = f32[1,256,256]{2,1,0:T(8,128)} fusion(f32[256,4096]{1,0:T(8,128)} %copy-done.42, f32[256,4096]{1,0:T(8,128)} %copy-done.2), kind=kOutput, calls=%fused_computation.180 | convolution fusion | flops 3225419776 | bytes 8650752 | tf_op jit(solution)/shard_map/transpose(jvp())/dot_general | solution.py:22
  305.6 9.5 %convolution_bitcast_fusion.8 = f32[1,256,256]{2,1,0:T(8,128)S(1)} fusion(f32[256,4096]{1,0:T(8,128)} %fusion.21, f32[256,4096]{1,0:T(8,128)} %copy-done.15, f32[4096]{0:T(1024)S(1)} %get-tuple-element.189, f32[256]{0:T(256)S(1)} %bitcast.444), kind=kOutput, calls=%fused_computation.178 | convolution fusion | flops 3235905536 | bytes 8668160 | tf_op jit(solution)/shard_map/transpose(jvp())/dot_general | solution.py:22
  315.1 6.0 %convolution_bitcast_fusion.9 = f32[1,256,256]{2,1,0:T(8,128)S(1)} fusion(f32[256,4096]{1,0:T(8,128)S(1)} %copy-done.6, f32[256,4096]{1,0:T(8,128)S(1)} %copy-done.14, f32[4096]{0:T(1024)S(1)} %get-tuple-element.175, f32[256]{0:T(256)S(1)} %bitcast.440), kind=kOutput, calls=%fused_computation.179 | convolution fusion | flops 3235905536 | bytes 8668160 | tf_op jit(solution)/shard_map/transpose(jvp())/dot_general | solution.py:22
  323.4 39.8 %pmax.7 = f32[]{:T(128)} all-reduce(f32[]{:T(128)} %get-tuple-element.169), channel_id=1, replica_groups=mesh['seed'=4,'dp'=8] {'seed','dp'}, use_global_device_ids=true, to_apply=%region_37.38 | all-reduce | flops 1 | bytes 8 | tf_op jit(solution)/shard_map/pmax | solution.py:200
  363.3 13.5 %all-reduce.15 = (f32[1,12]{1,0:T(1,128)}, f32[1,2]{1,0:T(1,128)}, f32[1]{0:T(128)}) all-reduce(f32[1,12]{1,0:T(1,128)S(1)} %bitcast.457, f32[1,2]{1,0:T(1,128)S(1)} %add_bitcast_fusion.5, f32[1]{0:T(128)} %bitcast.99), channel_id=1, replica_groups=mesh['seed'=4,'dp'=8] {'dp'}, use_global_device_ids=true, to_apply=%region_10.11 | all-reduce | flops 15 | bytes 120 | tf_op jit(solution)/shard_map/psum | solution.py:180
  383.5 18.6 %reduce-scatter.37.cloned.1.call-done = f32[32,12]{1,0:T(8,128)} async-done(((f32[256,12]{1,0:T(8,128)}), f32[32,12]{1,0:T(8,128)}) %reduce-scatter.37.cloned.1.call-update) | async-done | bytes 1552
  403.5 35.0 %reduce-scatter.31.cloned.1.call-done = f32[32,17]{1,0:T(8,128)} async-done(((f32[256,17]{1,0:T(8,128)}), f32[32,17]{1,0:T(8,128)}) %reduce-scatter.31.cloned.1.call-update) | async-done | bytes 2192
  440.0 20.3 %while.23 = (s32[]{:T(128)}, f32[2,4096]{1,0:T(2,128)S(1)}, f32[8,2,512]{2,1,0:T(2,128)S(1)}, f32[8,512]{1,0:T(8,128)S(1)}, s32[]{:T(128)}, /*index=5*/s32[]{:T(128)}) while((s32[]{:T(128)}, f32[2,4096]{1,0:T(2,128)S(1)}, f32[8,2,512]{2,1,0:T(2,128)S(1)}, f32[8,512]{1,0:T(8,128)S(1)}, s32[]{:T(128)}, ...), condition=%wide.region_35.36_spmd.clone, body=%wide.region_34.35_spmd.clone.sunk | while | flops 52449280 | bytes 108631 | solution.py:68
  460.9 14.3 %reduce-scatter.39.cloned.1.call-done = f32[32,46]{1,0:T(8,128)} async-done(((f32[256,46]{1,0:T(8,128)}), f32[32,46]{1,0:T(8,128)}) %reduce-scatter.39.cloned.1.call-update) | async-done | bytes 5904
  476.7 35.8 %reduce-scatter.27.cloned.1.call-done = f32[1,32,256]{2,1,0:T(8,128)} async-done(((f32[1,256,256]{2,1,0:T(8,128)}), f32[1,32,256]{2,1,0:T(8,128)}) %reduce-scatter.27.cloned.1.call-update) | async-done | bytes 32784 | tf_op jit(solution)/shard_map/reduce_scatter | solution.py:176
  512.4 38.0 %reduce-scatter.29.cloned.1.call-done = f32[1,2,32,256]{3,2,1,0:T(8,128)} async-done(((f32[1,2,256,256]{3,2,1,0:T(8,128)}), f32[1,2,32,256]{3,2,1,0:T(8,128)}) %reduce-scatter.29.cloned.1.call-update) | async-done | bytes 65552 | tf_op jit(solution)/shard_map/reduce_scatter | solution.py:169
  (247 shorter events, 177.8 us)
Async XLA Ops:
  7.2 27.9 %copy-start = (f32[1,256,256]{2,1,0:T(8,128)S(1)}, f32[1,256,256]{2,1,0:T(8,128)}, u32[]{:S(2)}) copy-start(f32[1,256,256]{2,1,0:T(8,128)} %param.49) | copy-start | bytes 786436
  7.2 27.9 %copy-start.40 = (f32[1,256]{1,0:T(1,128)S(1)}, f32[1,256]{1,0:T(1,128)}, u32[]{:S(2)}) copy-start(f32[1,256]{1,0:T(1,128)} %param.50) | copy-start | bytes 3076
  7.2 369.6 %reduce-scatter.33.cloned.1.call-start = ((), (), s32[]{:S(2)}) async-start(), calls=%async_computation.14 | async-start | bytes 147456
  71.9 7.9 %copy-start.12 = (f32[256,4096]{1,0:T(8,128)S(1)}, f32[256,4096]{1,0:T(8,128)}, u32[]{:S(2)}) copy-start(f32[256,4096]{1,0:T(8,128)} %copy-done.11) | copy-start | bytes 12582916
  83.5 5.6 copy-start.10
  98.8 6.8 %copy-start.42 = (f32[256,4096]{1,0:T(8,128)}, f32[256,4096]{1,0:T(8,128)S(1)}, u32[]{:S(2)}) copy-start(f32[256,4096]{1,0:T(8,128)S(1)} %get-tuple-element.209) | copy-start | bytes 12582916
  98.8 7.6 %copy-start.23 = (f32[1,6,4096]{2,0,1:T(1,128)S(1)}, f32[1,6,4096]{2,0,1:T(1,128)}, u32[]{:S(2)}) copy-start(f32[1,6,4096]{2,0,1:T(1,128)} %param.36) | copy-start | bytes 294916
  106.5 10.1 %copy-start.19 = (f32[1,17,4096]{2,0,1:T(1,128)S(1)}, f32[1,17,4096]{2,0,1:T(1,128)}, u32[]{:S(2)}) copy-start(f32[1,17,4096]{2,0,1:T(1,128)} %param.38) | copy-start | bytes 835588
  106.5 10.1 %copy-start.22 = (f32[1,256,17]{1,0,2:T(1,128)S(1)}, f32[1,256,17]{1,0,2:T(1,128)}, u32[]{:S(2)}) copy-start(f32[1,256,17]{1,0,2:T(1,128)} %param.47) | copy-start | bytes 52228
  106.5 10.1 %copy-start.31 = (f32[1,256]{1,0:T(1,128)S(1)}, f32[1,256]{1,0:T(1,128)}, u32[]{:S(2)}) copy-start(f32[1,256]{1,0:T(1,128)} %param.48) | copy-start | bytes 3076
  153.8 5.4 copy-start.39
  171.4 6.8 %copy-start.27 = (f32[1,4096]{1,0:T(1,128)S(1)}, f32[1,4096]{1,0:T(1,128)}, u32[]{:S(2)}) copy-start(f32[1,4096]{1,0:T(1,128)} %param.37) | copy-start | bytes 49156
  181.5 35.8 %copy-start.25 = (f32[1,4096]{1,0:T(1,128)S(1)}, f32[1,4096]{1,0:T(1,128)}, u32[]{:S(2)}) copy-start(f32[1,4096]{1,0:T(1,128)} %param.42) | copy-start | bytes 49156
  213.9 226.0 %all-to-all-start = ((f32[2,8,512]{2,0,1:T(2,128)}), f32[2,8,512]{2,0,1:T(2,128)S(1)}, u32[]{:S(2)}, u32[]{:S(2)}) async-start(f32[2,8,512]{2,0,1:T(2,128)} %bitcast.104), calls=%async_computation.2 | async-start | bytes 65536 | tf_op jit(solution)/shard_map/all_to_all | solution.py:192
  217.2 160.9 %reduce-scatter.35.cloned.1.call-start = ((), (), s32[]{:S(2)}) async-start(), calls=%async_computation.15 | async-start | bytes 147456
  218.7 160.8 %reduce-scatter.45.cloned.1.call-start = ((), (), s32[]{:S(2)}) async-start(), calls=%async_computation.20 | async-start | bytes 147456
  237.1 5.9 %copy-start.16 = (f32[256,4096]{1,0:T(8,128)S(1)}, f32[256,4096]{1,0:T(8,128)}, u32[]{:S(2)}) copy-start(f32[256,4096]{1,0:T(8,128)} %copy-done.15) | copy-start | bytes 12582916
  247.4 133.4 %reduce-scatter.43.cloned.1.call-start = ((), (), s32[]{:S(2)}) async-start(), calls=%async_computation.19 | async-start | bytes 147456
  254.0 128.2 %reduce-scatter.41.cloned.1.call-start = ((), (), s32[]{:S(2)}) async-start(), calls=%async_computation.18 | async-start | bytes 147456
  254.0 11.0 %copy-start.8 = (f32[256,4096]{1,0:T(8,128)S(1)}, f32[256,4096]{1,0:T(8,128)}, u32[]{:S(2)}) copy-start(f32[256,4096]{1,0:T(8,128)} %fusion.21) | copy-start | bytes 12582916
  254.0 11.0 %copy-start.17 = (f32[256,4096]{1,0:T(8,128)S(1)}, f32[256,4096]{1,0:T(8,128)}, u32[]{:S(2)}) copy-start(f32[256,4096]{1,0:T(8,128)} %copy-done.15) | copy-start | bytes 12582916
  274.3 6.1 %copy-start.18 = (f32[1,17,4096]{2,0,1:T(1,128)S(1)}, f32[1,17,4096]{2,0,1:T(1,128)}, u32[]{:S(2)}) copy-start(f32[1,17,4096]{2,0,1:T(1,128)} %param.35) | copy-start | bytes 835588
  274.3 127.8 %reduce-scatter.37.cloned.1.call-start = ((), (), s32[]{:S(2)}) async-start(), calls=%async_computation.16 | async-start | bytes 147456
  280.3 158.2 %reduce-scatter.31.cloned.1.call-start = ((), (), s32[]{:S(2)}) async-start(), calls=%async_computation.13 | async-start | bytes 147456
  286.2 189.0 %reduce-scatter.39.cloned.1.call-start = ((), (), s32[]{:S(2)}) async-start(), calls=%async_computation.17 | async-start | bytes 147456
  286.7 5.7 %copy-start.4 = (f32[256,4096]{1,0:T(8,128)S(1)}, f32[256,4096]{1,0:T(8,128)}, u32[]{:S(2)}) copy-start(f32[256,4096]{1,0:T(8,128)} %get-tuple-element.211) | copy-start | bytes 12582916
  296.8 215.6 %reduce-scatter.27.cloned.1.call-start = ((), (), s32[]{:S(2)}) async-start(), calls=%async_computation.11 | async-start | bytes 294912 | tf_op jit(solution)/shard_map/reduce_scatter | solution.py:176
  305.4 245.0 %reduce-scatter.29.cloned.1.call-start = ((), (), s32[]{:S(2)}) async-start(), calls=%async_computation.12 | async-start | bytes 589824 | tf_op jit(solution)/shard_map/reduce_scatter | solution.py:169
  305.6 9.5 %copy-start.6 = (f32[256,4096]{1,0:T(8,128)S(1)}, f32[256,4096]{1,0:T(8,128)}, u32[]{:S(2)}) copy-start(f32[256,4096]{1,0:T(8,128)} %fusion.28) | copy-start | bytes 12582916
  305.6 9.5 %copy-start.14 = (f32[256,4096]{1,0:T(8,128)S(1)}, f32[256,4096]{1,0:T(8,128)}, u32[]{:S(2)}) copy-start(f32[256,4096]{1,0:T(8,128)} %copy-done.13) | copy-start | bytes 12582916
  439.9 110.5 %copy-start.1 = (f32[1,256,256]{2,1,0:T(8,128)S(1)}, f32[1,256,256]{2,1,0:T(8,128)}, u32[]{:S(2)}) copy-start(f32[1,256,256]{2,1,0:T(8,128)} %param.49) | copy-start | bytes 786436
  439.9 20.3 %copy-start.30 = (f32[1,4096]{1,0:T(1,128)S(1)}, f32[1,4096]{1,0:T(1,128)}, u32[]{:S(2)}) copy-start(f32[1,4096]{1,0:T(1,128)} %param.46) | copy-start | bytes 49156
  (27 other events, 104.8 us)
Sparse Core Ops, SparseCore 0:
  106.5 32.7 reduce-scatter.32
  221.3 35.0 reduce-scatter.34
  259.4 33.3 reduce-scatter.44
  295.9 33.3 reduce-scatter.42
  332.2 33.3 reduce-scatter.40
  368.7 33.3 reduce-scatter.36
  405.1 33.3 reduce-scatter.30
  441.8 33.3 reduce-scatter.38
  478.8 33.6 reduce-scatter.26
  516.2 34.1 reduce-scatter.28
where the time goes:
time: 568 us; the launch traced here: 557 us
  matrix products  261 us (46%)
  waiting for transfers between devices  142 us (25%)
  blocking collectives  84.2 us (15%)
  local copies, waits for them, and re-layouts  26.3 us (5%)
  other arithmetic  21.9 us (4%)
  between operations  17.4 us (3%)
    dot_general x33, matrix products, dense(): return jnp.dot(weight, inputs, precision=HIGH) + bias[:, None]  181 us
    unnamed x18, waiting for transfers between devices  68 us
    dot_general x16, matrix products, step(): return (total + jnp.dot(values, picks, precision=HIGH), None)  52.3 us
    pmax x1, blocking collectives, shards(): top = lax.pmax(jnp.max(jnp.where(valid, priority, 0.0)), ('seed', 'dp'))  39.8 us
    reduce_scatter x1, waiting for transfers between devices, shards(): lax.psum_scatter(critic_three, 'dp', scatter_dimension=2, tiled=True)  38 us
    reduce_scatter x1, waiting for transfers between devices, shards(): lax.psum_scatter(actor_three, 'dp', scatter_dimension=1, tiled=True)  35.8 us
    dot_general x8, matrix products, critic_value(): return jnp.dot(w_out[index], hidden, precision=HIGH) + b_out[index]  28 us
    unnamed x116, local copies, waits for them, and re-layouts  20.7 us
  transfers between devices with their start and end apart: 11, of which 5 were waited for; matrix products, arithmetic and copies ran while one was open for 41% of the time, Pallas kernels for 0%

commit v1 on v0

v1 whole, which is shorter than its diff:
```python
import functools
import math

import jax
import jax.numpy as jnp
from jax import lax
from jax.experimental import pallas as pl
from jax.experimental.pallas import tpu as pltpu
from jax.sharding import PartitionSpec as P

F32 = jnp.float32
BF16 = jnp.bfloat16
GAMMA = 0.99
STD_LO = -5.0
STD_HI = 2.0
ENTROPY_AIM = -6.0
SOFT_TEMP = 0.1
BETA = 0.4
PRIO_EXP = 0.6
PRIO_EPS = 0.001
HALF_LOG_TAU = 0.5 * math.log(2.0 * math.pi)
LOG_TWO = math.log(2.0)

LANES = 128
OBS = 17
ACT = 6
HID = 256
JOIN = 24
HEAD = 16
CHUNK = 512
GROUP = CHUNK // LANES
VMEM_LIMIT = 56 * 1024 * 1024


def dot(left, right):
    return jnp.dot(left, right, preferred_element_type=F32)


def dot_t(left, right):
    return lax.dot_general(left, right, (((1,), (1,)), ((), ())), preferred_element_type=F32)


def split(value):
    high = value.astype(BF16)
    low = (value - high.astype(F32)).astype(BF16)
    return high, low


def split_wide(value):
    high = value.astype(BF16).astype(F32)
    return high, value - high


def dot3(weight, value):
    high, low = value
    return dot(weight[0], high) + dot(weight[0], low) + dot(weight[1], high)


def dot3_t(left, right):
    return dot_t(left[0], right[0]) + dot_t(left[0], right[1]) + dot_t(left[1], right[0])


def wide(column):
    return jnp.concatenate([column] * GROUP, axis=1)


def stack_join(value):
    high, low = split_wide(value)
    return jnp.concatenate([high, low, high], axis=0).astype(BF16)


def stack_weight(value):
    high, low = split_wide(value)
    return jnp.transpose(jnp.concatenate([high, high, low], axis=0)).astype(BF16)


def activate(half):
    bent = jnp.tanh(half)
    return bent, half + half * bent


def slope(bent, hidden):
    return (1.0 + hidden) + bent * (1.0 - hidden)


def soft_min(first, second):
    return jnp.minimum(first, second) - SOFT_TEMP * jnp.log(
        1.0 + jnp.exp(-jnp.abs(first - second) / SOFT_TEMP)
    )


def squash(head, noise):
    means, bend = head[:8], jnp.tanh(head[8:])
    log_std = STD_LO + 0.5 * (STD_HI - STD_LO) * (bend + 1.0)
    spread = jnp.exp(log_std) * noise
    pre = means + spread
    action = jnp.tanh(pre)
    size = jnp.abs(pre)
    log_jac = 2.0 * (LOG_TWO - size - jnp.log(1.0 + jnp.exp(-2.0 * size)))
    row = lax.broadcasted_iota(jnp.int32, pre.shape, 0)
    inside = (row >= 1) & (row <= ACT)
    terms = jnp.where(inside, -0.5 * noise * noise - log_std - HALF_LOG_TAU - log_jac, 0.0)
    return action, jnp.sum(terms, axis=0, keepdims=True), spread, bend


def load_rows(ref, count, block):
    blocks = ref.shape[0] // count
    return ref[pl.ds(block, count, stride=blocks), :]


def load_chunk(ref, count, first):
    return jnp.concatenate([load_rows(ref, count, first + g) for g in range(GROUP)], axis=1)


def load_row(ref, first):
    return jnp.concatenate([ref[pl.ds(first + g, 1), :] for g in range(GROUP)], axis=1)


def fill_join(join, obs_ref, act_ref, first):
    join[0:OBS, :] = load_chunk(obs_ref, OBS, first)
    if act_ref is not None:
        join[OBS : OBS + ACT, :] = load_chunk(act_ref, ACT, first)
    join[JOIN - 1 : JOIN, :] = jnp.ones((1, CHUNK), F32)


def with_action(join, action):
    row = lax.broadcasted_iota(jnp.int32, action.shape, 0)
    inside = (row >= 1) & (row <= ACT)
    return jnp.concatenate([join[:16], jnp.where(inside, action, join[16:])], axis=0)


def first_weights(weight_ref, bias_row, index, scratch):
    rows = weight_ref.shape[0]
    scratch[...] = jnp.zeros_like(scratch)
    scratch[0:rows, :] = weight_ref[:, index, :]
    scratch[JOIN - 1 : JOIN, :] = bias_row
    return stack_weight(0.5 * scratch[...])


def store_split(ref, index, value):
    high, low = split(value)
    ref[index, 0] = high
    ref[index, 1] = low


def pair(ref, index):
    return ref[index, 0], ref[index, 1]


def column(row):
    return jnp.transpose(jnp.broadcast_to(row, (LANES, row.shape[1])))


def head_weights(weight_ref, scratch):
    scratch[...] = jnp.zeros_like(scratch)
    scratch[1 : 1 + ACT, :] = weight_ref[0:ACT, 0, :]
    scratch[9 : 9 + ACT, :] = weight_ref[ACT : 2 * ACT, 0, :]
    return scratch[...]


def head_bias(bias_ref):
    row = lax.broadcasted_iota(jnp.int32, (HEAD, LANES), 0)
    out = jnp.zeros((HEAD, LANES), F32)
    for k in range(ACT):
        out = jnp.where(row == 1 + k, bias_ref[0, k], out)
        out = jnp.where(row == 9 + k, bias_ref[0, ACT + k], out)
    return out


def fold(value):
    total = value[:, :LANES]
    for g in range(1, GROUP):
        total = total + value[:, g * LANES : (g + 1) * LANES]
    return total


def valid_lanes(first, count):
    lane = lax.broadcasted_iota(jnp.int32, (1, CHUNK), 1)
    return lane + first * LANES < count


def spread_row(value):
    return jnp.broadcast_to(value, (1, LANES))


def critic_kernel(
    peers,
    count_ref,
    temper_ref,
    actor_b3,
    critic_b3,
    target_b3,
    states,
    actions,
    rewards,
    next_states,
    dones,
    noise_next,
    probs,
    owners,
    slots,
    actor_w1,
    actor_b1,
    actor_w2,
    actor_b2,
    actor_w3,
    critic_w1,
    critic_b1,
    critic_w2,
    critic_b2,
    critic_w3,
    target_w1,
    target_b1,
    target_w2,
    target_b2,
    target_w3,
    send,
    top,
    one,
    two,
    back,
    head,
    bias_two,
    last,
    wide_bias,
    join,
    turn,
    acc_two,
    acc_one,
    acc_side,
    acc_table,
    acc_row,
):
    count = count_ref[0, 0]
    alpha = jnp.exp(temper_ref[0])
    share = HID // peers
    depth = acc_table.shape[0] // peers
    one[0] = first_weights(actor_w1, actor_b1[...], 0, turn)
    for k in range(2):
        one[1 + k] = first_weights(target_w1, target_b1[k : k + 1, :], k, turn)
        one[3 + k] = first_weights(critic_w1, critic_b1[k : k + 1, :], k, turn)
    store_split(two, 0, 0.5 * actor_w2[...])
    bias_two[0] = column(0.5 * actor_b2[...])
    for k in range(2):
        store_split(two, 1 + k, 0.5 * target_w2[k])
        store_split(two, 3 + k, 0.5 * critic_w2[k])
        store_split(back, k, jnp.transpose(0.5 * critic_w2[k]))
        bias_two[1 + k] = column(0.5 * target_b2[k : k + 1, :])
        bias_two[3 + k] = column(0.5 * critic_b2[k : k + 1, :])
        last[k] = column(target_w3[k : k + 1, :])
        last[2 + k] = column(critic_w3[k : k + 1, :])
    store_split(head, 0, head_weights(actor_w3, turn.at[0:HEAD]))
    wide_bias[...] = head_bias(actor_b3)
    acc_two[...] = jnp.zeros_like(acc_two)
    acc_one[...] = jnp.zeros_like(acc_one)
    acc_side[...] = jnp.zeros_like(acc_side)
    acc_table[...] = jnp.zeros_like(acc_table)
    acc_row[...] = jnp.zeros_like(acc_row)

    def step(index, carry):
        first = index * GROUP
        fill_join(join, next_states, None, first)
        join[OBS : OBS + ACT, :] = jnp.zeros((ACT, CHUNK), F32)
        nexts = join[...]
        _, hidden = activate(dot(one[0], stack_join(nexts)))
        half = dot3(pair(two, 0), split(hidden)) + wide(bias_two[0])
        _, hidden = activate(half)
        out = dot3(pair(head, 0), split(hidden)) + wide(wide_bias[...])
        join[OBS : OBS + ACT, :] = load_chunk(noise_next, ACT, first)
        action, logp, _, _ = squash(out, join[16:24, :])
        given = stack_join(with_action(nexts, action))
        values = []
        for k in range(2):
            _, hidden = activate(dot(one[1 + k], given))
            _, hidden = activate(dot3(pair(two, 1 + k), split(hidden)) + wide(bias_two[1 + k]))
            values.append(
                jnp.sum(hidden * wide(last[k]), axis=0, keepdims=True) + target_b3[0, k]
            )
        keep = GAMMA * (1.0 - load_row(dones, first).astype(F32))
        target = load_row(rewards, first) + keep * (soft_min(values[0], values[1]) - alpha * logp)
        valid = valid_lanes(first, count)
        chance = load_row(probs, first)
        coef = jnp.where(valid, jnp.exp(-BETA * jnp.log(chance)), 0.0)
        fill_join(join, states, actions, first)
        given = stack_join(join[...])
        errors = []
        for k in range(2):
            bent, hidden = activate(dot(one[3 + k], given))
            slope_one = slope(bent, hidden)
            hidden_one = split(hidden)
            half = dot3(pair(two, 3 + k), hidden_one) + wide(bias_two[3 + k])
            bent, hidden = activate(half)
            weight = wide(last[2 + k])
            error = jnp.sum(hidden * weight, axis=0, keepdims=True) + critic_b3[0, k] - target
            errors.append(error)
            scaled = coef * error
            grad = (0.5 * scaled) * weight * slope(bent, hidden)
            acc_side[k] += fold(grad)
            acc_side[2 + k] += fold(scaled * hidden)
            acc_row[k : k + 1, :] += scaled
            grad_two = split(grad)
            acc_two[k] += dot3_t(grad_two, hidden_one)
            grad_one = split(dot3(pair(back, k), grad_two) * slope_one)
            acc_one[k] += dot_t(grad_one[0], given[:48]) + dot_t(grad_one[1], given[:48])
        delta = 0.5 * (errors[0] + errors[1])
        priority = jnp.exp(PRIO_EXP * jnp.log(jnp.abs(delta) + PRIO_EPS))
        priority = jnp.where(valid, priority, 0.0)
        acc_row[2:3, :] = jnp.maximum(acc_row[2:3, :], priority)
        slot = load_row(slots, first)
        place = load_row(owners, first) * depth + lax.shift_right_logical(slot, 7)
        lane = slot & (LANES - 1)
        rows = acc_table.shape[0]
        row_hit = lax.broadcasted_iota(jnp.int32, (rows, CHUNK), 0) == place
        lane_hit = lax.broadcasted_iota(jnp.int32, (LANES, CHUNK), 0) == lane
        high, low = split_wide(priority)
        picked = jnp.concatenate(
            [jnp.where(lane_hit, high, 0.0), jnp.where(lane_hit, low, 0.0)], axis=0
        ).astype(BF16)
        acc_table[...] += dot_t(jnp.where(row_hit, 1.0, 0.0).astype(BF16), picked)
        return carry

    lax.fori_loop(0, (count + CHUNK - 1) // CHUNK, step, 0)

    side = [jnp.sum(acc_side[k], axis=1, keepdims=True) for k in range(4)]
    small = [acc_one[k][:, :JOIN] + acc_one[k][:, JOIN:] for k in range(2)]
    joined = jnp.concatenate(small + side + [jnp.zeros((HID, LANES - 52), F32)], axis=1)
    acc_side[0] = joined
    lane = lax.broadcasted_iota(jnp.int32, probs.shape, 1)
    row = lax.broadcasted_iota(jnp.int32, probs.shape, 0)
    least = jnp.min(jnp.where(row * LANES + lane < count, probs[...], 1.0), keepdims=True)
    best = jnp.max(acc_row[2:3, :], keepdims=True)
    top[...] = jnp.broadcast_to(best, top.shape)
    sums = jnp.concatenate(
        [
            jnp.full((1, LANES), count.astype(F32)),
            spread_row(least),
            spread_row(jnp.sum(acc_row[0:1, :], keepdims=True)),
            spread_row(jnp.sum(acc_row[1:2, :], keepdims=True)),
            jnp.zeros((4, LANES), F32),
        ],
        axis=0,
    )
    table = acc_table[:, :LANES] + acc_table[:, LANES:]
    for p in range(peers):
        mine = slice(p * share, (p + 1) * share)
        at = 0
        for k in range(2):
            for t in range(2):
                send[p, at : at + share, :] = acc_two[k, mine, t * LANES : (t + 1) * LANES]
                at += share
        send[p, at : at + share, :] = acc_side[0, mine, :]
        at += share
        send[p, at : at + depth, :] = table[p * depth : (p + 1) * depth]
        at += depth
        send[p, at : at + 8, :] = sums


def actor_kernel(
    peers,
    count_ref,
    temper_ref,
    actor_b3,
    critic_b3,
    states,
    noise_now,
    actor_w1,
    actor_b1,
    actor_w2,
    actor_b2,
    actor_w3,
    critic_w1,
    critic_b1,
    critic_w2,
    critic_b2,
    critic_w3,
    send,
    one,
    two,
    back,
    head,
    head_back,
    entry,
    bias_two,
    last,
    wide_bias,
    join,
    turn,
    acc_two,
    acc_one,
    acc_head,
    acc_side,
    acc_out,
    acc_row,
):
    count = count_ref[0, 0]
    alpha = jnp.exp(temper_ref[0])
    share = HID // peers
    one[0] = first_weights(actor_w1, actor_b1[...], 0, turn)
    for k in range(2):
        one[1 + k] = first_weights(critic_w1, critic_b1[k : k + 1, :], k, turn)
        store_split(entry, k, turn[16:24, :])
    store_split(two, 0, 0.5 * actor_w2[...])
    store_split(back, 0, jnp.transpose(0.5 * actor_w2[...]))
    bias_two[0] = column(0.5 * actor_b2[...])
    for k in range(2):
        store_split(two, 1 + k, 0.5 * critic_w2[k])
        store_split(back, 1 + k, jnp.transpose(0.5 * critic_w2[k]))
        bias_two[1 + k] = column(0.5 * critic_b2[k : k + 1, :])
        last[k] = column(critic_w3[k : k + 1, :])
    final = head_weights(actor_w3, turn.at[0:HEAD])
    store_split(head, 0, final)
    head_back[...] = stack_weight(0.5 * final)
    wide_bias[...] = head_bias(actor_b3)
    acc_two[...] = jnp.zeros_like(acc_two)
    acc_one[...] = jnp.zeros_like(acc_one)
    acc_head[...] = jnp.zeros_like(acc_head)
    acc_side[...] = jnp.zeros_like(acc_side)
    acc_out[...] = jnp.zeros_like(acc_out)
    acc_row[...] = jnp.zeros_like(acc_row)

    def step(index, carry):
        first = index * GROUP
        valid = valid_lanes(first, count)
        mask = jnp.where(valid, 1.0, 0.0)
        fill_join(join, states, noise_now, first)
        noise = join[16:24, :]
        row = lax.broadcasted_iota(jnp.int32, noise.shape, 0)
        inside = (row >= 1) & (row <= ACT)
        tail = jnp.where(inside, 0.0, noise)
        given = stack_join(jnp.concatenate([join[0:16, :], tail], axis=0))
        bent, hidden = activate(dot(one[0], given))
        slope_one = slope(bent, hidden)
        hidden_one = split(hidden)
        bent, hidden = activate(dot3(pair(two, 0), hidden_one) + wide(bias_two[0]))
        slope_two = slope(bent, hidden)
        hidden_two = split(hidden)
        out = dot3(pair(head, 0), hidden_two) + wide(wide_bias[...])
        action, logp, spread, bend = squash(out, noise)
        acc_row[0:1, :] += mask * (logp + ENTROPY_AIM)
        fresh = stack_join(with_action(join[...], action))
        values, slopes = [], []
        for k in range(2):
            bent, hidden = activate(dot(one[1 + k], fresh))
            inner = slope(bent, hidden)
            bent, hidden = activate(dot3(pair(two, 1 + k), split(hidden)) + wide(bias_two[1 + k]))
            weight = wide(last[k])
            values.append(jnp.sum(hidden * weight, axis=0, keepdims=True) + critic_b3[0, k])
            slopes.append((inner, weight * slope(bent, hidden)))
        gap = (values[1] - values[0]) / SOFT_TEMP
        first_part = 0.5 + 0.5 * jnp.tanh(0.5 * gap)
        parts = (first_part, 0.5 - 0.5 * jnp.tanh(0.5 * gap))
        push = jnp.zeros((8, CHUNK), F32)
        for k in range(2):
            inner, outer = slopes[k]
            grad_two = split((-0.5 * mask * parts[k]) * outer)
            grad_one = split(dot3(pair(back, 1 + k), grad_two) * inner)
            push = push + dot3(pair(entry, k), grad_one)
        pull = alpha * mask
        grad_pre = jnp.where(inside, 2.0 * pull * action + push * (1.0 - action * action), 0.0)
        grad_std = jnp.where(inside, grad_pre * spread - pull, 0.0)
        grad_bend = 0.5 * (STD_HI - STD_LO) * grad_std * (1.0 - bend * bend)
        grad_out = jnp.concatenate([grad_pre, grad_bend], axis=0)
        acc_out[...] += fold(grad_out)
        outs = stack_join(grad_out)
        acc_head[...] += dot_t(hidden_two[0], outs[:32]) + dot_t(hidden_two[1], outs[:32])
        grad = dot(head_back[...], outs) * slope_two
        acc_side[...] += fold(grad)
        grad_two = split(grad)
        acc_two[...] += dot3_t(grad_two, hidden_one)
        grad_one = split(dot3(pair(back, 0), grad_two) * slope_one)
        acc_one[...] += dot_t(grad_one[0], given[:48]) + dot_t(grad_one[1], given[:48])
        return carry

    lax.fori_loop(0, (count + CHUNK - 1) // CHUNK, step, 0)

    joined = jnp.concatenate(
        [
            acc_one[:, :JOIN] + acc_one[:, JOIN:],
            acc_head[:, :HEAD] + acc_head[:, HEAD:],
            jnp.sum(acc_side[...], axis=1, keepdims=True),
            jnp.zeros((HID, LANES - JOIN - HEAD - 1), F32),
        ],
        axis=1,
    )
    acc_side[...] = joined
    gone = -jnp.sum(acc_row[0:1, :], keepdims=True)
    out_sum = jnp.broadcast_to(jnp.sum(acc_out[...], axis=1, keepdims=True), (HEAD, LANES))
    for p in range(peers):
        mine = slice(p * share, (p + 1) * share)
        send[p, 0:share, :] = acc_two[mine, 0:LANES]
        send[p, share : 2 * share, :] = acc_two[mine, LANES : 2 * LANES]
        send[p, 2 * share : 3 * share, :] = acc_side[mine, :]
        at = 3 * share
        send[p, at : at + 8, :] = jnp.broadcast_to(gone, (8, LANES))
        send[p, at + 8 : at + 8 + HEAD, :] = out_sum


def finish_kernel(
    critic_in,
    actor_in,
    old,
    a_one,
    a_bias_one,
    a_two,
    a_bias_two,
    a_three,
    a_bias_three,
    c_one,
    c_bias_one,
    c_two,
    c_bias_two,
    c_three,
    c_bias_three,
    g_alpha,
    new,
):
    peers = critic_in.shape[0]
    share = HID // peers
    depth = old.shape[0]

    def total(ref, start, size):
        value = ref[0, start : start + size, :]
        for p in range(1, peers):
            value = value + ref[p, start : start + size, :]
        return value

    at = 5 * share
    table = total(critic_in, at, depth)
    new[...] = jnp.where(table > 0.0, table, old[...])
    at += depth
    sums = total(critic_in, at, 8)
    least = critic_in[0, at + 1 : at + 2, :]
    for p in range(1, peers):
        least = jnp.minimum(least, critic_in[p, at + 1 : at + 2, :])
    actor_scale = 1.0 / sums[0:1, :]
    critic_scale = actor_scale * jnp.exp(BETA * jnp.log(least))
    for k in range(2):
        for t in range(2):
            c_two[k, :, t * LANES : (t + 1) * LANES] = critic_scale * total(
                critic_in, (2 * k + t) * share, share
            )
    small = jnp.transpose(critic_scale * total(critic_in, 4 * share, share))
    for k in range(2):
        for j in range(JOIN - 1):
            c_one[j, k : k + 1, :] = small[k * JOIN + j : k * JOIN + j + 1, :]
        c_bias_one[k : k + 1, :] = small[k * JOIN + JOIN - 1 : k * JOIN + JOIN, :]
        c_bias_two[k : k + 1, :] = small[48 + k : 49 + k, :]
        c_three[k : k + 1, :] = small[50 + k : 51 + k, :]
    lane = lax.broadcasted_iota(jnp.int32, (1, LANES), 1)
    both = jnp.where(lane == 0, sums[2:3, :], sums[3:4, :])
    c_bias_three[...] = (critic_scale * both)[:, 0:2]
    for t in range(2):
        a_two[:, t * LANES : (t + 1) * LANES] = actor_scale * total(actor_in, t * share, share)
    small = jnp.transpose(actor_scale * total(actor_in, 2 * share, share))
    for j in range(OBS):
        a_one[j] = small[j : j + 1, :]
    a_bias_one[...] = small[JOIN - 1 : JOIN, :]
    for j in range(ACT):
        a_three[j] = small[JOIN + 1 + j : JOIN + 2 + j, :]
        a_three[ACT + j] = small[JOIN + 9 + j : JOIN + 10 + j, :]
    a_bias_two[...] = small[JOIN + HEAD : JOIN + HEAD + 1, :]
    sums = total(actor_in, 3 * share, 8 + HEAD)
    g_alpha[...] = (actor_scale * sums[0:1, :])[:, 0:1]
    biases = jnp.zeros((1, LANES), F32)
    for j in range(ACT):
        biases = jnp.where(lane == j, sums[8 + 1 + j : 8 + 2 + j, :], biases)
        biases = jnp.where(lane == ACT + j, sums[8 + 9 + j : 8 + 10 + j, :], biases)
    a_bias_three[...] = (actor_scale * biases)[:, 0 : 2 * ACT]


SMEM = pl.BlockSpec(memory_space=pltpu.SMEM)
VMEM = pl.BlockSpec(memory_space=pltpu.VMEM)


def shards(
    states,
    actions,
    rewards,
    next_states,
    dones,
    noise_now,
    noise_next,
    probs,
    valid_counts,
    owners,
    slots,
    old_priorities,
    actor_w1,
    actor_b1,
    actor_w2,
    actor_b2,
    actor_w3,
    actor_b3,
    critic_w1,
    critic_b1,
    critic_w2,
    critic_b2,
    critic_w3,
    critic_b3,
    target_w1,
    target_b1,
    target_w2,
    target_b2,
    target_w3,
    target_b3,
    log_alpha,
):
    peers = lax.axis_size("dp")
    share = HID // peers

    def rows(value):
        return value.reshape(-1, LANES)

    states, actions, next_states = rows(states), rows(actions), rows(next_states)
    noise_now, noise_next = rows(noise_now), rows(noise_next)
    rewards, dones, probs = rows(rewards), rows(dones), rows(probs)
    owners, slots, old = rows(owners), rows(slots), rows(old_priorities)
    depth = old.shape[0]
    actor_one = jnp.transpose(actor_w1, (2, 0, 1))
    actor_three = jnp.transpose(actor_w3, (1, 0, 2))
    critic_one = jnp.transpose(critic_w1[0], (2, 0, 1))
    target_one = jnp.transpose(target_w1[0], (2, 0, 1))
    critic_rows = 5 * share + depth + 8
    actor_rows = 3 * share + 8 + HEAD
    params = pltpu.CompilerParams(vmem_limit_bytes=VMEM_LIMIT)
    critic_send, top = pl.pallas_call(
        functools.partial(critic_kernel, peers),
        out_shape=(
            jax.ShapeDtypeStruct((peers, critic_rows, LANES), F32),
            jax.ShapeDtypeStruct((8, LANES), F32),
        ),
        in_specs=[SMEM] * 5 + [VMEM] * 24,
        out_specs=(VMEM, VMEM),
        scratch_shapes=[
            pltpu.VMEM((5, HID, 3 * JOIN), BF16),
            pltpu.VMEM((5, 2, HID, HID), BF16),
            pltpu.VMEM((2, 2, HID, HID), BF16),
            pltpu.VMEM((1, 2, HEAD, HID), BF16),
            pltpu.VMEM((5, HID, LANES), F32),
            pltpu.VMEM((4, HID, LANES), F32),
            pltpu.VMEM((HEAD, LANES), F32),
            pltpu.VMEM((JOIN, CHUNK), F32),
            pltpu.VMEM((JOIN, HID), F32),
            pltpu.VMEM((2, HID, HID), F32),
            pltpu.VMEM((2, HID, 2 * JOIN), F32),
            pltpu.VMEM((4, HID, LANES), F32),
            pltpu.VMEM((peers * depth, 2 * LANES), F32),
            pltpu.VMEM((8, CHUNK), F32),
        ],
        compiler_params=params,
        cost_estimate=pl.CostEstimate(flops=20 * 10**9, bytes_accessed=4 * 10**6, transcendentals=10**7),
        name="critic",
    )(
        valid_counts,
        log_alpha,
        actor_b3,
        critic_b3,
        target_b3,
        states,
        actions,
        rewards,
        next_states,
        dones,
        noise_next,
        probs,
        owners,
        slots,
        actor_one,
        actor_b1,
        actor_w2[0],
        actor_b2,
        actor_three,
        critic_one,
        critic_b1[0],
        critic_w2[0],
        critic_b2[0],
        critic_w3[0],
        target_one,
        target_b1[0],
        target_w2[0],
        target_b2[0],
        target_w3[0],
    )
    critic_in = lax.all_to_all(critic_send, "dp", split_axis=0, concat_axis=0, tiled=True)
    actor_send = pl.pallas_call(
        functools.partial(actor_kernel, peers),
        out_shape=jax.ShapeDtypeStruct((peers, actor_rows, LANES), F32),
        in_specs=[SMEM] * 4 + [VMEM] * 12,
        out_specs=VMEM,
        scratch_shapes=[
            pltpu.VMEM((3, HID, 3 * JOIN), BF16),
            pltpu.VMEM((3, 2, HID, HID), BF16),
            pltpu.VMEM((3, 2, HID, HID), BF16),
            pltpu.VMEM((1, 2, HEAD, HID), BF16),
            pltpu.VMEM((HID, 3 * HEAD), BF16),
            pltpu.VMEM((2, 2, 8, HID), BF16),
            pltpu.VMEM((3, HID, LANES), F32),
            pltpu.VMEM((2, HID, LANES), F32),
            pltpu.VMEM((HEAD, LANES), F32),
            pltpu.VMEM((JOIN, CHUNK), F32),
            pltpu.VMEM((JOIN, HID), F32),
            pltpu.VMEM((HID, HID), F32),
            pltpu.VMEM((HID, 2 * JOIN), F32),
            pltpu.VMEM((HID, 2 * HEAD), F32),
            pltpu.VMEM((HID, LANES), F32),
            pltpu.VMEM((HEAD, LANES), F32),
            pltpu.VMEM((8, CHUNK), F32),
        ],
        compiler_params=params,
        cost_estimate=pl.CostEstimate(flops=20 * 10**9, bytes_accessed=4 * 10**6, transcendentals=10**7),
        name="actor",
    )(
        valid_counts,
        log_alpha,
        actor_b3,
        critic_b3,
        states,
        noise_now,
        actor_one,
        actor_b1,
        actor_w2[0],
        actor_b2,
        actor_three,
        critic_one,
        critic_b1[0],
        critic_w2[0],
        critic_b2[0],
        critic_w3[0],
    )
    actor_in = lax.all_to_all(actor_send, "dp", split_axis=0, concat_axis=0, tiled=True)
    tops = lax.all_to_all(jnp.broadcast_to(top[0:1], (lax.axis_size("seed"), LANES)), "seed", split_axis=0, concat_axis=0, tiled=True)
    best = lax.pmax(jnp.max(tops), "dp")
    shape = jax.ShapeDtypeStruct
    outs = pl.pallas_call(
        finish_kernel,
        out_shape=(
            shape((OBS, 1, share), F32),
            shape((1, share), F32),
            shape((share, HID), F32),
            shape((1, share), F32),
            shape((2 * ACT, 1, share), F32),
            shape((1, 2 * ACT), F32),
            shape((JOIN - 1, 2, share), F32),
            shape((2, share), F32),
            shape((2, share, HID), F32),
            shape((2, share), F32),
            shape((2, share), F32),
            shape((1, 2), F32),
            shape((1, 1), F32),
            shape((depth, LANES), F32),
        ),
        in_specs=[VMEM] * 3,
        out_specs=(VMEM,) * 14,
        compiler_params=params,
        name="finish",
    )(critic_in, actor_in, old)
    return (
        jnp.transpose(outs[0], (1, 2, 0)),
        outs[1],
        outs[2][None],
        outs[3],
        jnp.transpose(outs[4], (1, 0, 2)),
        outs[5],
        jnp.transpose(outs[6], (1, 2, 0))[None],
        outs[7][None],
        outs[8][None],
        outs[9][None],
        outs[10][None],
        outs[11],
        outs[12].reshape(1),
        outs[13].reshape(1, -1),
        best,
    )


def solution(mesh):
    token = P("seed", None, "dp")
    line = P("seed", "dp")
    agent = P("seed")
    placed = (
        (token, token, line, token, line, token, token, line, line, line, line, line)
        + (agent,) * 19
    )
    return jax.shard_map(
        shards,
        mesh=mesh,
        in_specs=placed,
        out_specs=(
            P("seed", "dp", None),
            P("seed", "dp"),
            P("seed", "dp", None),
            P("seed", "dp"),
            P("seed", None, "dp"),
            P("seed", None),
            P("seed", None, "dp", None),
            P("seed", None, "dp"),
            P("seed", None, "dp", None),
            P("seed", None, "dp"),
            P("seed", None, "dp"),
            P("seed", None),
            P("seed"),
            P("seed", "dp"),
            P(),
        ),
        check_vma=False,
    )
```

time: 568 us -> 125 us (0.22); the launches traced: 557 us -> 124 us
  matrix products: 261 us -> 0 us
  waiting for transfers between devices: 142 us -> 0.01 us
  Pallas kernels: 0 us -> 78.5 us
  blocking collectives: 84.2 us -> 32.7 us
  local copies, waits for them, and re-layouts: 26.3 us -> 2.17 us
  other arithmetic: 21.9 us -> 0.6 us
  between operations: 17.4 us -> 1.96 us
    dot_general x57 -> x0, matrix products: 261 us -> none  [the longest x33 181 us: dense(): return jnp.dot(weight, inputs, precision=HIGH) + bias[:, None]]
    pallas_call x0 -> x3, Pallas kernels: none -> 78.5 us  [the longest x1 39.2 us: shards(): pl.pallas_call(functools.partial(critic_kernel, peers), out_shape=(jax.Sh...]
    reduce_scatter x2 -> x0, waiting for transfers between devices: 73.7 us -> none  [the longest x1 38 us: shards(): lax.psum_scatter(critic_three, 'dp', scatter_dimension=2, tiled=True)]
    unnamed x18 -> x0, waiting for transfers between devices: 68 us -> none
    psum x2 -> x0, blocking collectives: 29.3 us -> none  [the longest x1 15.8 us: shards(): total = lax.psum(jnp.sum(mask), 'dp')]
    pmax x1, blocking collectives: 39.8 us -> 19.2 us  [shards(): best = lax.pmax(jnp.max(tops), 'dp')]
    unnamed x116 -> x2, local copies, waits for them, and re-layouts: 20.7 us -> 0.9 us
    pmin x1 -> x0, blocking collectives: 15.1 us -> none  [shards(): least = lax.pmin(jnp.min(jnp.where(valid, chance, 1.0)), 'dp')]
  transfers between devices with their start and end apart: 11 -> 2, of which waited for: 5 -> 0; matrix products, arithmetic and copies ran while one was open for 41% -> 0% of each run, Pallas kernels for 0% -> 30%
where the time goes in v1:
time: 125 us; the launch traced here: 124 us
  Pallas kernels  78.5 us (63%)
  blocking collectives  32.7 us (26%)
  starting transfers between devices  7.84 us (6%)
  local copies, waits for them, and re-layouts  2.17 us (2%)
  between operations  1.96 us (2%)
    pallas_call x1, Pallas kernels, shards(): pl.pallas_call(functools.partial(critic_kernel, peers), out_shape=(jax.Sh...  39.2 us
    pallas_call x1, Pallas kernels, shards(): pl.pallas_call(functools.partial(actor_kernel, peers), out_shape=jax.Shap...  37.2 us
    pmax x1, blocking collectives, shards(): best = lax.pmax(jnp.max(tops), 'dp')  19.2 us
    all_to_all x1, blocking collectives, shards(): lax.all_to_all(actor_send, 'dp', split_axis=0, concat_axis=0, tiled=True)  13.5 us
    all_to_all x1, starting transfers between devices, shards(): lax.all_to_all(jnp.broadcast_to(top[0:1], (lax.axis_size('seed'), LANES))...  4.29 us
    all_to_all x1, starting transfers between devices, shards(): lax.all_to_all(critic_send, 'dp', split_axis=0, concat_axis=0, tiled=True)  3.55 us
  transfers between devices with their start and end apart: 2, of which 0 were waited for; matrix products, arithmetic and copies ran while one was open for 0% of the time, Pallas kernels for 30%

profile of v1, /device:TPU:0, one launch (start us, length us, event | category | flops | bytes accessed | tf_op | source)
XLA Modules:
  0.0 123.8 jit_solution(6874305651055712593)
XLA Ops:
  1.9 39.2 %critic.1 = (f32[8,200,128]{2,1,0:T(8,128)}, f32[8,128]{1,0:T(8,128)}) custom-call(s32[1,1]{1,0:T(1,128)S(6)} %copy.47.count_ref, f32[1]{0:T(128)S(6)} %copy.48.temper_ref, f32[1,12]{1,0:T(1,128)} %actor_b3.3, f32[1,2]{1,0:T(1,128)} %critic_b3.3, f32[1,2]{1,0:T(1,128)} %target_b3.1, f32[544,128]{1,0:T(8,128)} %bitcast.49, f32[192,128]{1,0:T(8,128)} %bitcast.53, ...), custom_call_target="tpu_custom_call" | custom-call | flops 20000000000 | bytes 4000000 | tf_op jit(solution)/shard_map/critic/pallas_call | solution.py:626
  41.2 0.7 slice_bitcast_fusion
  41.9 0.6 broadcast_in_dim.29
  42.5 4.3 %all-to-all-start.2 = ((f32[4,1,128]{2,1,0:T(1,128)}), f32[4,1,128]{2,1,0:T(1,128)S(1)}, u32[]{:S(2)}, u32[]{:S(2)}) async-start(f32[4,1,128]{2,1,0:T(1,128)} %broadcast_in_dim.29), calls=%async_computation.2 | async-start | bytes 4096 | tf_op jit(solution)/shard_map/all_to_all | solution.py:731
  46.8 37.2 %actor.1 = f32[8,120,128]{2,1,0:T(8,128)} custom-call(s32[1,1]{1,0:T(1,128)S(6)} %copy.47.count_ref, f32[1]{0:T(128)S(6)} %copy.48.temper_ref, f32[1,12]{1,0:T(1,128)} %actor_b3.3, f32[1,2]{1,0:T(1,128)} %critic_b3.3, f32[544,128]{1,0:T(8,128)} %bitcast.50, f32[192,128]{1,0:T(8,128)} %bitcast.55, f32[17,1,256]{2,1,0:T(1,128)} %bitcast.63, ...), custom_call_target="tpu_custom_call" | custom-call | flops 20000000000 | bytes 4000000 | tf_op jit(solution)/shard_map/actor/pallas_call | solution.py:685
  84.0 0.0 all-to-all-done.2
  84.0 13.5 %all_to_all.16.actor_in = f32[8,120,128]{2,1,0:T(8,128)} all-to-all(f32[8,120,128]{2,1,0:T(8,128)} %actor.1), channel_id=1, replica_groups=mesh['seed'=4,'dp'=8] {'dp'}, dimensions={0} | all-to-all | bytes 983040 | tf_op jit(solution)/shard_map/all_to_all | solution.py:730
  97.5 3.5 %all-to-all-start = ((f32[8,200,128]{2,1,0:T(8,128)}), f32[8,200,128]{2,1,0:T(8,128)S(1)}, u32[]{:S(2)}, u32[]{:S(2)}) async-start(f32[8,200,128]{2,1,0:T(8,128)} %get-tuple-element.31), calls=%async_computation | async-start | bytes 1638400 | tf_op jit(solution)/shard_map/all_to_all | solution.py:684
  101.0 0.6 reduce_max.9
  101.7 19.2 %pmax.7 = f32[]{:T(128)} all-reduce(f32[]{:T(128)} %reduce_max.9), channel_id=1, replica_groups=mesh['seed'=4,'dp'=8] {'dp'}, use_global_device_ids=true, to_apply=%region_1.0 | all-reduce | flops 1 | bytes 8 | tf_op jit(solution)/shard_map/pmax | solution.py:732
  120.9 0.0 all-to-all-done.critic_in
  120.9 0.0 copy-start
  120.9 0.9 copy-done
  121.8 2.1 %finish.1 = (f32[17,1,32]{2,1,0:T(1,128)}, f32[1,32]{1,0:T(1,128)}, f32[32,256]{1,0:T(8,128)}, f32[1,32]{1,0:T(1,128)}, f32[12,1,32]{2,1,0:T(1,128)}, /*index=5*...) custom-call(f32[8,200,128]{2,1,0:T(8,128)} %copy-done, ...), custom_call_target="tpu_custom_call" | custom-call | tf_op jit(solution)/shard_map/finish/pallas_call | solution.py:734
Async XLA Ops:
  42.5 41.5 %all-to-all-start.2 = ((f32[4,1,128]{2,1,0:T(1,128)}), f32[4,1,128]{2,1,0:T(1,128)S(1)}, u32[]{:S(2)}, u32[]{:S(2)}) async-start(f32[4,1,128]{2,1,0:T(1,128)} %broadcast_in_dim.29), calls=%async_computation.2 | async-start | bytes 4096 | tf_op jit(solution)/shard_map/all_to_all | solution.py:731
  97.5 23.4 %all-to-all-start = ((f32[8,200,128]{2,1,0:T(8,128)}), f32[8,200,128]{2,1,0:T(8,128)S(1)}, u32[]{:S(2)}, u32[]{:S(2)}) async-start(f32[8,200,128]{2,1,0:T(8,128)} %get-tuple-element.31), calls=%async_computation | async-start | bytes 1638400 | tf_op jit(solution)/shard_map/all_to_all | solution.py:684
  120.9 0.9 copy-start

commit v2 on v1

--- a/solution.py
+++ b/solution.py
@@ -27,9 +27,13 @@
 HID = 256
 JOIN = 24
 HEAD = 16
-CHUNK = 512
+CHUNK = 256
 GROUP = CHUNK // LANES
-VMEM_LIMIT = 56 * 1024 * 1024
+STREAMS = 4
+STRIDE = STREAMS * GROUP
+CRITIC_LIMIT = 56 * 1024 * 1024
+ACTOR_LIMIT = 24 * 1024 * 1024
+FINISH_LIMIT = 8 * 1024 * 1024
 
 
 def dot(left, right):
@@ -75,12 +79,51 @@
 
 
 def activate(half):
+    return half * (1.0 + jnp.tanh(half))
+
+
+def activate_slope(half):
     bent = jnp.tanh(half)
-    return bent, half + half * bent
-
-
-def slope(bent, hidden):
-    return (1.0 + hidden) + bent * (1.0 - hidden)
+    rise = 1.0 + bent
+    hidden = half * rise
+    return hidden, rise + hidden * (1.0 - bent)
+
+
+def interleave(tasks):
+    free = {"mxu": 0, "vpu": 0}
+    times = {}
+    queue = []
+
+    def advance(task, now):
+        generator, known = task
+        seen = set(known)
+        asked = next(generator, None)
+        for name in known:
+            if name not in seen:
+                times[(id(known), name)] = now
+        if asked is not None:
+            queue.append((now, task, asked))
+
+    for task in tasks:
+        advance(task, 0)
+    while queue:
+        best = None
+        for place, (ready, task, (unit, cost)) in enumerate(queue):
+            if unit is None:
+                if cost not in task[1]:
+                    continue
+                start = max(ready, times[(id(task[1]), cost)])
+            else:
+                start = max(ready, free[unit])
+            if best is None or start < best[0]:
+                best = (start, place)
+        start, place = best
+        ready, task, (unit, cost) = queue.pop(place)
+        if unit is None:
+            advance(task, start)
+        else:
+            free[unit] = start + cost
+            advance(task, start + cost)
 
 
 def soft_min(first, second):
@@ -149,6 +192,11 @@
 
 def column(row):
     return jnp.transpose(jnp.broadcast_to(row, (LANES, row.shape[1])))
+
+
+def back_weights(weight, scale):
+    both = jnp.concatenate([scale, scale], axis=1)
+    return jnp.transpose(0.25 * both * weight)
 
 
 def head_weights(weight_ref, scratch):
@@ -215,7 +263,6 @@
     target_b2,
     target_w3,
     send,
-    top,
     one,
     two,
     back,
@@ -231,8 +278,8 @@
     acc_table,
     acc_row,
 ):
-    count = count_ref[0, 0]
-    alpha = jnp.exp(temper_ref[0])
+    count = jnp.max(count_ref[...].astype(F32)).astype(jnp.int32)
+    alpha = jnp.exp(temper_ref[...])
     share = HID // peers
     depth = acc_table.shape[0] // peers
     one[0] = first_weights(actor_w1, actor_b1[...], 0, turn)
@@ -244,11 +291,11 @@
     for k in range(2):
         store_split(two, 1 + k, 0.5 * target_w2[k])
         store_split(two, 3 + k, 0.5 * critic_w2[k])
-        store_split(back, k, jnp.transpose(0.5 * critic_w2[k]))
         bias_two[1 + k] = column(0.5 * target_b2[k : k + 1, :])
         bias_two[3 + k] = column(0.5 * critic_b2[k : k + 1, :])
         last[k] = column(target_w3[k : k + 1, :])
         last[2 + k] = column(critic_w3[k : k + 1, :])
+        store_split(back, k, back_weights(critic_w2[k], last[2 + k]))
     store_split(head, 0, head_weights(actor_w3, turn.at[0:HEAD]))
     wide_bias[...] = head_bias(actor_b3)
     acc_two[...] = jnp.zeros_like(acc_two)
@@ -257,54 +304,94 @@
     acc_table[...] = jnp.zeros_like(acc_table)
     acc_row[...] = jnp.zeros_like(acc_row)
 
-    def step(index, carry):
-        first = index * GROUP
-        fill_join(join, next_states, None, first)
-        join[OBS : OBS + ACT, :] = jnp.zeros((ACT, CHUNK), F32)
-        nexts = join[...]
-        _, hidden = activate(dot(one[0], stack_join(nexts)))
-        half = dot3(pair(two, 0), split(hidden)) + wide(bias_two[0])
-        _, hidden = activate(half)
-        out = dot3(pair(head, 0), split(hidden)) + wide(wide_bias[...])
-        join[OBS : OBS + ACT, :] = load_chunk(noise_next, ACT, first)
-        action, logp, _, _ = squash(out, join[16:24, :])
-        given = stack_join(with_action(nexts, action))
-        values = []
-        for k in range(2):
-            _, hidden = activate(dot(one[1 + k], given))
-            _, hidden = activate(dot3(pair(two, 1 + k), split(hidden)) + wide(bias_two[1 + k]))
-            values.append(
-                jnp.sum(hidden * wide(last[k]), axis=0, keepdims=True) + target_b3[0, k]
-            )
+    def next_action(first, known, lane):
+        yield "mxu", 64
+        fill_join(join.at[lane], next_states, None, first)
+        join[lane, OBS : OBS + ACT, :] = jnp.zeros((ACT, CHUNK), F32)
+        nexts = join[lane]
+        half = dot(one[0], stack_join(nexts))
+        yield "vpu", 110
+        hidden = split(activate(half))
+        yield "mxu", 192
+        half = dot3(pair(two, 0), hidden)
+        yield "vpu", 130
+        hidden = split(activate(half + wide(bias_two[0])))
+        yield "mxu", 128
+        out = dot3(pair(head, 0), hidden)
+        yield "vpu", 100
+        join[lane, OBS : OBS + ACT, :] = load_chunk(noise_next, ACT, first)
+        action, known["logp"], _, _ = squash(out + wide(wide_bias[...]), join[lane, 16:24, :])
+        known["given_next"] = stack_join(with_action(nexts, action))
+
+    def target_value(first, known, k):
+        yield None, "given_next"
+        yield "mxu", 64
+        half = dot(one[1 + k], known["given_next"])
+        yield "vpu", 110
+        hidden = split(activate(half))
+        yield "mxu", 192
+        half = dot3(pair(two, 1 + k), hidden)
+        yield "vpu", 120
+        hidden = activate(half + wide(bias_two[1 + k]))
+        total = jnp.sum(hidden * wide(last[k]), axis=0, keepdims=True)
+        known["next", k] = total + target_b3[0, k]
+
+    def target_row(first, known):
+        yield None, "logp"
+        yield None, ("next", 0)
+        yield None, ("next", 1)
+        yield "vpu", 40
         keep = GAMMA * (1.0 - load_row(dones, first).astype(F32))
-        target = load_row(rewards, first) + keep * (soft_min(values[0], values[1]) - alpha * logp)
-        valid = valid_lanes(first, count)
-        chance = load_row(probs, first)
-        coef = jnp.where(valid, jnp.exp(-BETA * jnp.log(chance)), 0.0)
-        fill_join(join, states, actions, first)
-        given = stack_join(join[...])
-        errors = []
-        for k in range(2):
-            bent, hidden = activate(dot(one[3 + k], given))
-            slope_one = slope(bent, hidden)
-            hidden_one = split(hidden)
-            half = dot3(pair(two, 3 + k), hidden_one) + wide(bias_two[3 + k])
-            bent, hidden = activate(half)
-            weight = wide(last[2 + k])
-            error = jnp.sum(hidden * weight, axis=0, keepdims=True) + critic_b3[0, k] - target
-            errors.append(error)
-            scaled = coef * error
-            grad = (0.5 * scaled) * weight * slope(bent, hidden)
-            acc_side[k] += fold(grad)
-            acc_side[2 + k] += fold(scaled * hidden)
-            acc_row[k : k + 1, :] += scaled
-            grad_two = split(grad)
-            acc_two[k] += dot3_t(grad_two, hidden_one)
-            grad_one = split(dot3(pair(back, k), grad_two) * slope_one)
-            acc_one[k] += dot_t(grad_one[0], given[:48]) + dot_t(grad_one[1], given[:48])
-        delta = 0.5 * (errors[0] + errors[1])
+        worth = soft_min(known["next", 0], known["next", 1]) - alpha * known["logp"]
+        known["target"] = load_row(rewards, first) + keep * worth
+        known["valid"] = valid_lanes(first, count)
+        coef = jnp.exp(-BETA * jnp.log(load_row(probs, first)))
+        known["coef"] = jnp.where(known["valid"], coef, 0.0)
+
+    def given_now(first, known, lane):
+        yield "vpu", 20
+        fill_join(join.at[lane], states, actions, first)
+        known["given"] = stack_join(join[lane])
+
+    def critic(first, known, k):
+        yield None, "given"
+        given = known["given"]
+        yield "mxu", 64
+        half = dot(one[3 + k], given)
+        yield "vpu", 160
+        hidden, slope_one = activate_slope(half)
+        hidden_one = split(hidden)
+        yield "mxu", 192
+        half = dot3(pair(two, 3 + k), hidden_one)
+        yield "vpu", 170
+        hidden, slope_two = activate_slope(half + wide(bias_two[3 + k]))
+        value = jnp.sum(hidden * wide(last[2 + k]), axis=0, keepdims=True) + critic_b3[0, k]
+        yield None, "target"
+        yield "vpu", 160
+        error = value - known["target"]
+        known["error", k] = error
+        scaled = known["coef"] * error
+        grad = scaled * slope_two
+        acc_side[k] += fold(grad)
+        acc_side[2 + k] += fold(scaled * hidden)
+        acc_row[k : k + 1, :] += scaled
+        grad_two = split(grad)
+        yield "mxu", 192
+        half = dot3(pair(back, k), grad_two)
+        yield "vpu", 90
+        grad_one = split(half * slope_one)
+        yield "mxu", 192
+        acc_two[k] += dot3_t(grad_two, hidden_one)
+        yield "mxu", 128
+        acc_one[k] += dot_t(grad_one[0], given[:48]) + dot_t(grad_one[1], given[:48])
+
+    def priorities(first, known):
+        yield None, ("error", 0)
+        yield None, ("error", 1)
+        yield "vpu", 120
+        delta = 0.5 * (known["error", 0] + known["error", 1])
         priority = jnp.exp(PRIO_EXP * jnp.log(jnp.abs(delta) + PRIO_EPS))
-        priority = jnp.where(valid, priority, 0.0)
+        priority = jnp.where(known["valid"], priority, 0.0)
         acc_row[2:3, :] = jnp.maximum(acc_row[2:3, :], priority)
         slot = load_row(slots, first)
         place = load_row(owners, first) * depth + lax.shift_right_logical(slot, 7)
@@ -316,11 +403,31 @@
         picked = jnp.concatenate(
             [jnp.where(lane_hit, high, 0.0), jnp.where(lane_hit, low, 0.0)], axis=0
         ).astype(BF16)
-        acc_table[...] += dot_t(jnp.where(row_hit, 1.0, 0.0).astype(BF16), picked)
+        hits = jnp.where(row_hit, 1.0, 0.0).astype(BF16)
+        yield "mxu", 64
+        acc_table[...] += dot_t(hits, picked)
+
+    def step(index, carry):
+        tasks = []
+        for lane in range(STREAMS):
+            first = index * STRIDE + lane * GROUP
+            known = {}
+            tasks.append((next_action(first, known, 2 * lane), known))
+            tasks.append((given_now(first, known, 2 * lane + 1), known))
+            for k in range(2):
+                tasks.append((critic(first, known, k), known))
+            for k in range(2):
+                tasks.append((target_value(first, known, k), known))
+            tasks.append((target_row(first, known), known))
+            tasks.append((priorities(first, known), known))
+        interleave(tasks)
         return carry
 
-    lax.fori_loop(0, (count + CHUNK - 1) // CHUNK, step, 0)
-
+    span = STREAMS * CHUNK
+    lax.fori_loop(0, (count + span - 1) // span, step, 0)
+
+    for k in range(2):
+        acc_side[k] = 0.5 * last[2 + k] * acc_side[k]
     side = [jnp.sum(acc_side[k], axis=1, keepdims=True) for k in range(4)]
     small = [acc_one[k][:, :JOIN] + acc_one[k][:, JOIN:] for k in range(2)]
     joined = jnp.concatenate(small + side + [jnp.zeros((HID, LANES - 52), F32)], axis=1)
@@ -329,14 +436,14 @@
     row = lax.broadcasted_iota(jnp.int32, probs.shape, 0)
     least = jnp.min(jnp.where(row * LANES + lane < count, probs[...], 1.0), keepdims=True)
     best = jnp.max(acc_row[2:3, :], keepdims=True)
-    top[...] = jnp.broadcast_to(best, top.shape)
     sums = jnp.concatenate(
         [
             jnp.full((1, LANES), count.astype(F32)),
             spread_row(least),
             spread_row(jnp.sum(acc_row[0:1, :], keepdims=True)),
             spread_row(jnp.sum(acc_row[1:2, :], keepdims=True)),
-            jnp.zeros((4, LANES), F32),
+            spread_row(best),
+            jnp.zeros((3, LANES), F32),
         ],
         axis=0,
     )
@@ -346,7 +453,8 @@
         at = 0
         for k in range(2):
             for t in range(2):
-                send[p, at : at + share, :] = acc_two[k, mine, t * LANES : (t + 1) * LANES]
+                block = acc_two[k, mine, t * LANES : (t + 1) * LANES]
+                send[p, at : at + share, :] = 0.5 * last[2 + k, mine, :] * block
                 at += share
         send[p, at : at + share, :] = acc_side[0, mine, :]
         at += share
@@ -357,6 +465,7 @@
 
 def actor_kernel(
     peers,
+    core_ref,
     count_ref,
     temper_ref,
     actor_b3,
@@ -373,7 +482,8 @@
     critic_w2,
     critic_b2,
     critic_w3,
-    send,
+    keep,
+    give,
     one,
     two,
     back,
@@ -392,8 +502,8 @@
     acc_out,
     acc_row,
 ):
-    count = count_ref[0, 0]
-    alpha = jnp.exp(temper_ref[0])
+    count = jnp.max(count_ref[...].astype(F32)).astype(jnp.int32)
+    alpha = jnp.exp(temper_ref[...])
     share = HID // peers
     one[0] = first_weights(actor_w1, actor_b1[...], 0, turn)
     for k in range(2):
@@ -404,9 +514,9 @@
     bias_two[0] = column(0.5 * actor_b2[...])
     for k in range(2):
         store_split(two, 1 + k, 0.5 * critic_w2[k])
-        store_split(back, 1 + k, jnp.transpose(0.5 * critic_w2[k]))
         bias_two[1 + k] = column(0.5 * critic_b2[k : k + 1, :])
         last[k] = column(critic_w3[k : k + 1, :])
+        store_split(back, 1 + k, back_weights(critic_w2[k], last[k]))
     final = head_weights(actor_w3, turn.at[0:HEAD])
     store_split(head, 0, final)
     head_back[...] = stack_weight(0.5 * final)
@@ -418,60 +528,104 @@
     acc_out[...] = jnp.zeros_like(acc_out)
     acc_row[...] = jnp.zeros_like(acc_row)
 
-    def step(index, carry):
-        first = index * GROUP
+    row = lax.broadcasted_iota(jnp.int32, (8, CHUNK), 0)
+    inside = (row >= 1) & (row <= ACT)
+
+    def forward(first, known, lane):
+        yield "mxu", 64
         valid = valid_lanes(first, count)
-        mask = jnp.where(valid, 1.0, 0.0)
-        fill_join(join, states, noise_now, first)
-        noise = join[16:24, :]
-        row = lax.broadcasted_iota(jnp.int32, noise.shape, 0)
-        inside = (row >= 1) & (row <= ACT)
+        known["mask"] = jnp.where(valid, 1.0, 0.0)
+        fill_join(join.at[lane], states, noise_now, first)
+        noise = join[lane, 16:24, :]
         tail = jnp.where(inside, 0.0, noise)
-        given = stack_join(jnp.concatenate([join[0:16, :], tail], axis=0))
-        bent, hidden = activate(dot(one[0], given))
-        slope_one = slope(bent, hidden)
+        given = stack_join(jnp.concatenate([join[lane, 0:16, :], tail], axis=0))
+        half = dot(one[0], given)
+        yield "vpu", 160
+        hidden, slope_one = activate_slope(half)
         hidden_one = split(hidden)
-        bent, hidden = activate(dot3(pair(two, 0), hidden_one) + wide(bias_two[0]))
-        slope_two = slope(bent, hidden)
+        yield "mxu", 192
+        half = dot3(pair(two, 0), hidden_one)
+        yield "vpu", 170
+        hidden, slope_two = activate_slope(half + wide(bias_two[0]))
         hidden_two = split(hidden)
-        out = dot3(pair(head, 0), hidden_two) + wide(wide_bias[...])
-        action, logp, spread, bend = squash(out, noise)
-        acc_row[0:1, :] += mask * (logp + ENTROPY_AIM)
-        fresh = stack_join(with_action(join[...], action))
-        values, slopes = [], []
-        for k in range(2):
-            bent, hidden = activate(dot(one[1 + k], fresh))
-            inner = slope(bent, hidden)
-            bent, hidden = activate(dot3(pair(two, 1 + k), split(hidden)) + wide(bias_two[1 + k]))
-            weight = wide(last[k])
-            values.append(jnp.sum(hidden * weight, axis=0, keepdims=True) + critic_b3[0, k])
-            slopes.append((inner, weight * slope(bent, hidden)))
-        gap = (values[1] - values[0]) / SOFT_TEMP
-        first_part = 0.5 + 0.5 * jnp.tanh(0.5 * gap)
-        parts = (first_part, 0.5 - 0.5 * jnp.tanh(0.5 * gap))
-        push = jnp.zeros((8, CHUNK), F32)
-        for k in range(2):
-            inner, outer = slopes[k]
-            grad_two = split((-0.5 * mask * parts[k]) * outer)
-            grad_one = split(dot3(pair(back, 1 + k), grad_two) * inner)
-            push = push + dot3(pair(entry, k), grad_one)
-        pull = alpha * mask
+        yield "mxu", 128
+        out = dot3(pair(head, 0), hidden_two)
+        yield "vpu", 100
+        action, logp, spread, bend = squash(out + wide(wide_bias[...]), noise)
+        acc_row[0:1, :] += known["mask"] * (logp + ENTROPY_AIM)
+        known["fresh"] = stack_join(with_action(join[lane], action))
+        yield None, "push"
+        yield "vpu", 60
+        push = known["push"]
+        pull = alpha * known["mask"]
         grad_pre = jnp.where(inside, 2.0 * pull * action + push * (1.0 - action * action), 0.0)
         grad_std = jnp.where(inside, grad_pre * spread - pull, 0.0)
         grad_bend = 0.5 * (STD_HI - STD_LO) * grad_std * (1.0 - bend * bend)
         grad_out = jnp.concatenate([grad_pre, grad_bend], axis=0)
         acc_out[...] += fold(grad_out)
         outs = stack_join(grad_out)
-        acc_head[...] += dot_t(hidden_two[0], outs[:32]) + dot_t(hidden_two[1], outs[:32])
-        grad = dot(head_back[...], outs) * slope_two
+        yield "mxu", 64
+        half = dot(head_back[...], outs)
+        yield "vpu", 100
+        grad = half * slope_two
         acc_side[...] += fold(grad)
         grad_two = split(grad)
+        yield "mxu", 192
+        half = dot3(pair(back, 0), grad_two)
+        yield "vpu", 90
+        grad_one = split(half * slope_one)
+        yield "mxu", 128
+        acc_head[...] += dot_t(hidden_two[0], outs[:32]) + dot_t(hidden_two[1], outs[:32])
+        yield "mxu", 192
         acc_two[...] += dot3_t(grad_two, hidden_one)
-        grad_one = split(dot3(pair(back, 0), grad_two) * slope_one)
+        yield "mxu", 128
         acc_one[...] += dot_t(grad_one[0], given[:48]) + dot_t(grad_one[1], given[:48])
+
+    def critic(first, known, k):
+        yield None, "fresh"
+        yield "mxu", 64
+        half = dot(one[1 + k], known["fresh"])
+        yield "vpu", 160
+        hidden, slope_one = activate_slope(half)
+        hidden_one = split(hidden)
+        yield "mxu", 192
+        half = dot3(pair(two, 1 + k), hidden_one)
+        yield "vpu", 220
+        hidden, slope_two = activate_slope(half + wide(bias_two[1 + k]))
+        value = jnp.sum(hidden * wide(last[k]), axis=0, keepdims=True) + critic_b3[0, k]
+        known["value", k] = value
+        grad_two = split(slope_two)
+        yield "mxu", 192
+        half = dot3(pair(back, 1 + k), grad_two)
+        yield "vpu", 90
+        grad_one = split(half * slope_one)
+        yield "mxu", 128
+        known["pull", k] = dot3(pair(entry, k), grad_one)
+
+    def mix(first, known):
+        for k in range(2):
+            yield None, ("value", k)
+            yield None, ("pull", k)
+        yield "vpu", 10
+        gap = (known["value", 1] - known["value", 0]) / SOFT_TEMP
+        lean = 0.5 * jnp.tanh(0.5 * gap)
+        parts = (0.5 + lean) * known["pull", 0] + (0.5 - lean) * known["pull", 1]
+        known["push"] = -known["mask"] * parts
+
+    def step(index, carry):
+        tasks = []
+        for lane in range(STREAMS):
+            first = index * STRIDE + lane * GROUP
+            known = {}
+            tasks.append((forward(first, known, lane), known))
+            for k in range(2):
+                tasks.append((critic(first, known, k), known))
+            tasks.append((mix(first, known), known))
+        interleave(tasks)
         return carry
 
-    lax.fori_loop(0, (count + CHUNK - 1) // CHUNK, step, 0)
+    span = STREAMS * CHUNK
+    lax.fori_loop(0, (count + span - 1) // span, step, 0)
 
     joined = jnp.concatenate(
         [
@@ -485,19 +639,24 @@
     acc_side[...] = joined
     gone = -jnp.sum(acc_row[0:1, :], keepdims=True)
     out_sum = jnp.broadcast_to(jnp.sum(acc_out[...], axis=1, keepdims=True), (HEAD, LANES))
-    for p in range(peers):
-        mine = slice(p * share, (p + 1) * share)
-        send[p, 0:share, :] = acc_two[mine, 0:LANES]
-        send[p, share : 2 * share, :] = acc_two[mine, LANES : 2 * LANES]
-        send[p, 2 * share : 3 * share, :] = acc_side[mine, :]
-        at = 3 * share
-        send[p, at : at + 8, :] = jnp.broadcast_to(gone, (8, LANES))
-        send[p, at + 8 : at + 8 + HEAD, :] = out_sum
+    core = core_ref[0]
+    for side, part in ((keep, core), (give, 1 - core)):
+        for q in range(peers // 2):
+            mine = pl.ds(pl.multiple_of((2 * q + part) * share, 8), share)
+            side[q, 0:share, :] = acc_two[mine, 0:LANES]
+            side[q, share : 2 * share, :] = acc_two[mine, LANES : 2 * LANES]
+            side[q, 2 * share : 3 * share, :] = acc_side[mine, :]
+            at = 3 * share
+            side[q, at : at + 8, :] = jnp.broadcast_to(gone, (8, LANES))
+            side[q, at + 8 : at + 8 + HEAD, :] = out_sum
 
 
 def finish_kernel(
     critic_in,
+    actor_kept,
     actor_in,
+    best_kept,
+    best_in,
     old,
     a_one,
     a_bias_one,
@@ -513,10 +672,14 @@
     c_bias_three,
     g_alpha,
     new,
+    best,
 ):
     peers = critic_in.shape[0]
     share = HID // peers
     depth = old.shape[0]
+
+    def actor_total(start, size):
+        return actor_kept[start : start + size, :] + actor_in[start : start + size, :]
 
     def total(ref, start, size):
         value = ref[0, start : start + size, :]
@@ -550,8 +713,8 @@
     both = jnp.where(lane == 0, sums[2:3, :], sums[3:4, :])
     c_bias_three[...] = (critic_scale * both)[:, 0:2]
     for t in range(2):
-        a_two[:, t * LANES : (t + 1) * LANES] = actor_scale * total(actor_in, t * share, share)
-    small = jnp.transpose(actor_scale * total(actor_in, 2 * share, share))
+        a_two[:, t * LANES : (t + 1) * LANES] = actor_scale * actor_total(t * share, share)
+    small = jnp.transpose(actor_scale * actor_total(2 * share, share))
     for j in range(OBS):
         a_one[j] = small[j : j + 1, :]
     a_bias_one[...] = small[JOIN - 1 : JOIN, :]
@@ -559,13 +722,14 @@
         a_three[j] = small[JOIN + 1 + j : JOIN + 2 + j, :]
         a_three[ACT + j] = small[JOIN + 9 + j : JOIN + 10 + j, :]
     a_bias_two[...] = small[JOIN + HEAD : JOIN + HEAD + 1, :]
-    sums = total(actor_in, 3 * share, 8 + HEAD)
+    sums = actor_total(3 * share, 8 + HEAD)
     g_alpha[...] = (actor_scale * sums[0:1, :])[:, 0:1]
     biases = jnp.zeros((1, LANES), F32)
     for j in range(ACT):
         biases = jnp.where(lane == j, sums[8 + 1 + j : 8 + 2 + j, :], biases)
         biases = jnp.where(lane == ACT + j, sums[8 + 9 + j : 8 + 10 + j, :], biases)
     a_bias_three[...] = (actor_scale * biases)[:, 0 : 2 * ACT]
+    best[...] = jnp.maximum(best_kept[...], best_in[...])[:, 0:1]
 
 
 SMEM = pl.BlockSpec(memory_space=pltpu.SMEM)
@@ -606,6 +770,7 @@
     log_alpha,
 ):
     peers = lax.axis_size("dp")
+    me = lax.axis_index("dp")
     share = HID // peers
 
     def rows(value):
@@ -622,15 +787,11 @@
     target_one = jnp.transpose(target_w1[0], (2, 0, 1))
     critic_rows = 5 * share + depth + 8
     actor_rows = 3 * share + 8 + HEAD
-    params = pltpu.CompilerParams(vmem_limit_bytes=VMEM_LIMIT)
-    critic_send, top = pl.pallas_call(
+    critic_send = pl.pallas_call(
         functools.partial(critic_kernel, peers),
-        out_shape=(
-            jax.ShapeDtypeStruct((peers, critic_rows, LANES), F32),
-            jax.ShapeDtypeStruct((8, LANES), F32),
-        ),
-        in_specs=[SMEM] * 5 + [VMEM] * 24,
-        out_specs=(VMEM, VMEM),
+        out_shape=jax.ShapeDtypeStruct((peers, critic_rows, LANES), F32),
+        in_specs=[VMEM] * 2 + [SMEM] * 3 + [VMEM] * 24,
+        out_specs=VMEM,
         scratch_shapes=[
             pltpu.VMEM((5, HID, 3 * JOIN), BF16),
             pltpu.VMEM((5, 2, HID, HID), BF16),
@@ -639,7 +800,7 @@
             pltpu.VMEM((5, HID, LANES), F32),
             pltpu.VMEM((4, HID, LANES), F32),
             pltpu.VMEM((HEAD, LANES), F32),
-            pltpu.VMEM((JOIN, CHUNK), F32),
+            pltpu.VMEM((2 * STREAMS, JOIN, CHUNK), F32),
             pltpu.VMEM((JOIN, HID), F32),
             pltpu.VMEM((2, HID, HID), F32),
             pltpu.VMEM((2, HID, 2 * JOIN), F32),
@@ -647,12 +808,12 @@
             pltpu.VMEM((peers * depth, 2 * LANES), F32),
             pltpu.VMEM((8, CHUNK), F32),
         ],
-        compiler_params=params,
+        compiler_params=pltpu.CompilerParams(vmem_limit_bytes=CRITIC_LIMIT),
         cost_estimate=pl.CostEstimate(flops=20 * 10**9, bytes_accessed=4 * 10**6, transcendentals=10**7),
         name="critic",
     )(
         valid_counts,
-        log_alpha,
+        log_alpha.reshape(1, 1),
         actor_b3,
         critic_b3,
         target_b3,
@@ -682,11 +843,11 @@
         target_w3[0],
     )
     critic_in = lax.all_to_all(critic_send, "dp", split_axis=0, concat_axis=0, tiled=True)
-    actor_send = pl.pallas_call(
+    kept, given = pl.pallas_call(
         functools.partial(actor_kernel, peers),
-        out_shape=jax.ShapeDtypeStruct((peers, actor_rows, LANES), F32),
-        in_specs=[SMEM] * 4 + [VMEM] * 12,
-        out_specs=VMEM,
+        out_shape=(jax.ShapeDtypeStruct((peers // 2, actor_rows, LANES), F32),) * 2,
+        in_specs=[SMEM] + [VMEM] * 2 + [SMEM] * 2 + [VMEM] * 12,
+        out_specs=(VMEM, VMEM),
         scratch_shapes=[
             pltpu.VMEM((3, HID, 3 * JOIN), BF16),
             pltpu.VMEM((3, 2, HID, HID), BF16),
@@ -697,7 +858,7 @@
             pltpu.VMEM((3, HID, LANES), F32),
             pltpu.VMEM((2, HID, LANES), F32),
             pltpu.VMEM((HEAD, LANES), F32),
-            pltpu.VMEM((JOIN, CHUNK), F32),
+            pltpu.VMEM((STREAMS, JOIN, CHUNK), F32),
             pltpu.VMEM((JOIN, HID), F32),
             pltpu.VMEM((HID, HID), F32),
             pltpu.VMEM((HID, 2 * JOIN), F32),
@@ -706,12 +867,13 @@
             pltpu.VMEM((HEAD, LANES), F32),
             pltpu.VMEM((8, CHUNK), F32),
         ],
-        compiler_params=params,
+        compiler_params=pltpu.CompilerParams(vmem_limit_bytes=ACTOR_LIMIT),
         cost_estimate=pl.CostEstimate(flops=20 * 10**9, bytes_accessed=4 * 10**6, transcendentals=10**7),
         name="actor",
     )(
+        (me % 2).reshape(1),
         valid_counts,
-        log_alpha,
+        log_alpha.reshape(1, 1),
         actor_b3,
         critic_b3,
         states,
@@ -727,9 +889,24 @@
         critic_b2[0],
         critic_w3[0],
     )
-    actor_in = lax.all_to_all(actor_send, "dp", split_axis=0, concat_axis=0, tiled=True)
-    tops = lax.all_to_all(jnp.broadcast_to(top[0:1], (lax.axis_size("seed"), LANES)), "seed", split_axis=0, concat_axis=0, tiled=True)
-    best = lax.pmax(jnp.max(tops), "dp")
+    at = 5 * share + depth + 4
+    best = jnp.max(critic_in[:, at : at + 1, :], axis=0)
+    best_in = best
+    agents = lax.axis_size("seed")
+    spans = (agents - 1).bit_length()
+    bits = (peers - 1).bit_length()
+    actor_in = lax.ppermute(given, "dp", [(k, k ^ 1) for k in range(peers)])
+    for bit in range(1, max(bits, 1 + spans)):
+        if bit < bits:
+            both = (kept + actor_in).reshape(-1, 2, actor_rows, LANES)
+            mine = (me >> bit) & 1
+            kept = lax.dynamic_index_in_dim(both, mine, 1, False)
+            given = lax.dynamic_index_in_dim(both, 1 - mine, 1, False)
+            actor_in = lax.ppermute(given, "dp", [(k, k ^ (1 << bit)) for k in range(peers)])
+        if bit <= spans:
+            best = jnp.maximum(best, best_in)
+            best_in = lax.ppermute(best, "seed", [(k, k ^ (1 << (bit - 1))) for k in range(agents)])
+        actor_in, best_in = lax.optimization_barrier((actor_in, best_in))
     shape = jax.ShapeDtypeStruct
     outs = pl.pallas_call(
         finish_kernel,
@@ -748,12 +925,13 @@
             shape((1, 2), F32),
             shape((1, 1), F32),
             shape((depth, LANES), F32),
+            shape((1, 1), F32),
         ),
-        in_specs=[VMEM] * 3,
-        out_specs=(VMEM,) * 14,
-        compiler_params=params,
+        in_specs=[VMEM] * 6,
+        out_specs=(VMEM,) * 15,
+        compiler_params=pltpu.CompilerParams(vmem_limit_bytes=FINISH_LIMIT),
         name="finish",
-    )(critic_in, actor_in, old)
+    )(critic_in, kept[0], actor_in[0], best, best_in, old)
     return (
         jnp.transpose(outs[0], (1, 2, 0)),
         outs[1],
@@ -769,7 +947,7 @@
         outs[11],
         outs[12].reshape(1),
         outs[13].reshape(1, -1),
-        best,
+        outs[14].reshape(()),
     )
 
 

time: 125 us -> 76.3 us (0.61)
  Pallas kernels: 78.5 us -> 30.5 us
  blocking collectives: 32.7 us -> 0 us
  starting transfers between devices: 7.84 us -> 36.7 us
  waiting for transfers between devices: 0.01 us -> 5.56 us
  local copies, waits for them, and re-layouts: 2.17 us -> 0.7 us
    pallas_call x2, Pallas kernels: 76.5 us -> 29.7 us  [the longest x1 16.9 us: shards(): pl.pallas_call(functools.partial(critic_kernel, peers), out_shape=jax.Sha...]
    pmax x1 -> x0, blocking collectives: 19.2 us -> none  [shards(): best = lax.pmax(jnp.max(tops), 'dp')]
    ppermute x0 -> x5, starting transfers between devices: none -> 18.7 us  [the longest x1 11.6 us: shards(): actor_in = lax.ppermute(given, 'dp', [(k, k ^ 1) for k in range(peers)])]
    all_to_all x1, starting transfers between devices: 3.55 us -> 18 us  [shards(): lax.all_to_all(critic_send, 'dp', split_axis=0, concat_axis=0, tiled=True)]
    all_to_all x1 -> x0, blocking collectives: 13.5 us -> none  [shards(): lax.all_to_all(actor_send, 'dp', split_axis=0, concat_axis=0, tiled=True)]
    ppermute x0 -> x5, waiting for transfers between devices: none -> 5.56 us  [the longest x2 2.59 us: shards(): lax.ppermute(given, 'dp', [(k, k ^ 1 << bit) for k in range(peers)])]
    all_to_all x1 -> x0, starting transfers between devices: 4.29 us -> none  [shards(): lax.all_to_all(jnp.broadcast_to(top[0:1], (lax.axis_size('seed'), LANES))...]
    pallas_call x1, Pallas kernels: 2.08 us -> 0.76 us  [shards(): pl.pallas_call(finish_kernel, out_shape=(shape((OBS, 1, share), F32), sha...]
  transfers between devices with their start and end apart: 2 -> 6, of which waited for: 0 -> 3; matrix products, arithmetic and copies ran while one was open for 0% -> 0% of each run, Pallas kernels for 30% -> 17%
where the time goes in v2:
time: 76.3 us; the launch traced here: 75.9 us
  starting transfers between devices  36.7 us (48%)
  Pallas kernels  30.5 us (40%)
  waiting for transfers between devices  5.56 us (7%)
  between operations  2.33 us (3%)
    all_to_all x1, starting transfers between devices, shards(): lax.all_to_all(critic_send, 'dp', split_axis=0, concat_axis=0, tiled=True)  18 us
    pallas_call x1, Pallas kernels, shards(): pl.pallas_call(functools.partial(critic_kernel, peers), out_shape=jax.Sha...  16.9 us
    pallas_call x1, Pallas kernels, shards(): pl.pallas_call(functools.partial(actor_kernel, peers), out_shape=(jax.Sha...  12.9 us
    ppermute x1, starting transfers between devices, shards(): actor_in = lax.ppermute(given, 'dp', [(k, k ^ 1) for k in range(peers)])  11.6 us
    ppermute x2, starting transfers between devices, shards(): lax.ppermute(best, 'seed', [(k, k ^ 1 << bit - 1) for k in range(agents)])  5.57 us
    ppermute x2, waiting for transfers between devices, shards(): lax.ppermute(given, 'dp', [(k, k ^ 1 << bit) for k in range(peers)])  2.59 us
    ppermute x2, waiting for transfers between devices, shards(): lax.ppermute(best, 'seed', [(k, k ^ 1 << bit - 1) for k in range(agents)])  1.83 us
    ppermute x2, starting transfers between devices, shards(): lax.ppermute(given, 'dp', [(k, k ^ 1 << bit) for k in range(peers)])  1.53 us
  transfers between devices with their start and end apart: 6, of which 3 were waited for; matrix products, arithmetic and copies ran while one was open for 0% of the time, Pallas kernels for 17%

profile of v2, /device:TPU:0, one launch (start us, length us, event | category | flops | bytes accessed | tf_op | source)
XLA Modules:
  0.0 75.9 jit_solution(14147741493428352945)
XLA Ops:
  1.9 16.9 %critic.1 = f32[8,200,128]{2,1,0:T(8,128)} custom-call(s32[1,1]{1,0:T(1,128)S(6)} %copy.50.count_ref, f32[1,1]{1,0:T(1,128)} %bitcast.57.temper_ref, f32[1,12]{1,0:T(1,128)} %actor_b3.3, f32[1,2]{1,0:T(1,128)} %critic_b3.3, f32[1,2]{1,0:T(1,128)} %target_b3.1, f32[544,128]{1,0:T(8,128)} %bitcast.63, f32[192,128]{1,0:T(8,128)} %bitcast.85, ...), custom_call_target="tpu_custom_call" | custom-call | flops 20000000000 | bytes 4000000 | tf_op jit(solution)/shard_map/critic/pallas_call | solution.py:790
  18.8 0.0 copy-start.2
  18.8 0.0 copy-start.3
  18.9 0.0 copy-start.4
  18.9 0.0 copy-start.5
  18.9 0.0 copy-start.9
  18.9 0.0 copy-start.10
  18.9 0.0 copy-start.12
  18.9 0.0 copy-start.13
  18.9 0.0 copy-start.14
  18.9 18.0 %all-to-all-start = ((f32[8,200,128]{2,1,0:T(8,128)}), f32[8,200,128]{2,1,0:T(8,128)S(1)}, u32[]{:S(2)}, u32[]{:S(2)}) async-start(f32[8,200,128]{2,1,0:T(8,128)} %critic.1), calls=%async_computation | async-start | bytes 1638400 | tf_op jit(solution)/shard_map/all_to_all | solution.py:845
  36.9 0.0 copy-start.7
  37.0 0.0 copy-start.8
  37.0 0.0 copy-start.11
  37.0 0.0 copy-done.1
  37.0 0.0 copy-done.2
  37.0 0.0 copy-done.3
  37.1 0.6 copy-done.6
  37.7 12.9 %actor.1 = (f32[4,120,128]{2,1,0:T(8,128)S(1)}, f32[4,120,128]{2,1,0:T(8,128)S(1)}) custom-call(s32[1]{0:T(128)} %bitcast.25.core_ref, s32[1,1]{1,0:T(1,128)S(6)} %copy.50.count_ref, f32[1,1]{1,0:T(1,128)} %bitcast.58.temper_ref, f32[1,12]{1,0:T(1,128)S(1)} %copy-done.13, f32[1,2]{1,0:T(1,128)S(1)} %copy-done.14, f32[544,128]{1,0:T(8,128)S(1)} %bitcast.64, ...), custom_call_target="tpu_custom_call" | custom-call | flops 20000000000 | bytes 4000000 | tf_op jit(solution)/shard_map/actor/pallas_call | solution.py:846
  50.5 11.6 %collective-permute-start = (f32[4,120,128]{2,1,0:T(8,128)S(1)}, f32[4,120,128]{2,1,0:T(8,128)S(1)}, u32[]{:S(2)}, u32[]{:S(2)}) collective-permute-start(f32[4,120,128]{2,1,0:T(8,128)S(1)} %get-tuple-element.37), channel_id=1, source_target_pairs={{0,1},{1,0},{2,3},{3,2},{4,5},{5,4},{6,7},{7,6},{8,9},{9,8},{10,11... | collective-permute-start | bytes 737288 | tf_op jit(solution)/shard_map/ppermute | solution.py:898
  62.1 1.1 %collective-permute-done = f32[4,120,128]{2,1,0:T(8,128)S(1)} collective-permute-done((f32[4,120,128]{2,1,0:T(8,128)S(1)}, f32[4,120,128]{2,1,0:T(8,128)S(1)}, u32[]{:S(2)}, u32[]{:S(2)}) %collective-permute-start) | collective-permute-done | bytes 245792 | tf_op jit(solution)/shard_map/ppermute | solution.py:898
  63.3 0.1 collective-permute-start.1
  63.4 0.0 all-to-all-done.critic_in
  63.4 3.0 %collective-permute-start.2 = (f32[1,128]{1,0:T(1,128)S(1)}, f32[1,128]{1,0:T(1,128)S(1)}, u32[]{:S(2)}, u32[]{:S(2)}) collective-permute-start(f32[1,128]{1,0:T(1,128)S(1)} %bitcast.82), channel_id=1, source_target_pairs={{0,8},{8,0},{16,24},{24,16},{1,9},{9,1},{17,25},{25,17},{2,10},{10... | collective-permute-start | bytes 1544 | tf_op jit(solution)/shard_map/ppermute | solution.py:908
  66.4 2.6 %collective-permute-done.1 = f32[2,120,128]{2,1,0:T(8,128)S(1)} collective-permute-done((f32[2,120,128]{2,1,0:T(8,128)S(1)}, f32[2,120,128]{2,1,0:T(8,128)S(1)}, u32[]{:S(2)}, u32[]{:S(2)}) %collective-permute-start.1) | collective-permute-done | bytes 122912 | tf_op jit(solution)/shard_map/ppermute | solution.py:905
  69.0 0.0 collective-permute-done.2
  69.0 0.0 copy-start
  69.0 1.5 %collective-permute-start.3 = (f32[1,120,128]{2,1,0:T(8,128)S(1)}, f32[1,120,128]{2,1,0:T(8,128)S(1)}, u32[]{:S(2)}, u32[]{:S(2)}) collective-permute-start(f32[1,120,128]{2,1,0:T(8,128)S(1)} %get-tuple-element.57), channel_id=1, source_target_pairs={{0,4},{1,5},{2,6},{3,7},{4,0},{5,1},{6,2},{7,3},{8,12},{9,13},{10,... | collective-permute-start | bytes 184328 | tf_op jit(solution)/shard_map/ppermute | solution.py:905
  70.5 2.6 %collective-permute-start.4 = (f32[1,128]{1,0:T(1,128)S(1)}, f32[1,128]{1,0:T(1,128)S(1)}, u32[]{:S(2)}, u32[]{:S(2)}) collective-permute-start(f32[1,128]{1,0:T(1,128)S(1)} %bitcast_maximum_fusion.best_kept), channel_id=1, source_target_pairs={{0,16},{8,24},{16,0},{24,8},{1,17},{9,25},{17,1},{25,9},{2,18},{10... | collective-permute-start | bytes 1544 | tf_op jit(solution)/shard_map/ppermute | solution.py:908
  73.1 1.8 %collective-permute-done.4.best_in = f32[1,128]{1,0:T(1,128)S(1)} collective-permute-done((f32[1,128]{1,0:T(1,128)S(1)}, f32[1,128]{1,0:T(1,128)S(1)}, u32[]{:S(2)}, u32[]{:S(2)}) %collective-permute-start.4) | collective-permute-done | bytes 544 | tf_op jit(solution)/shard_map/ppermute | solution.py:908
  74.9 0.0 collective-permute-done.3
  74.9 0.8 %finish.1 = (f32[17,1,32]{2,1,0:T(1,128)}, f32[1,32]{1,0:T(1,128)}, f32[32,256]{1,0:T(8,128)}, f32[1,32]{1,0:T(1,128)}, f32[12,1,32]{2,1,0:T(1,128)}, /*index=5*...) custom-call(f32[8,200,128]{2,1,0:T(8,128)S(1)} %all-to-all-done.crit, ...), custom_call_target="tpu_custom_call" | custom-call | tf_op jit(solution)/shard_map/finish/pallas_call | solution.py:911
  (19 shorter events, 0.2 us)
Async XLA Ops:
  18.8 18.2 %copy-start.1 = (f32[1,2,256,256]{3,2,1,0:T(8,128)S(1)}, f32[1,2,256,256]{3,2,1,0:T(8,128)}, u32[]{:S(2)}) copy-start(f32[1,2,256,256]{3,2,1,0:T(8,128)} %param.51) | copy-start | bytes 1572868
  18.8 18.2 %copy-start.2 = (f32[1,17,4096]{2,0,1:T(1,128)S(1)}, f32[1,17,4096]{2,0,1:T(1,128)}, u32[]{:S(2)}) copy-start(f32[1,17,4096]{2,0,1:T(1,128)} %param.31) | copy-start | bytes 835588
  18.8 18.2 %copy-start.3 = (f32[1,256,256]{2,1,0:T(8,128)S(1)}, f32[1,256,256]{2,1,0:T(8,128)}, u32[]{:S(2)}) copy-start(f32[1,256,256]{2,1,0:T(8,128)} %param.45) | copy-start | bytes 786436
  18.9 18.2 %copy-start.4 = (f32[1,6,4096]{2,0,1:T(1,128)S(1)}, f32[1,6,4096]{2,0,1:T(1,128)}, u32[]{:S(2)}) copy-start(f32[1,6,4096]{2,0,1:T(1,128)} %param.36) | copy-start | bytes 294916
  18.9 18.2 %copy-start.5 = (f32[1,2,256,23]{2,1,3,0:T(2,128)S(1)}, f32[1,2,256,23]{2,1,3,0:T(2,128)}, u32[]{:S(2)}) copy-start(f32[1,2,256,23]{2,1,3,0:T(2,128)} %param.49) | copy-start | bytes 141316
  18.9 18.2 %copy-start.9 = (f32[1,2,256]{2,1,0:T(2,128)S(1)}, f32[1,2,256]{2,1,0:T(2,128)}, u32[]{:S(2)}) copy-start(f32[1,2,256]{2,1,0:T(2,128)} %param.52) | copy-start | bytes 6148
  18.9 18.2 %copy-start.10 = (f32[1,2,256]{2,1,0:T(2,128)S(1)}, f32[1,2,256]{2,1,0:T(2,128)}, u32[]{:S(2)}) copy-start(f32[1,2,256]{2,1,0:T(2,128)} %param.53) | copy-start | bytes 6148
  18.9 18.2 %copy-start.12 = (f32[1,256]{1,0:T(1,128)S(1)}, f32[1,256]{1,0:T(1,128)}, u32[]{:S(2)}) copy-start(f32[1,256]{1,0:T(1,128)} %actor_b2.3) | copy-start | bytes 3076
  18.9 18.2 %copy-start.13 = (f32[1,12]{1,0:T(1,128)S(1)}, f32[1,12]{1,0:T(1,128)}, u32[]{:S(2)}) copy-start(f32[1,12]{1,0:T(1,128)} %actor_b3.3) | copy-start | bytes 148
  18.9 18.1 %copy-start.14 = (f32[1,2]{1,0:T(1,128)S(1)}, f32[1,2]{1,0:T(1,128)}, u32[]{:S(2)}) copy-start(f32[1,2]{1,0:T(1,128)} %critic_b3.3) | copy-start | bytes 28
  18.9 44.5 %all-to-all-start = ((f32[8,200,128]{2,1,0:T(8,128)}), f32[8,200,128]{2,1,0:T(8,128)S(1)}, u32[]{:S(2)}, u32[]{:S(2)}) async-start(f32[8,200,128]{2,1,0:T(8,128)} %critic.1), calls=%async_computation | async-start | bytes 1638400 | tf_op jit(solution)/shard_map/all_to_all | solution.py:845
  36.9 0.7 copy-start.6
  36.9 0.7 copy-start.7
  37.0 0.7 copy-start.8
  37.0 0.7 copy-start.11
  50.5 12.7 %collective-permute-start = (f32[4,120,128]{2,1,0:T(8,128)S(1)}, f32[4,120,128]{2,1,0:T(8,128)S(1)}, u32[]{:S(2)}, u32[]{:S(2)}) collective-permute-start(f32[4,120,128]{2,1,0:T(8,128)S(1)} %get-tuple-element.37), channel_id=1, source_target_pairs={{0,1},{1,0},{2,3},{3,2},{4,5},{5,4},{6,7},{7,6},{8,9},{9,8},{10,11... | collective-permute-start | bytes 737288 | tf_op jit(solution)/shard_map/ppermute | solution.py:898
  63.3 5.7 %collective-permute-start.1 = (f32[2,120,128]{2,1,0:T(8,128)S(1)}, f32[2,120,128]{2,1,0:T(8,128)S(1)}, u32[]{:S(2)}, u32[]{:S(2)}) collective-permute-start(f32[2,120,128]{2,1,0:T(8,128)S(1)} %dynamic-slice_bitcast_fusion), channel_id=1, source_target_pairs={{0,2},{1,3},{2,0},{3,1},{4,6},{5,7},{6,4},{7,5},{8,10},{9,11},{10,... | collective-permute-start | bytes 368648 | tf_op jit(solution)/shard_map/ppermute | solution.py:905
  63.4 5.6 %collective-permute-start.2 = (f32[1,128]{1,0:T(1,128)S(1)}, f32[1,128]{1,0:T(1,128)S(1)}, u32[]{:S(2)}, u32[]{:S(2)}) collective-permute-start(f32[1,128]{1,0:T(1,128)S(1)} %bitcast.82), channel_id=1, source_target_pairs={{0,8},{8,0},{16,24},{24,16},{1,9},{9,1},{17,25},{25,17},{2,10},{10... | collective-permute-start | bytes 1544 | tf_op jit(solution)/shard_map/ppermute | solution.py:908
  69.0 5.9 %copy-start = (f32[1,4096]{1,0:T(1,128)S(1)}, f32[1,4096]{1,0:T(1,128)}, u32[]{:S(2)}) copy-start(f32[1,4096]{1,0:T(1,128)} %param.42) | copy-start | bytes 49156
  69.0 5.9 %collective-permute-start.3 = (f32[1,120,128]{2,1,0:T(8,128)S(1)}, f32[1,120,128]{2,1,0:T(8,128)S(1)}, u32[]{:S(2)}, u32[]{:S(2)}) collective-permute-start(f32[1,120,128]{2,1,0:T(8,128)S(1)} %get-tuple-element.57), channel_id=1, source_target_pairs={{0,4},{1,5},{2,6},{3,7},{4,0},{5,1},{6,2},{7,3},{8,12},{9,13},{10,... | collective-permute-start | bytes 184328 | tf_op jit(solution)/shard_map/ppermute | solution.py:905
  70.5 4.4 %collective-permute-start.4 = (f32[1,128]{1,0:T(1,128)S(1)}, f32[1,128]{1,0:T(1,128)S(1)}, u32[]{:S(2)}, u32[]{:S(2)}) collective-permute-start(f32[1,128]{1,0:T(1,128)S(1)} %bitcast_maximum_fusion.best_kept), channel_id=1, source_target_pairs={{0,16},{8,24},{16,0},{24,8},{1,17},{9,25},{17,1},{25,9},{2,18},{10... | collective-permute-start | bytes 1544 | tf_op jit(solution)/shard_map/ppermute | solution.py:908

commit v3 on v2

--- a/solution.py
+++ b/solution.py
@@ -26,13 +26,16 @@
 ACT = 6
 HID = 256
 JOIN = 24
+OUT_LANE = 48
+HEAD_ROW = 3 * JOIN
+REST_ROW = HEAD_ROW + 16
+BIAS_ROW = REST_ROW + 8
+SMALL = BIAS_ROW + 16
 HEAD = 16
-CHUNK = 256
-GROUP = CHUNK // LANES
-STREAMS = 4
-STRIDE = STREAMS * GROUP
+CRITIC_BLOCKS, CRITIC_STREAMS, CRITIC_LAG = 4, 4, 2000
+ACTOR_BLOCKS, ACTOR_STREAMS = 8, 2
 CRITIC_LIMIT = 56 * 1024 * 1024
-ACTOR_LIMIT = 24 * 1024 * 1024
+ACTOR_LIMIT = 36 * 1024 * 1024
 FINISH_LIMIT = 8 * 1024 * 1024
 
 
@@ -60,12 +63,18 @@
     return dot(weight[0], high) + dot(weight[0], low) + dot(weight[1], high)
 
 
+def dot3_few(weight, value):
+    rows = weight[0].shape[0]
+    both = dot(jnp.concatenate(weight, axis=0), value[0])
+    return both[:rows] + both[rows:] + dot(weight[0], value[1])
+
+
 def dot3_t(left, right):
     return dot_t(left[0], right[0]) + dot_t(left[0], right[1]) + dot_t(left[1], right[0])
 
 
-def wide(column):
-    return jnp.concatenate([column] * GROUP, axis=1)
+def wide(column, blocks):
+    return jnp.concatenate([column] * blocks, axis=1)
 
 
 def stack_join(value):
@@ -105,7 +114,7 @@
             queue.append((now, task, asked))
 
     for task in tasks:
-        advance(task, 0)
+        advance(task, task[1]["begin"])
     while queue:
         best = None
         for place, (ready, task, (unit, cost)) in enumerate(queue):
@@ -122,6 +131,7 @@
         if unit is None:
             advance(task, start)
         else:
+            cost = cost * 3 // 2 if unit == "vpu" else cost
             free[unit] = start + cost
             advance(task, start + cost)
 
@@ -151,19 +161,20 @@
     return ref[pl.ds(block, count, stride=blocks), :]
 
 
-def load_chunk(ref, count, first):
-    return jnp.concatenate([load_rows(ref, count, first + g) for g in range(GROUP)], axis=1)
-
-
-def load_row(ref, first):
-    return jnp.concatenate([ref[pl.ds(first + g, 1), :] for g in range(GROUP)], axis=1)
+def load_chunk(ref, count, first, blocks):
+    return jnp.concatenate([load_rows(ref, count, first + g) for g in range(blocks)], axis=1)
+
+
+def load_row(ref, first, blocks):
+    return jnp.concatenate([ref[pl.ds(first + g, 1), :] for g in range(blocks)], axis=1)
 
 
 def fill_join(join, obs_ref, act_ref, first):
-    join[0:OBS, :] = load_chunk(obs_ref, OBS, first)
+    blocks = join.shape[1] // LANES
+    join[0:OBS, :] = load_chunk(obs_ref, OBS, first, blocks)
     if act_ref is not None:
-        join[OBS : OBS + ACT, :] = load_chunk(act_ref, ACT, first)
-    join[JOIN - 1 : JOIN, :] = jnp.ones((1, CHUNK), F32)
+        join[OBS : OBS + ACT, :] = load_chunk(act_ref, ACT, first, blocks)
+    join[JOIN - 1 : JOIN, :] = jnp.ones((1, join.shape[1]), F32)
 
 
 def with_action(join, action):
@@ -172,12 +183,10 @@
     return jnp.concatenate([join[:16], jnp.where(inside, action, join[16:])], axis=0)
 
 
-def first_weights(weight_ref, bias_row, index, scratch):
+def fill_first(ref, row, weight_ref, bias_row, index):
     rows = weight_ref.shape[0]
-    scratch[...] = jnp.zeros_like(scratch)
-    scratch[0:rows, :] = weight_ref[:, index, :]
-    scratch[JOIN - 1 : JOIN, :] = bias_row
-    return stack_weight(0.5 * scratch[...])
+    ref[row : row + rows, :] = weight_ref[:, index, :]
+    ref[row + JOIN - 1 : row + JOIN, :] = bias_row
 
 
 def store_split(ref, index, value):
@@ -190,20 +199,14 @@
     return ref[index, 0], ref[index, 1]
 
 
-def column(row):
-    return jnp.transpose(jnp.broadcast_to(row, (LANES, row.shape[1])))
+def columns(rows):
+    turned = jnp.transpose(rows)
+    return [jnp.broadcast_to(turned[:, k : k + 1], (HID, LANES)) for k in range(rows.shape[0])]
 
 
 def back_weights(weight, scale):
     both = jnp.concatenate([scale, scale], axis=1)
     return jnp.transpose(0.25 * both * weight)
-
-
-def head_weights(weight_ref, scratch):
-    scratch[...] = jnp.zeros_like(scratch)
-    scratch[1 : 1 + ACT, :] = weight_ref[0:ACT, 0, :]
-    scratch[9 : 9 + ACT, :] = weight_ref[ACT : 2 * ACT, 0, :]
-    return scratch[...]
 
 
 def head_bias(bias_ref):
@@ -217,13 +220,13 @@
 
 def fold(value):
     total = value[:, :LANES]
-    for g in range(1, GROUP):
+    for g in range(1, value.shape[1] // LANES):
         total = total + value[:, g * LANES : (g + 1) * LANES]
     return total
 
 
-def valid_lanes(first, count):
-    lane = lax.broadcasted_iota(jnp.int32, (1, CHUNK), 1)
+def valid_lanes(first, count, width):
+    lane = lax.broadcasted_iota(jnp.int32, (1, width), 1)
     return lane + first * LANES < count
 
 
@@ -263,6 +266,7 @@
     target_b2,
     target_w3,
     send,
+    small,
     one,
     two,
     back,
@@ -271,33 +275,52 @@
     last,
     wide_bias,
     join,
-    turn,
     acc_two,
     acc_one,
     acc_side,
     acc_table,
     acc_row,
+    turn,
 ):
     count = jnp.max(count_ref[...].astype(F32)).astype(jnp.int32)
     alpha = jnp.exp(temper_ref[...])
     share = HID // peers
+    blocks = CRITIC_BLOCKS
+    width = blocks * LANES
     depth = acc_table.shape[0] // peers
-    one[0] = first_weights(actor_w1, actor_b1[...], 0, turn)
+    small[...] = jnp.zeros_like(small)
+    fill_first(small, 0, actor_w1, actor_b1[...], 0)
     for k in range(2):
-        one[1 + k] = first_weights(target_w1, target_b1[k : k + 1, :], k, turn)
-        one[3 + k] = first_weights(critic_w1, critic_b1[k : k + 1, :], k, turn)
+        fill_first(small, (1 + k) * JOIN, critic_w1, critic_b1[k : k + 1, :], k)
+        fill_first(turn, k * JOIN, target_w1, target_b1[k : k + 1, :], k)
+    small[HEAD_ROW + 1 : HEAD_ROW + 1 + ACT, :] = actor_w3[0:ACT, 0, :]
+    small[HEAD_ROW + 9 : HEAD_ROW + 9 + ACT, :] = actor_w3[ACT : 2 * ACT, 0, :]
+    small[REST_ROW : REST_ROW + 1, :] = 0.5 * actor_b2[...]
+    small[REST_ROW + 1 : REST_ROW + 3, :] = 0.5 * critic_b2[...]
+    small[REST_ROW + 3 : REST_ROW + 5, :] = critic_w3[...]
+    turn[2 * JOIN : 2 * JOIN + 2, :] = 0.5 * target_b2[...]
+    turn[2 * JOIN + 2 : 2 * JOIN + 4, :] = target_w3[...]
+    turn[2 * JOIN + 4 : 2 * JOIN + 8, :] = jnp.zeros((4, HID), F32)
+    one[0] = stack_weight(0.5 * small[0:JOIN, :])
     store_split(two, 0, 0.5 * actor_w2[...])
-    bias_two[0] = column(0.5 * actor_b2[...])
+    given = columns(small[REST_ROW : REST_ROW + 8, :])
+    aims = columns(turn[2 * JOIN : 2 * JOIN + 8, :])
+    bias_two[0] = given[0]
     for k in range(2):
+        one[1 + k] = stack_weight(0.5 * turn[k * JOIN : (k + 1) * JOIN, :])
+        one[3 + k] = stack_weight(0.5 * small[(1 + k) * JOIN : (2 + k) * JOIN, :])
         store_split(two, 1 + k, 0.5 * target_w2[k])
         store_split(two, 3 + k, 0.5 * critic_w2[k])
-        bias_two[1 + k] = column(0.5 * target_b2[k : k + 1, :])
-        bias_two[3 + k] = column(0.5 * critic_b2[k : k + 1, :])
-        last[k] = column(target_w3[k : k + 1, :])
-        last[2 + k] = column(critic_w3[k : k + 1, :])
+        bias_two[1 + k] = aims[k]
+        bias_two[3 + k] = given[1 + k]
+        last[k] = aims[2 + k]
+        last[2 + k] = given[3 + k]
         store_split(back, k, back_weights(critic_w2[k], last[2 + k]))
-    store_split(head, 0, head_weights(actor_w3, turn.at[0:HEAD]))
+    store_split(head, 0, small[HEAD_ROW : HEAD_ROW + HEAD, :])
     wide_bias[...] = head_bias(actor_b3)
+    small[BIAS_ROW : BIAS_ROW + HEAD, 0:LANES] = wide_bias[...]
+    for k in range(2):
+        small[BIAS_ROW + k : BIAS_ROW + k + 1, LANES:] = jnp.full((1, LANES), critic_b3[0, k])
     acc_two[...] = jnp.zeros_like(acc_two)
     acc_one[...] = jnp.zeros_like(acc_one)
     acc_side[...] = jnp.zeros_like(acc_side)
@@ -307,7 +330,7 @@
     def next_action(first, known, lane):
         yield "mxu", 64
         fill_join(join.at[lane], next_states, None, first)
-        join[lane, OBS : OBS + ACT, :] = jnp.zeros((ACT, CHUNK), F32)
+        join[lane, OBS : OBS + ACT, :] = jnp.zeros((ACT, width), F32)
         nexts = join[lane]
         half = dot(one[0], stack_join(nexts))
         yield "vpu", 110
@@ -315,12 +338,12 @@
         yield "mxu", 192
         half = dot3(pair(two, 0), hidden)
         yield "vpu", 130
-        hidden = split(activate(half + wide(bias_two[0])))
+        hidden = split(activate(half + wide(bias_two[0], blocks)))
         yield "mxu", 128
-        out = dot3(pair(head, 0), hidden)
+        out = dot3_few(pair(head, 0), hidden)
         yield "vpu", 100
-        join[lane, OBS : OBS + ACT, :] = load_chunk(noise_next, ACT, first)
-        action, known["logp"], _, _ = squash(out + wide(wide_bias[...]), join[lane, 16:24, :])
+        join[lane, OBS : OBS + ACT, :] = load_chunk(noise_next, ACT, first, blocks)
+        action, known["logp"], _, _ = squash(out + wide(wide_bias[...], blocks), join[lane, 16:24, :])
         known["given_next"] = stack_join(with_action(nexts, action))
 
     def target_value(first, known, k):
@@ -332,8 +355,8 @@
         yield "mxu", 192
         half = dot3(pair(two, 1 + k), hidden)
         yield "vpu", 120
-        hidden = activate(half + wide(bias_two[1 + k]))
-        total = jnp.sum(hidden * wide(last[k]), axis=0, keepdims=True)
+        hidden = activate(half + wide(bias_two[1 + k], blocks))
+        total = jnp.sum(hidden * wide(last[k], blocks), axis=0, keepdims=True)
         known["next", k] = total + target_b3[0, k]
 
     def target_row(first, known):
@@ -341,11 +364,11 @@
         yield None, ("next", 0)
         yield None, ("next", 1)
         yield "vpu", 40
-        keep = GAMMA * (1.0 - load_row(dones, first).astype(F32))
+        keep = GAMMA * (1.0 - load_row(dones, first, blocks).astype(F32))
         worth = soft_min(known["next", 0], known["next", 1]) - alpha * known["logp"]
-        known["target"] = load_row(rewards, first) + keep * worth
-        known["valid"] = valid_lanes(first, count)
-        coef = jnp.exp(-BETA * jnp.log(load_row(probs, first)))
+        known["target"] = load_row(rewards, first, blocks) + keep * worth
+        known["valid"] = valid_lanes(first, count, width)
+        coef = jnp.exp(-BETA * jnp.log(load_row(probs, first, blocks)))
         known["coef"] = jnp.where(known["valid"], coef, 0.0)
 
     def given_now(first, known, lane):
@@ -364,8 +387,8 @@
         yield "mxu", 192
         half = dot3(pair(two, 3 + k), hidden_one)
         yield "vpu", 170
-        hidden, slope_two = activate_slope(half + wide(bias_two[3 + k]))
-        value = jnp.sum(hidden * wide(last[2 + k]), axis=0, keepdims=True) + critic_b3[0, k]
+        hidden, slope_two = activate_slope(half + wide(bias_two[3 + k], blocks))
+        value = jnp.sum(hidden * wide(last[2 + k], blocks), axis=0, keepdims=True) + critic_b3[0, k]
         yield None, "target"
         yield "vpu", 160
         error = value - known["target"]
@@ -383,7 +406,7 @@
         yield "mxu", 192
         acc_two[k] += dot3_t(grad_two, hidden_one)
         yield "mxu", 128
-        acc_one[k] += dot_t(grad_one[0], given[:48]) + dot_t(grad_one[1], given[:48])
+        acc_one[k] += dot_t(given[:48], grad_one[0]) + dot_t(given[:48], grad_one[1])
 
     def priorities(first, known):
         yield None, ("error", 0)
@@ -393,12 +416,12 @@
         priority = jnp.exp(PRIO_EXP * jnp.log(jnp.abs(delta) + PRIO_EPS))
         priority = jnp.where(known["valid"], priority, 0.0)
         acc_row[2:3, :] = jnp.maximum(acc_row[2:3, :], priority)
-        slot = load_row(slots, first)
-        place = load_row(owners, first) * depth + lax.shift_right_logical(slot, 7)
+        slot = load_row(slots, first, blocks)
+        place = load_row(owners, first, blocks) * depth + lax.shift_right_logical(slot, 7)
         lane = slot & (LANES - 1)
         rows = acc_table.shape[0]
-        row_hit = lax.broadcasted_iota(jnp.int32, (rows, CHUNK), 0) == place
-        lane_hit = lax.broadcasted_iota(jnp.int32, (LANES, CHUNK), 0) == lane
+        row_hit = lax.broadcasted_iota(jnp.int32, (rows, width), 0) == place
+        lane_hit = lax.broadcasted_iota(jnp.int32, (LANES, width), 0) == lane
         high, low = split_wide(priority)
         picked = jnp.concatenate(
             [jnp.where(lane_hit, high, 0.0), jnp.where(lane_hit, low, 0.0)], axis=0
@@ -409,9 +432,9 @@
 
     def step(index, carry):
         tasks = []
-        for lane in range(STREAMS):
-            first = index * STRIDE + lane * GROUP
-            known = {}
+        for lane in range(CRITIC_STREAMS):
+            first = (index * CRITIC_STREAMS + lane) * blocks
+            known = {"begin": CRITIC_LAG * (2 * lane // CRITIC_STREAMS)}
             tasks.append((next_action(first, known, 2 * lane), known))
             tasks.append((given_now(first, known, 2 * lane + 1), known))
             for k in range(2):
@@ -423,13 +446,13 @@
         interleave(tasks)
         return carry
 
-    span = STREAMS * CHUNK
+    span = CRITIC_STREAMS * width
     lax.fori_loop(0, (count + span - 1) // span, step, 0)
 
     for k in range(2):
         acc_side[k] = 0.5 * last[2 + k] * acc_side[k]
     side = [jnp.sum(acc_side[k], axis=1, keepdims=True) for k in range(4)]
-    small = [acc_one[k][:, :JOIN] + acc_one[k][:, JOIN:] for k in range(2)]
+    small = [jnp.transpose(acc_one[k][:JOIN] + acc_one[k][JOIN:]) for k in range(2)]
     joined = jnp.concatenate(small + side + [jnp.zeros((HID, LANES - 52), F32)], axis=1)
     acc_side[0] = joined
     lane = lax.broadcasted_iota(jnp.int32, probs.shape, 1)
@@ -468,20 +491,11 @@
     core_ref,
     count_ref,
     temper_ref,
-    actor_b3,
-    critic_b3,
     states,
     noise_now,
-    actor_w1,
-    actor_b1,
+    small,
     actor_w2,
-    actor_b2,
-    actor_w3,
-    critic_w1,
-    critic_b1,
     critic_w2,
-    critic_b2,
-    critic_w3,
     keep,
     give,
     one,
@@ -494,7 +508,6 @@
     last,
     wide_bias,
     join,
-    turn,
     acc_two,
     acc_one,
     acc_head,
@@ -505,22 +518,26 @@
     count = jnp.max(count_ref[...].astype(F32)).astype(jnp.int32)
     alpha = jnp.exp(temper_ref[...])
     share = HID // peers
-    one[0] = first_weights(actor_w1, actor_b1[...], 0, turn)
-    for k in range(2):
-        one[1 + k] = first_weights(critic_w1, critic_b1[k : k + 1, :], k, turn)
-        store_split(entry, k, turn[16:24, :])
+    blocks = ACTOR_BLOCKS
+    width = blocks * LANES
+    given = columns(small[REST_ROW : REST_ROW + 8, :])
+    final = small[HEAD_ROW : HEAD_ROW + HEAD, :]
     store_split(two, 0, 0.5 * actor_w2[...])
     store_split(back, 0, jnp.transpose(0.5 * actor_w2[...]))
-    bias_two[0] = column(0.5 * actor_b2[...])
+    bias_two[0] = given[0]
+    one[0] = stack_weight(0.5 * small[0:JOIN, :])
     for k in range(2):
+        first = (1 + k) * JOIN
+        one[1 + k] = stack_weight(0.5 * small[first : first + JOIN, :])
+        store_split(entry, k, small[first + 8 : first + 24, :])
         store_split(two, 1 + k, 0.5 * critic_w2[k])
-        bias_two[1 + k] = column(0.5 * critic_b2[k : k + 1, :])
-        last[k] = column(critic_w3[k : k + 1, :])
+        bias_two[1 + k] = given[1 + k]
+        last[k] = given[3 + k]
         store_split(back, 1 + k, back_weights(critic_w2[k], last[k]))
-    final = head_weights(actor_w3, turn.at[0:HEAD])
     store_split(head, 0, final)
     head_back[...] = stack_weight(0.5 * final)
-    wide_bias[...] = head_bias(actor_b3)
+    wide_bias[...] = small[BIAS_ROW : BIAS_ROW + HEAD, 0:LANES]
+    critic_b3 = [small[BIAS_ROW + k : BIAS_ROW + k + 1, LANES : LANES + 1] for k in range(2)]
     acc_two[...] = jnp.zeros_like(acc_two)
     acc_one[...] = jnp.zeros_like(acc_one)
     acc_head[...] = jnp.zeros_like(acc_head)
@@ -528,12 +545,12 @@
     acc_out[...] = jnp.zeros_like(acc_out)
     acc_row[...] = jnp.zeros_like(acc_row)
 
-    row = lax.broadcasted_iota(jnp.int32, (8, CHUNK), 0)
+    row = lax.broadcasted_iota(jnp.int32, (8, width), 0)
     inside = (row >= 1) & (row <= ACT)
 
     def forward(first, known, lane):
         yield "mxu", 64
-        valid = valid_lanes(first, count)
+        valid = valid_lanes(first, count, width)
         known["mask"] = jnp.where(valid, 1.0, 0.0)
         fill_join(join.at[lane], states, noise_now, first)
         noise = join[lane, 16:24, :]
@@ -546,12 +563,12 @@
         yield "mxu", 192
         half = dot3(pair(two, 0), hidden_one)
         yield "vpu", 170
-        hidden, slope_two = activate_slope(half + wide(bias_two[0]))
+        hidden, slope_two = activate_slope(half + wide(bias_two[0], blocks))
         hidden_two = split(hidden)
         yield "mxu", 128
-        out = dot3(pair(head, 0), hidden_two)
+        out = dot3_few(pair(head, 0), hidden_two)
         yield "vpu", 100
-        action, logp, spread, bend = squash(out + wide(wide_bias[...]), noise)
+        action, logp, spread, bend = squash(out + wide(wide_bias[...], blocks), noise)
         acc_row[0:1, :] += known["mask"] * (logp + ENTROPY_AIM)
         known["fresh"] = stack_join(with_action(join[lane], action))
         yield None, "push"
@@ -591,8 +608,8 @@
         yield "mxu", 192
         half = dot3(pair(two, 1 + k), hidden_one)
         yield "vpu", 220
-        hidden, slope_two = activate_slope(half + wide(bias_two[1 + k]))
-        value = jnp.sum(hidden * wide(last[k]), axis=0, keepdims=True) + critic_b3[0, k]
+        hidden, slope_two = activate_slope(half + wide(bias_two[1 + k], blocks))
+        value = jnp.sum(hidden * wide(last[k], blocks), axis=0, keepdims=True) + critic_b3[k]
         known["value", k] = value
         grad_two = split(slope_two)
         yield "mxu", 192
@@ -600,7 +617,7 @@
         yield "vpu", 90
         grad_one = split(half * slope_one)
         yield "mxu", 128
-        known["pull", k] = dot3(pair(entry, k), grad_one)
+        known["pull", k] = dot3_few(pair(entry, k), grad_one)[8:]
 
     def mix(first, known):
         for k in range(2):
@@ -614,9 +631,9 @@
 
     def step(index, carry):
         tasks = []
-        for lane in range(STREAMS):
-            first = index * STRIDE + lane * GROUP
-            known = {}
+        for lane in range(ACTOR_STREAMS):
+            first = (index * ACTOR_STREAMS + lane) * blocks
+            known = {"begin": 0}
             tasks.append((forward(first, known, lane), known))
             for k in range(2):
                 tasks.append((critic(first, known, k), known))
@@ -624,21 +641,23 @@
         interleave(tasks)
         return carry
 
-    span = STREAMS * CHUNK
+    span = ACTOR_STREAMS * width
     lax.fori_loop(0, (count + span - 1) // span, step, 0)
 
+    acc_out[...] = jnp.broadcast_to(jnp.sum(acc_out[...], axis=1, keepdims=True), (HEAD, LANES))
     joined = jnp.concatenate(
         [
             acc_one[:, :JOIN] + acc_one[:, JOIN:],
             acc_head[:, :HEAD] + acc_head[:, HEAD:],
             jnp.sum(acc_side[...], axis=1, keepdims=True),
-            jnp.zeros((HID, LANES - JOIN - HEAD - 1), F32),
+            jnp.broadcast_to(-jnp.sum(acc_row[0:1, :], keepdims=True), (HID, 1)),
+            jnp.zeros((HID, OUT_LANE - JOIN - HEAD - 2), F32),
+            jnp.broadcast_to(jnp.transpose(acc_out[...])[0:1, :], (HID, HEAD)),
+            jnp.zeros((HID, LANES - OUT_LANE - HEAD), F32),
         ],
         axis=1,
     )
     acc_side[...] = joined
-    gone = -jnp.sum(acc_row[0:1, :], keepdims=True)
-    out_sum = jnp.broadcast_to(jnp.sum(acc_out[...], axis=1, keepdims=True), (HEAD, LANES))
     core = core_ref[0]
     for side, part in ((keep, core), (give, 1 - core)):
         for q in range(peers // 2):
@@ -646,40 +665,21 @@
             side[q, 0:share, :] = acc_two[mine, 0:LANES]
             side[q, share : 2 * share, :] = acc_two[mine, LANES : 2 * LANES]
             side[q, 2 * share : 3 * share, :] = acc_side[mine, :]
-            at = 3 * share
-            side[q, at : at + 8, :] = jnp.broadcast_to(gone, (8, LANES))
-            side[q, at + 8 : at + 8 + HEAD, :] = out_sum
-
-
-def finish_kernel(
-    critic_in,
-    actor_kept,
-    actor_in,
-    best_kept,
-    best_in,
-    old,
-    a_one,
-    a_bias_one,
-    a_two,
-    a_bias_two,
-    a_three,
-    a_bias_three,
-    c_one,
-    c_bias_one,
-    c_two,
-    c_bias_two,
-    c_three,
-    c_bias_three,
-    g_alpha,
-    new,
-    best,
-):
+
+
+def finish_kernel(critic_in, old, *refs):
+    actor_in, best_in, outs = refs[:2], refs[2:4], refs[4:]
+    a_one, a_bias_one, a_two, a_bias_two, a_three, a_bias_three = outs[:6]
+    c_one, c_bias_one, c_two, c_bias_two, c_three, c_bias_three, g_alpha, new, best = outs[6:]
     peers = critic_in.shape[0]
     share = HID // peers
     depth = old.shape[0]
 
     def actor_total(start, size):
-        return actor_kept[start : start + size, :] + actor_in[start : start + size, :]
+        value = actor_in[0][start : start + size, :]
+        for ref in actor_in[1:]:
+            value = value + ref[start : start + size, :]
+        return value
 
     def total(ref, start, size):
         value = ref[0, start : start + size, :]
@@ -714,7 +714,8 @@
     c_bias_three[...] = (critic_scale * both)[:, 0:2]
     for t in range(2):
         a_two[:, t * LANES : (t + 1) * LANES] = actor_scale * actor_total(t * share, share)
-    small = jnp.transpose(actor_scale * actor_total(2 * share, share))
+    flat = actor_scale * actor_total(2 * share, share)
+    small = jnp.transpose(flat)
     for j in range(OBS):
         a_one[j] = small[j : j + 1, :]
     a_bias_one[...] = small[JOIN - 1 : JOIN, :]
@@ -722,14 +723,13 @@
         a_three[j] = small[JOIN + 1 + j : JOIN + 2 + j, :]
         a_three[ACT + j] = small[JOIN + 9 + j : JOIN + 10 + j, :]
     a_bias_two[...] = small[JOIN + HEAD : JOIN + HEAD + 1, :]
-    sums = actor_total(3 * share, 8 + HEAD)
-    g_alpha[...] = (actor_scale * sums[0:1, :])[:, 0:1]
-    biases = jnp.zeros((1, LANES), F32)
-    for j in range(ACT):
-        biases = jnp.where(lane == j, sums[8 + 1 + j : 8 + 2 + j, :], biases)
-        biases = jnp.where(lane == ACT + j, sums[8 + 9 + j : 8 + 10 + j, :], biases)
-    a_bias_three[...] = (actor_scale * biases)[:, 0 : 2 * ACT]
-    best[...] = jnp.maximum(best_kept[...], best_in[...])[:, 0:1]
+    g_alpha[...] = flat[0:1, JOIN + HEAD + 1 : JOIN + HEAD + 2]
+    a_bias_three[:, 0:ACT] = flat[0:1, OUT_LANE + 1 : OUT_LANE + 1 + ACT]
+    a_bias_three[:, ACT : 2 * ACT] = flat[0:1, OUT_LANE + 9 : OUT_LANE + 9 + ACT]
+    largest = best_in[0][...]
+    for ref in best_in[1:]:
+        largest = jnp.maximum(largest, ref[...])
+    best[...] = largest[:, 0:1]
 
 
 SMEM = pl.BlockSpec(memory_space=pltpu.SMEM)
@@ -786,12 +786,15 @@
     critic_one = jnp.transpose(critic_w1[0], (2, 0, 1))
     target_one = jnp.transpose(target_w1[0], (2, 0, 1))
     critic_rows = 5 * share + depth + 8
-    actor_rows = 3 * share + 8 + HEAD
-    critic_send = pl.pallas_call(
+    actor_rows = 3 * share
+    critic_send, small = pl.pallas_call(
         functools.partial(critic_kernel, peers),
-        out_shape=jax.ShapeDtypeStruct((peers, critic_rows, LANES), F32),
+        out_shape=(
+            jax.ShapeDtypeStruct((peers, critic_rows, LANES), F32),
+            jax.ShapeDtypeStruct((SMALL, HID), F32),
+        ),
         in_specs=[VMEM] * 2 + [SMEM] * 3 + [VMEM] * 24,
-        out_specs=VMEM,
+        out_specs=(VMEM, VMEM),
         scratch_shapes=[
             pltpu.VMEM((5, HID, 3 * JOIN), BF16),
             pltpu.VMEM((5, 2, HID, HID), BF16),
@@ -800,13 +803,13 @@
             pltpu.VMEM((5, HID, LANES), F32),
             pltpu.VMEM((4, HID, LANES), F32),
             pltpu.VMEM((HEAD, LANES), F32),
-            pltpu.VMEM((2 * STREAMS, JOIN, CHUNK), F32),
-            pltpu.VMEM((JOIN, HID), F32),
+            pltpu.VMEM((2 * CRITIC_STREAMS, JOIN, CRITIC_BLOCKS * LANES), F32),
             pltpu.VMEM((2, HID, HID), F32),
-            pltpu.VMEM((2, HID, 2 * JOIN), F32),
+            pltpu.VMEM((2, 2 * JOIN, HID), F32),
             pltpu.VMEM((4, HID, LANES), F32),
             pltpu.VMEM((peers * depth, 2 * LANES), F32),
-            pltpu.VMEM((8, CHUNK), F32),
+            pltpu.VMEM((8, CRITIC_BLOCKS * LANES), F32),
+            pltpu.VMEM((2 * JOIN + 8, HID), F32),
         ],
         compiler_params=pltpu.CompilerParams(vmem_limit_bytes=CRITIC_LIMIT),
         cost_estimate=pl.CostEstimate(flops=20 * 10**9, bytes_accessed=4 * 10**6, transcendentals=10**7),
@@ -846,7 +849,7 @@
     kept, given = pl.pallas_call(
         functools.partial(actor_kernel, peers),
         out_shape=(jax.ShapeDtypeStruct((peers // 2, actor_rows, LANES), F32),) * 2,
-        in_specs=[SMEM] + [VMEM] * 2 + [SMEM] * 2 + [VMEM] * 12,
+        in_specs=[SMEM] + [VMEM] * 7,
         out_specs=(VMEM, VMEM),
         scratch_shapes=[
             pltpu.VMEM((3, HID, 3 * JOIN), BF16),
@@ -854,18 +857,17 @@
             pltpu.VMEM((3, 2, HID, HID), BF16),
             pltpu.VMEM((1, 2, HEAD, HID), BF16),
             pltpu.VMEM((HID, 3 * HEAD), BF16),
-            pltpu.VMEM((2, 2, 8, HID), BF16),
+            pltpu.VMEM((2, 2, 16, HID), BF16),
             pltpu.VMEM((3, HID, LANES), F32),
             pltpu.VMEM((2, HID, LANES), F32),
             pltpu.VMEM((HEAD, LANES), F32),
-            pltpu.VMEM((STREAMS, JOIN, CHUNK), F32),
-            pltpu.VMEM((JOIN, HID), F32),
+            pltpu.VMEM((ACTOR_STREAMS, JOIN, ACTOR_BLOCKS * LANES), F32),
             pltpu.VMEM((HID, HID), F32),
             pltpu.VMEM((HID, 2 * JOIN), F32),
             pltpu.VMEM((HID, 2 * HEAD), F32),
             pltpu.VMEM((HID, LANES), F32),
             pltpu.VMEM((HEAD, LANES), F32),
-            pltpu.VMEM((8, CHUNK), F32),
+            pltpu.VMEM((8, ACTOR_BLOCKS * LANES), F32),
         ],
         compiler_params=pltpu.CompilerParams(vmem_limit_bytes=ACTOR_LIMIT),
         cost_estimate=pl.CostEstimate(flops=20 * 10**9, bytes_accessed=4 * 10**6, transcendentals=10**7),
@@ -874,20 +876,11 @@
         (me % 2).reshape(1),
         valid_counts,
         log_alpha.reshape(1, 1),
-        actor_b3,
-        critic_b3,
         states,
         noise_now,
-        actor_one,
-        actor_b1,
+        small,
         actor_w2[0],
-        actor_b2,
-        actor_three,
-        critic_one,
-        critic_b1[0],
         critic_w2[0],
-        critic_b2[0],
-        critic_w3[0],
     )
     at = 5 * share + depth + 4
     best = jnp.max(critic_in[:, at : at + 1, :], axis=0)
@@ -907,6 +900,7 @@
             best = jnp.maximum(best, best_in)
             best_in = lax.ppermute(best, "seed", [(k, k ^ (1 << (bit - 1))) for k in range(agents)])
         actor_in, best_in = lax.optimization_barrier((actor_in, best_in))
+    actor_parts, bests = (kept[0], actor_in[0]), (best, best_in)
     shape = jax.ShapeDtypeStruct
     outs = pl.pallas_call(
         finish_kernel,
@@ -931,7 +925,7 @@
         out_specs=(VMEM,) * 15,
         compiler_params=pltpu.CompilerParams(vmem_limit_bytes=FINISH_LIMIT),
         name="finish",
-    )(critic_in, kept[0], actor_in[0], best, best_in, old)
+    )(critic_in, old, *actor_parts, *bests)
     return (
         jnp.transpose(outs[0], (1, 2, 0)),
         outs[1],

time: 76.3 us -> 71.7 us (0.940)
  Pallas kernels: 30.5 us -> 28.4 us
  starting transfers between devices: 36.7 us -> 35.8 us
    ppermute x2, starting transfers between devices: 1.53 us -> 3.48 us  [shards(): lax.ppermute(given, 'dp', [(k, k ^ 1 << bit) for k in range(peers)])]
    pallas_call x1, Pallas kernels: 12.9 us -> 11.5 us  [shards(): pl.pallas_call(functools.partial(actor_kernel, peers), out_shape=(jax.Sha...]
    ppermute x2, starting transfers between devices: 5.57 us -> 4.22 us  [shards(): lax.ppermute(best, 'seed', [(k, k ^ 1 << bit - 1) for k in range(agents)])]
    ppermute x2, waiting for transfers between devices: 2.59 us -> 1.73 us  [shards(): lax.ppermute(given, 'dp', [(k, k ^ 1 << bit) for k in range(peers)])]
    all_to_all x1, starting transfers between devices: 18 us -> 17.2 us  [shards(): lax.all_to_all(critic_send, 'dp', split_axis=0, concat_axis=0, tiled=True)]
  transfers between devices with their start and end apart: 6 -> 6, of which waited for: 3 -> 4; matrix products, arithmetic and copies ran while one was open for 0% -> 0% of each run, Pallas kernels for 17% -> 16%
where the time goes in v3:
time: 71.7 us; the launch traced here: 71.4 us
  starting transfers between devices  35.8 us (50%)
  Pallas kernels  28.4 us (40%)
  waiting for transfers between devices  4.89 us (7%)
  between operations  2.2 us (3%)
    all_to_all x1, starting transfers between devices, shards(): lax.all_to_all(critic_send, 'dp', split_axis=0, concat_axis=0, tiled=True)  17.2 us
    pallas_call x1, Pallas kernels, shards(): pl.pallas_call(functools.partial(critic_kernel, peers), out_shape=(jax.Sh...  16.1 us
    pallas_call x1, Pallas kernels, shards(): pl.pallas_call(functools.partial(actor_kernel, peers), out_shape=(jax.Sha...  11.5 us
    ppermute x1, starting transfers between devices, shards(): actor_in = lax.ppermute(given, 'dp', [(k, k ^ 1) for k in range(peers)])  10.9 us
    ppermute x2, starting transfers between devices, shards(): lax.ppermute(best, 'seed', [(k, k ^ 1 << bit - 1) for k in range(agents)])  4.22 us
    ppermute x2, starting transfers between devices, shards(): lax.ppermute(given, 'dp', [(k, k ^ 1 << bit) for k in range(peers)])  3.48 us
    ppermute x2, waiting for transfers between devices, shards(): lax.ppermute(best, 'seed', [(k, k ^ 1 << bit - 1) for k in range(agents)])  2.08 us
    ppermute x2, waiting for transfers between devices, shards(): lax.ppermute(given, 'dp', [(k, k ^ 1 << bit) for k in range(peers)])  1.73 us
  transfers between devices with their start and end apart: 6, of which 4 were waited for; matrix products, arithmetic and copies ran while one was open for 0% of the time, Pallas kernels for 16%

profile of v3, /device:TPU:0, one launch (start us, length us, event | category | flops | bytes accessed | tf_op | source)
XLA Modules:
  0.0 71.4 jit_solution(12655400522463433930)
XLA Ops:
  1.9 16.1 %critic.1 = (f32[8,200,128]{2,1,0:T(8,128)}, f32[112,256]{1,0:T(8,128)}) custom-call(s32[1,1]{1,0:T(1,128)S(6)} %copy.50.count_ref, f32[1,1]{1,0:T(1,128)} %bitcast.57.temper_ref, f32[1,12]{1,0:T(1,128)} %actor_b3.1, f32[1,2]{1,0:T(1,128)} %critic_b3.1, f32[1,2]{1,0:T(1,128)} %target_b3.1, f32[544,128]{1,0:T(8,128)} %bitcast.63, f32[192,128]{1,0:T(8,128)} %bitcast.73, ...), custom_call_target="tpu_custom_call" | custom-call | flops 20000000000 | bytes 4000000 | tf_op jit(solution)/shard_map/critic/pallas_call | solution.py:790
  18.1 0.0 copy-start.1
  18.1 0.0 copy-start.2
  18.1 0.0 copy-start.3
  18.1 0.0 copy-start.4
  18.1 0.0 copy-start.5
  18.1 17.2 %all-to-all-start = ((f32[8,200,128]{2,1,0:T(8,128)}), f32[8,200,128]{2,1,0:T(8,128)S(1)}, u32[]{:S(2)}, u32[]{:S(2)}) async-start(f32[8,200,128]{2,1,0:T(8,128)} %get-tuple-element.38), calls=%async_computation | async-start | bytes 1638400 | tf_op jit(solution)/shard_map/all_to_all | solution.py:848
  35.4 0.0 copy-done.1
  35.4 0.0 copy-done.2
  35.4 0.0 copy-done.3
  35.4 0.0 copy-done.4
  35.4 0.0 copy-done.5
  35.4 11.5 %actor.1 = (f32[4,96,128]{2,1,0:T(8,128)S(1)}, f32[4,96,128]{2,1,0:T(8,128)S(1)}) custom-call(s32[1]{0:T(128)} %bitcast.26.core_ref, s32[1,1]{1,0:T(1,128)S(6)} %copy.50.count_ref, f32[1,1]{1,0:T(1,128)} %bitcast.58.temper_ref, f32[544,128]{1,0:T(8,128)S(1)} %bitcast.64, f32[192,128]{1,0:T(8,128)S(1)} %bitcast.67, f32[112,256]{1,0:T(8,128)S(1)} %copy-done.5, ...), custom_call_target="tpu_custom_call" | custom-call | flops 20000000000 | bytes 4000000 | tf_op jit(solution)/shard_map/actor/pallas_call | solution.py:849
  46.9 10.9 %collective-permute-start = (f32[4,96,128]{2,1,0:T(8,128)S(1)}, f32[4,96,128]{2,1,0:T(8,128)S(1)}, u32[]{:S(2)}, u32[]{:S(2)}) collective-permute-start(f32[4,96,128]{2,1,0:T(8,128)S(1)} %get-tuple-element.41), channel_id=1, source_target_pairs={{0,1},{1,0},{2,3},{3,2},{4,5},{5,4},{6,7},{7,6},{8,9},{9,8},{10,11... | collective-permute-start | bytes 589832 | tf_op jit(solution)/shard_map/ppermute | solution.py:891
  57.8 1.1 %collective-permute-done = f32[4,96,128]{2,1,0:T(8,128)S(1)} collective-permute-done((f32[4,96,128]{2,1,0:T(8,128)S(1)}, f32[4,96,128]{2,1,0:T(8,128)S(1)}, u32[]{:S(2)}, u32[]{:S(2)}) %collective-permute-start) | collective-permute-done | bytes 196640 | tf_op jit(solution)/shard_map/ppermute | solution.py:891
  58.9 1.7 %collective-permute-start.1 = (f32[2,96,128]{2,1,0:T(8,128)S(1)}, f32[2,96,128]{2,1,0:T(8,128)S(1)}, u32[]{:S(2)}, u32[]{:S(2)}) collective-permute-start(f32[2,96,128]{2,1,0:T(8,128)S(1)} %dynamic-slice_bitcast_fusion), channel_id=1, source_target_pairs={{0,2},{1,3},{2,0},{3,1},{4,6},{5,7},{6,4},{7,5},{8,10},{9,11},{10,... | collective-permute-start | bytes 294920 | tf_op jit(solution)/shard_map/ppermute | solution.py:898
  60.6 0.0 all-to-all-done.critic_in
  60.7 1.6 %collective-permute-start.2 = (f32[1,128]{1,0:T(1,128)S(1)}, f32[1,128]{1,0:T(1,128)S(1)}, u32[]{:S(2)}, u32[]{:S(2)}) collective-permute-start(f32[1,128]{1,0:T(1,128)S(1)} %bitcast.70), channel_id=1, source_target_pairs={{0,8},{8,0},{16,24},{24,16},{1,9},{9,1},{17,25},{25,17},{2,10},{10... | collective-permute-start | bytes 1544 | tf_op jit(solution)/shard_map/ppermute | solution.py:901
  62.3 1.7 %collective-permute-done.1 = f32[2,96,128]{2,1,0:T(8,128)S(1)} collective-permute-done((f32[2,96,128]{2,1,0:T(8,128)S(1)}, f32[2,96,128]{2,1,0:T(8,128)S(1)}, u32[]{:S(2)}, u32[]{:S(2)}) %collective-permute-start.1) | collective-permute-done | bytes 98336 | tf_op jit(solution)/shard_map/ppermute | solution.py:898
  64.0 0.2 collective-permute-done.2
  64.3 0.0 copy-start
  64.3 1.7 %collective-permute-start.3 = (f32[1,96,128]{2,1,0:T(8,128)S(1)}, f32[1,96,128]{2,1,0:T(8,128)S(1)}, u32[]{:S(2)}, u32[]{:S(2)}) collective-permute-start(f32[1,96,128]{2,1,0:T(8,128)S(1)} %get-tuple-element.61), channel_id=1, source_target_pairs={{0,4},{1,5},{2,6},{3,7},{4,0},{5,1},{6,2},{7,3},{8,12},{9,13},{10,... | collective-permute-start | bytes 147464 | tf_op jit(solution)/shard_map/ppermute | solution.py:898
  66.1 2.6 %collective-permute-start.4 = (f32[1,128]{1,0:T(1,128)S(1)}, f32[1,128]{1,0:T(1,128)S(1)}, u32[]{:S(2)}, u32[]{:S(2)}) collective-permute-start(f32[1,128]{1,0:T(1,128)S(1)} %bitcast_maximum_fusion.refs_2_), channel_id=1, source_target_pairs={{0,16},{8,24},{16,0},{24,8},{1,17},{9,25},{17,1},{25,9},{2,18},{10... | collective-permute-start | bytes 1544 | tf_op jit(solution)/shard_map/ppermute | solution.py:901
  68.6 1.8 %collective-permute-done.4.refs_3_ = f32[1,128]{1,0:T(1,128)S(1)} collective-permute-done((f32[1,128]{1,0:T(1,128)S(1)}, f32[1,128]{1,0:T(1,128)S(1)}, u32[]{:S(2)}, u32[]{:S(2)}) %collective-permute-start.4) | collective-permute-done | bytes 544 | tf_op jit(solution)/shard_map/ppermute | solution.py:901
  70.5 0.0 collective-permute-done.3
  70.5 0.0 copy-done
  70.5 0.8 %finish.1 = (f32[17,1,32]{2,1,0:T(1,128)}, f32[1,32]{1,0:T(1,128)}, f32[32,256]{1,0:T(8,128)}, f32[1,32]{1,0:T(1,128)}, f32[12,1,32]{2,1,0:T(1,128)}, /*index=5*...) custom-call(f32[8,200,128]{2,1,0:T(8,128)S(1)} %all-to-all-done.crit, ...), custom_call_target="tpu_custom_call" | custom-call | tf_op jit(solution)/shard_map/finish/pallas_call | solution.py:905
  (6 shorter events, 0.1 us)
Async XLA Ops:
  18.1 17.3 %copy-start.1 = (f32[1,2,256,256]{3,2,1,0:T(8,128)S(1)}, f32[1,2,256,256]{3,2,1,0:T(8,128)}, u32[]{:S(2)}) copy-start(f32[1,2,256,256]{3,2,1,0:T(8,128)} %param.51) | copy-start | bytes 1572868
  18.1 17.3 %copy-start.2 = (f32[1,17,4096]{2,0,1:T(1,128)S(1)}, f32[1,17,4096]{2,0,1:T(1,128)}, u32[]{:S(2)}) copy-start(f32[1,17,4096]{2,0,1:T(1,128)} %param.31) | copy-start | bytes 835588
  18.1 17.3 %copy-start.3 = (f32[1,256,256]{2,1,0:T(8,128)S(1)}, f32[1,256,256]{2,1,0:T(8,128)}, u32[]{:S(2)}) copy-start(f32[1,256,256]{2,1,0:T(8,128)} %param.45) | copy-start | bytes 786436
  18.1 17.3 %copy-start.4 = (f32[1,6,4096]{2,0,1:T(1,128)S(1)}, f32[1,6,4096]{2,0,1:T(1,128)}, u32[]{:S(2)}) copy-start(f32[1,6,4096]{2,0,1:T(1,128)} %param.36) | copy-start | bytes 294916
  18.1 17.3 %copy-start.5 = (f32[112,256]{1,0:T(8,128)S(1)}, f32[112,256]{1,0:T(8,128)}, u32[]{:S(2)}) copy-start(f32[112,256]{1,0:T(8,128)} %get-tuple-element.39.small) | copy-start | bytes 344068
  18.1 42.5 %all-to-all-start = ((f32[8,200,128]{2,1,0:T(8,128)}), f32[8,200,128]{2,1,0:T(8,128)S(1)}, u32[]{:S(2)}, u32[]{:S(2)}) async-start(f32[8,200,128]{2,1,0:T(8,128)} %get-tuple-element.38), calls=%async_computation | async-start | bytes 1638400 | tf_op jit(solution)/shard_map/all_to_all | solution.py:848
  46.9 11.9 %collective-permute-start = (f32[4,96,128]{2,1,0:T(8,128)S(1)}, f32[4,96,128]{2,1,0:T(8,128)S(1)}, u32[]{:S(2)}, u32[]{:S(2)}) collective-permute-start(f32[4,96,128]{2,1,0:T(8,128)S(1)} %get-tuple-element.41), channel_id=1, source_target_pairs={{0,1},{1,0},{2,3},{3,2},{4,5},{5,4},{6,7},{7,6},{8,9},{9,8},{10,11... | collective-permute-start | bytes 589832 | tf_op jit(solution)/shard_map/ppermute | solution.py:891
  58.9 5.1 %collective-permute-start.1 = (f32[2,96,128]{2,1,0:T(8,128)S(1)}, f32[2,96,128]{2,1,0:T(8,128)S(1)}, u32[]{:S(2)}, u32[]{:S(2)}) collective-permute-start(f32[2,96,128]{2,1,0:T(8,128)S(1)} %dynamic-slice_bitcast_fusion), channel_id=1, source_target_pairs={{0,2},{1,3},{2,0},{3,1},{4,6},{5,7},{6,4},{7,5},{8,10},{9,11},{10,... | collective-permute-start | bytes 294920 | tf_op jit(solution)/shard_map/ppermute | solution.py:898
  60.7 3.6 %collective-permute-start.2 = (f32[1,128]{1,0:T(1,128)S(1)}, f32[1,128]{1,0:T(1,128)S(1)}, u32[]{:S(2)}, u32[]{:S(2)}) collective-permute-start(f32[1,128]{1,0:T(1,128)S(1)} %bitcast.70), channel_id=1, source_target_pairs={{0,8},{8,0},{16,24},{24,16},{1,9},{9,1},{17,25},{25,17},{2,10},{10... | collective-permute-start | bytes 1544 | tf_op jit(solution)/shard_map/ppermute | solution.py:901
  64.3 6.2 %copy-start = (f32[1,4096]{1,0:T(1,128)S(1)}, f32[1,4096]{1,0:T(1,128)}, u32[]{:S(2)}) copy-start(f32[1,4096]{1,0:T(1,128)} %param.42) | copy-start | bytes 49156
  64.3 6.2 %collective-permute-start.3 = (f32[1,96,128]{2,1,0:T(8,128)S(1)}, f32[1,96,128]{2,1,0:T(8,128)S(1)}, u32[]{:S(2)}, u32[]{:S(2)}) collective-permute-start(f32[1,96,128]{2,1,0:T(8,128)S(1)} %get-tuple-element.61), channel_id=1, source_target_pairs={{0,4},{1,5},{2,6},{3,7},{4,0},{5,1},{6,2},{7,3},{8,12},{9,13},{10,... | collective-permute-start | bytes 147464 | tf_op jit(solution)/shard_map/ppermute | solution.py:898
  66.1 4.4 %collective-permute-start.4 = (f32[1,128]{1,0:T(1,128)S(1)}, f32[1,128]{1,0:T(1,128)S(1)}, u32[]{:S(2)}, u32[]{:S(2)}) collective-permute-start(f32[1,128]{1,0:T(1,128)S(1)} %bitcast_maximum_fusion.refs_2_), channel_id=1, source_target_pairs={{0,16},{8,24},{16,0},{24,8},{1,17},{9,25},{17,1},{25,9},{2,18},{10... | collective-permute-start | bytes 1544 | tf_op jit(solution)/shard_map/ppermute | solution.py:901

commit v4 on v3

--- a/solution.py
+++ b/solution.py
@@ -34,6 +34,7 @@
 HEAD = 16
 CRITIC_BLOCKS, CRITIC_STREAMS, CRITIC_LAG = 4, 4, 2000
 ACTOR_BLOCKS, ACTOR_STREAMS = 8, 2
+SOURCES = 29
 CRITIC_LIMIT = 56 * 1024 * 1024
 ACTOR_LIMIT = 36 * 1024 * 1024
 FINISH_LIMIT = 8 * 1024 * 1024
@@ -63,7 +64,7 @@
     return dot(weight[0], high) + dot(weight[0], low) + dot(weight[1], high)
 
 
-def dot3_few(weight, value):
+def dot3_joint(weight, value):
     rows = weight[0].shape[0]
     both = dot(jnp.concatenate(weight, axis=0), value[0])
     return both[:rows] + both[rows:] + dot(weight[0], value[1])
@@ -131,7 +132,7 @@
         if unit is None:
             advance(task, start)
         else:
-            cost = cost * 3 // 2 if unit == "vpu" else cost
+            cost = cost * 2 if unit == "vpu" else cost
             free[unit] = start + cost
             advance(task, start + cost)
 
@@ -234,61 +235,38 @@
     return jnp.broadcast_to(value, (1, LANES))
 
 
-def critic_kernel(
-    peers,
-    count_ref,
-    temper_ref,
-    actor_b3,
-    critic_b3,
-    target_b3,
-    states,
-    actions,
-    rewards,
-    next_states,
-    dones,
-    noise_next,
-    probs,
-    owners,
-    slots,
-    actor_w1,
-    actor_b1,
-    actor_w2,
-    actor_b2,
-    actor_w3,
-    critic_w1,
-    critic_b1,
-    critic_w2,
-    critic_b2,
-    critic_w3,
-    target_w1,
-    target_b1,
-    target_w2,
-    target_b2,
-    target_w3,
-    send,
-    small,
-    one,
-    two,
-    back,
-    head,
-    bias_two,
-    last,
-    wide_bias,
-    join,
-    acc_two,
-    acc_one,
-    acc_side,
-    acc_table,
-    acc_row,
-    turn,
-):
-    count = jnp.max(count_ref[...].astype(F32)).astype(jnp.int32)
-    alpha = jnp.exp(temper_ref[...])
+def critic_kernel(peers, *refs):
+    sources, refs = refs[:SOURCES], refs[SOURCES:]
+    (send, small), refs = refs[:2], refs[2:]
+    places, refs = refs[:SOURCES], refs[SOURCES:]
+    one, two, back, head, bias_two, last, wide_bias, join = refs[:8]
+    acc_two, acc_one, acc_side, acc_table, acc_row, turn, arrived = refs[8:]
+    copies = [
+        pltpu.make_async_copy(source, place, arrived.at[k])
+        for k, (source, place) in enumerate(zip(sources, places))
+    ]
+    for copy in copies:
+        copy.start()
+    count_ref, temper_ref, actor_b3, critic_b3, target_b3 = places[:5]
+    actor_w1, actor_b1, actor_b2, actor_w3 = places[5:9]
+    critic_w1, critic_b1, critic_b2, critic_w3 = places[9:13]
+    target_w1, target_b1, target_b2, target_w3 = places[13:17]
+    actor_w2, target_w2, critic_w2 = places[17:20]
+    states, actions, rewards, next_states, dones, noise_next, probs, owners, slots = places[20:]
+    acc_two[...] = jnp.zeros_like(acc_two)
+    acc_one[...] = jnp.zeros_like(acc_one)
+    acc_side[...] = jnp.zeros_like(acc_side)
+    acc_table[...] = jnp.zeros_like(acc_table)
+    acc_row[...] = jnp.zeros_like(acc_row)
+    small[...] = jnp.zeros_like(small)
+    for copy in copies[:17]:
+        copy.wait()
+    count = count_ref[0, 0]
+    alpha = jnp.exp(temper_ref[0, 0])
     share = HID // peers
     blocks = CRITIC_BLOCKS
     width = blocks * LANES
     depth = acc_table.shape[0] // peers
-    small[...] = jnp.zeros_like(small)
     fill_first(small, 0, actor_w1, actor_b1[...], 0)
     for k in range(2):
         fill_first(small, (1 + k) * JOIN, critic_w1, critic_b1[k : k + 1, :], k)
@@ -301,31 +279,31 @@
     turn[2 * JOIN : 2 * JOIN + 2, :] = 0.5 * target_b2[...]
     turn[2 * JOIN + 2 : 2 * JOIN + 4, :] = target_w3[...]
     turn[2 * JOIN + 4 : 2 * JOIN + 8, :] = jnp.zeros((4, HID), F32)
+    wide_bias[...] = head_bias(actor_b3)
+    small[BIAS_ROW : BIAS_ROW + HEAD, 0:LANES] = wide_bias[...]
+    for k in range(2):
+        small[BIAS_ROW + k : BIAS_ROW + k + 1, LANES:] = jnp.full((1, LANES), critic_b3[0, k])
+    store_split(head, 0, small[HEAD_ROW : HEAD_ROW + HEAD, :])
     one[0] = stack_weight(0.5 * small[0:JOIN, :])
-    store_split(two, 0, 0.5 * actor_w2[...])
     given = columns(small[REST_ROW : REST_ROW + 8, :])
     aims = columns(turn[2 * JOIN : 2 * JOIN + 8, :])
     bias_two[0] = given[0]
     for k in range(2):
         one[1 + k] = stack_weight(0.5 * turn[k * JOIN : (k + 1) * JOIN, :])
         one[3 + k] = stack_weight(0.5 * small[(1 + k) * JOIN : (2 + k) * JOIN, :])
-        store_split(two, 1 + k, 0.5 * target_w2[k])
-        store_split(two, 3 + k, 0.5 * critic_w2[k])
         bias_two[1 + k] = aims[k]
         bias_two[3 + k] = given[1 + k]
         last[k] = aims[2 + k]
         last[2 + k] = given[3 + k]
+    for copy in copies[17:20]:
+        copy.wait()
+    store_split(two, 0, 0.5 * actor_w2[...])
+    for k in range(2):
+        store_split(two, 1 + k, 0.5 * target_w2[k])
+        store_split(two, 3 + k, 0.5 * critic_w2[k])
         store_split(back, k, back_weights(critic_w2[k], last[2 + k]))
-    store_split(head, 0, small[HEAD_ROW : HEAD_ROW + HEAD, :])
-    wide_bias[...] = head_bias(actor_b3)
-    small[BIAS_ROW : BIAS_ROW + HEAD, 0:LANES] = wide_bias[...]
-    for k in range(2):
-        small[BIAS_ROW + k : BIAS_ROW + k + 1, LANES:] = jnp.full((1, LANES), critic_b3[0, k])
-    acc_two[...] = jnp.zeros_like(acc_two)
-    acc_one[...] = jnp.zeros_like(acc_one)
-    acc_side[...] = jnp.zeros_like(acc_side)
-    acc_table[...] = jnp.zeros_like(acc_table)
-    acc_row[...] = jnp.zeros_like(acc_row)
+    for copy in copies[20:]:
+        copy.wait()
 
     def next_action(first, known, lane):
         yield "mxu", 64
@@ -340,7 +318,7 @@
         yield "vpu", 130
         hidden = split(activate(half + wide(bias_two[0], blocks)))
         yield "mxu", 128
-        out = dot3_few(pair(head, 0), hidden)
+        out = dot3_joint(pair(head, 0), hidden)
         yield "vpu", 100
         join[lane, OBS : OBS + ACT, :] = load_chunk(noise_next, ACT, first, blocks)
         action, known["logp"], _, _ = squash(out + wide(wide_bias[...], blocks), join[lane, 16:24, :])
@@ -561,12 +539,12 @@
         hidden, slope_one = activate_slope(half)
         hidden_one = split(hidden)
         yield "mxu", 192
-        half = dot3(pair(two, 0), hidden_one)
+        half = dot3_joint(pair(two, 0), hidden_one)
         yield "vpu", 170
         hidden, slope_two = activate_slope(half + wide(bias_two[0], blocks))
         hidden_two = split(hidden)
         yield "mxu", 128
-        out = dot3_few(pair(head, 0), hidden_two)
+        out = dot3_joint(pair(head, 0), hidden_two)
         yield "vpu", 100
         action, logp, spread, bend = squash(out + wide(wide_bias[...], blocks), noise)
         acc_row[0:1, :] += known["mask"] * (logp + ENTROPY_AIM)
@@ -588,7 +566,7 @@
         acc_side[...] += fold(grad)
         grad_two = split(grad)
         yield "mxu", 192
-        half = dot3(pair(back, 0), grad_two)
+        half = dot3_joint(pair(back, 0), grad_two)
         yield "vpu", 90
         grad_one = split(half * slope_one)
         yield "mxu", 128
@@ -606,18 +584,18 @@
         hidden, slope_one = activate_slope(half)
         hidden_one = split(hidden)
         yield "mxu", 192
-        half = dot3(pair(two, 1 + k), hidden_one)
+        half = dot3_joint(pair(two, 1 + k), hidden_one)
         yield "vpu", 220
         hidden, slope_two = activate_slope(half + wide(bias_two[1 + k], blocks))
         value = jnp.sum(hidden * wide(last[k], blocks), axis=0, keepdims=True) + critic_b3[k]
         known["value", k] = value
         grad_two = split(slope_two)
         yield "mxu", 192
-        half = dot3(pair(back, 1 + k), grad_two)
+        half = dot3_joint(pair(back, 1 + k), grad_two)
         yield "vpu", 90
         grad_one = split(half * slope_one)
         yield "mxu", 128
-        known["pull", k] = dot3_few(pair(entry, k), grad_one)[8:]
+        known["pull", k] = dot3_joint(pair(entry, k), grad_one)[8:]
 
     def mix(first, known):
         for k in range(2):
@@ -733,6 +711,7 @@
 
 
 SMEM = pl.BlockSpec(memory_space=pltpu.SMEM)
+HBM = pl.BlockSpec(memory_space=pltpu.HBM)
 VMEM = pl.BlockSpec(memory_space=pltpu.VMEM)
 
 
@@ -787,15 +766,50 @@
     target_one = jnp.transpose(target_w1[0], (2, 0, 1))
     critic_rows = 5 * share + depth + 8
     actor_rows = 3 * share
+    sources = (
+        valid_counts,
+        log_alpha.reshape(1, 1),
+        actor_b3,
+        critic_b3,
+        target_b3,
+        actor_one,
+        actor_b1,
+        actor_b2,
+        actor_three,
+        critic_one,
+        critic_b1[0],
+        critic_b2[0],
+        critic_w3[0],
+        target_one,
+        target_b1[0],
+        target_b2[0],
+        target_w3[0],
+        actor_w2[0],
+        target_w2[0],
+        critic_w2[0],
+        states,
+        actions,
+        rewards,
+        next_states,
+        dones,
+        noise_next,
+        probs,
+        owners,
+        slots,
+    )
     critic_send, small = pl.pallas_call(
         functools.partial(critic_kernel, peers),
         out_shape=(
             jax.ShapeDtypeStruct((peers, critic_rows, LANES), F32),
             jax.ShapeDtypeStruct((SMALL, HID), F32),
         ),
-        in_specs=[VMEM] * 2 + [SMEM] * 3 + [VMEM] * 24,
+        in_specs=[HBM] * SOURCES,
         out_specs=(VMEM, VMEM),
         scratch_shapes=[
+            (pltpu.SMEM if k < 5 else pltpu.VMEM)(source.shape, source.dtype)
+            for k, source in enumerate(sources)
+        ]
+        + [
             pltpu.VMEM((5, HID, 3 * JOIN), BF16),
             pltpu.VMEM((5, 2, HID, HID), BF16),
             pltpu.VMEM((2, 2, HID, HID), BF16),
@@ -810,41 +824,12 @@
             pltpu.VMEM((peers * depth, 2 * LANES), F32),
             pltpu.VMEM((8, CRITIC_BLOCKS * LANES), F32),
             pltpu.VMEM((2 * JOIN + 8, HID), F32),
+            pltpu.SemaphoreType.DMA((SOURCES,)),
         ],
         compiler_params=pltpu.CompilerParams(vmem_limit_bytes=CRITIC_LIMIT),
         cost_estimate=pl.CostEstimate(flops=20 * 10**9, bytes_accessed=4 * 10**6, transcendentals=10**7),
         name="critic",
-    )(
-        valid_counts,
-        log_alpha.reshape(1, 1),
-        actor_b3,
-        critic_b3,
-        target_b3,
-        states,
-        actions,
-        rewards,
-        next_states,
-        dones,
-        noise_next,
-        probs,
-        owners,
-        slots,
-        actor_one,
-        actor_b1,
-        actor_w2[0],
-        actor_b2,
-        actor_three,
-        critic_one,
-        critic_b1[0],
-        critic_w2[0],
-        critic_b2[0],
-        critic_w3[0],
-        target_one,
-        target_b1[0],
-        target_w2[0],
-        target_b2[0],
-        target_w3[0],
-    )
+    )(*sources)
     critic_in = lax.all_to_all(critic_send, "dp", split_axis=0, concat_axis=0, tiled=True)
     kept, given = pl.pallas_call(
         functools.partial(actor_kernel, peers),

time: 71.7 us -> 70.9 us (0.989)
  starting transfers between devices: 35.8 us -> 34.1 us
  waiting for transfers between devices: 4.89 us -> 6.45 us
    ppermute x1, starting transfers between devices: 10.9 us -> 0.56 us  [shards(): actor_in = lax.ppermute(given, 'dp', [(k, k ^ 1) for k in range(peers)])]
    ppermute x2, starting transfers between devices: 3.48 us -> 13.6 us  [shards(): lax.ppermute(given, 'dp', [(k, k ^ 1 << bit) for k in range(peers)])]
    ppermute x2, starting transfers between devices: 4.22 us -> 2.65 us  [shards(): lax.ppermute(best, 'seed', [(k, k ^ 1 << bit - 1) for k in range(agents)])]
    ppermute x2, waiting for transfers between devices: 1.73 us -> 3.01 us  [shards(): lax.ppermute(given, 'dp', [(k, k ^ 1 << bit) for k in range(peers)])]
where the time goes in v4:
time: 70.9 us; the launch traced here: 70.6 us
  starting transfers between devices  34.1 us (48%)
  Pallas kernels  27.8 us (39%)
  waiting for transfers between devices  6.45 us (9%)
  between operations  2.22 us (3%)
    all_to_all x1, starting transfers between devices, shards(): lax.all_to_all(critic_send, 'dp', split_axis=0, concat_axis=0, tiled=True)  17.2 us
    pallas_call x1, Pallas kernels, shards(): pl.pallas_call(functools.partial(critic_kernel, peers), out_shape=(jax.Sh...  15.6 us
    ppermute x2, starting transfers between devices, shards(): lax.ppermute(given, 'dp', [(k, k ^ 1 << bit) for k in range(peers)])  13.6 us
    pallas_call x1, Pallas kernels, shards(): pl.pallas_call(functools.partial(actor_kernel, peers), out_shape=(jax.Sha...  11.3 us
    ppermute x2, waiting for transfers between devices, shards(): lax.ppermute(given, 'dp', [(k, k ^ 1 << bit) for k in range(peers)])  3.01 us
    ppermute x2, starting transfers between devices, shards(): lax.ppermute(best, 'seed', [(k, k ^ 1 << bit - 1) for k in range(agents)])  2.65 us
    ppermute x2, waiting for transfers between devices, shards(): lax.ppermute(best, 'seed', [(k, k ^ 1 << bit - 1) for k in range(agents)])  2.37 us
  transfers between devices with their start and end apart: 6, of which 4 were waited for; matrix products, arithmetic and copies ran while one was open for 0% of the time, Pallas kernels for 16%

profile of v4, /device:TPU:0, one launch (start us, length us, event | category | flops | bytes accessed | tf_op | source)
XLA Modules:
  0.0 70.6 jit_solution(15475187515202038168)
XLA Ops:
  1.9 15.6 %critic.1 = (f32[8,200,128]{2,1,0:T(8,128)}, f32[112,256]{1,0:T(8,128)}) custom-call(s32[1,1]{1,0:T(1,128)S(6)} %copy.50.refs_0_.count_ref, f32[1,1]{1,0:T(1,128)} %bitcast.57.refs_1_, f32[1,12]{1,0:T(1,128)} %refs_2_.1, f32[1,2]{1,0:T(1,128)} %refs_3_.1, f32[1,2]{1,0:T(1,128)} %refs_4_.1, f32[17,1,256]{2,1,0:T(1,128)} %bitcast.80, f32[1,256]{1,0:T(1,128)} %refs_6_.1, ...), custom_call_target="tpu_custom_call" | custom-call | flops 20000000000 | bytes 4000000 | tf_op jit(solution)/shard_map/critic/pallas_call | solution.py:800
  17.6 0.0 copy-start.1
  17.6 0.0 copy-start.2
  17.6 0.0 copy-start.3
  17.6 0.0 copy-start.4
  17.6 0.0 copy-start.5
  17.6 17.2 %all-to-all-start = ((f32[8,200,128]{2,1,0:T(8,128)}), f32[8,200,128]{2,1,0:T(8,128)S(1)}, u32[]{:S(2)}, u32[]{:S(2)}) async-start(f32[8,200,128]{2,1,0:T(8,128)} %get-tuple-element.38), calls=%async_computation | async-start | bytes 1638400 | tf_op jit(solution)/shard_map/all_to_all | solution.py:833
  34.9 0.0 copy-done.1
  34.9 0.0 copy-done.2
  34.9 0.0 copy-done.3
  34.9 0.0 copy-done.4
  34.9 0.0 copy-done.5
  34.9 11.3 %actor.1 = (f32[4,96,128]{2,1,0:T(8,128)S(1)}, f32[4,96,128]{2,1,0:T(8,128)S(1)}) custom-call(s32[1]{0:T(128)} %bitcast.26.core_ref, s32[1,1]{1,0:T(1,128)S(6)} %copy.50.refs_0_.count_ref, f32[1,1]{1,0:T(1,128)} %bitcast.58.temper_ref, f32[544,128]{1,0:T(8,128)S(1)} %bitcast.64, f32[192,128]{1,0:T(8,128)S(1)} %bitcast.67, f32[112,256]{1,0:T(8,128)S(1)} %copy-done.5, ...), custom_call_target="tpu_custom_call" | custom-call | flops 20000000000 | bytes 4000000 | tf_op jit(solution)/shard_map/actor/pallas_call | solution.py:834
  46.3 0.6 collective-permute-start
  46.8 1.1 %collective-permute-done = f32[4,96,128]{2,1,0:T(8,128)S(1)} collective-permute-done((f32[4,96,128]{2,1,0:T(8,128)S(1)}, f32[4,96,128]{2,1,0:T(8,128)S(1)}, u32[]{:S(2)}, u32[]{:S(2)}) %collective-permute-start) | collective-permute-done | bytes 196640 | tf_op jit(solution)/shard_map/ppermute | solution.py:876
  48.0 12.1 %collective-permute-start.1 = (f32[2,96,128]{2,1,0:T(8,128)S(1)}, f32[2,96,128]{2,1,0:T(8,128)S(1)}, u32[]{:S(2)}, u32[]{:S(2)}) collective-permute-start(f32[2,96,128]{2,1,0:T(8,128)S(1)} %dynamic-slice_bitcast_fusion), channel_id=1, source_target_pairs={{0,2},{1,3},{2,0},{3,1},{4,6},{5,7},{6,4},{7,5},{8,10},{9,11},{10,... | collective-permute-start | bytes 294920 | tf_op jit(solution)/shard_map/ppermute | solution.py:883
  60.1 0.0 all-to-all-done.critic_in
  60.1 0.1 collective-permute-start.2
  60.2 3.0 %collective-permute-done.1 = f32[2,96,128]{2,1,0:T(8,128)S(1)} collective-permute-done((f32[2,96,128]{2,1,0:T(8,128)S(1)}, f32[2,96,128]{2,1,0:T(8,128)S(1)}, u32[]{:S(2)}, u32[]{:S(2)}) %collective-permute-start.1) | collective-permute-done | bytes 98336 | tf_op jit(solution)/shard_map/ppermute | solution.py:883
  63.2 0.5 collective-permute-done.2
  63.7 0.0 copy-start
  63.7 1.5 %collective-permute-start.3 = (f32[1,96,128]{2,1,0:T(8,128)S(1)}, f32[1,96,128]{2,1,0:T(8,128)S(1)}, u32[]{:S(2)}, u32[]{:S(2)}) collective-permute-start(f32[1,96,128]{2,1,0:T(8,128)S(1)} %get-tuple-element.61), channel_id=1, source_target_pairs={{0,4},{1,5},{2,6},{3,7},{4,0},{5,1},{6,2},{7,3},{8,12},{9,13},{10,... | collective-permute-start | bytes 147464 | tf_op jit(solution)/shard_map/ppermute | solution.py:883
  65.3 2.6 %collective-permute-start.4 = (f32[1,128]{1,0:T(1,128)S(1)}, f32[1,128]{1,0:T(1,128)S(1)}, u32[]{:S(2)}, u32[]{:S(2)}) collective-permute-start(f32[1,128]{1,0:T(1,128)S(1)} %bitcast_maximum_fusion.refs_2_), channel_id=1, source_target_pairs={{0,16},{8,24},{16,0},{24,8},{1,17},{9,25},{17,1},{25,9},{2,18},{10... | collective-permute-start | bytes 1544 | tf_op jit(solution)/shard_map/ppermute | solution.py:886
  67.9 1.8 %collective-permute-done.4.refs_3_ = f32[1,128]{1,0:T(1,128)S(1)} collective-permute-done((f32[1,128]{1,0:T(1,128)S(1)}, f32[1,128]{1,0:T(1,128)S(1)}, u32[]{:S(2)}, u32[]{:S(2)}) %collective-permute-start.4) | collective-permute-done | bytes 544 | tf_op jit(solution)/shard_map/ppermute | solution.py:886
  69.7 0.0 collective-permute-done.3
  69.7 0.0 copy-done
  69.7 0.8 %finish.1 = (f32[17,1,32]{2,1,0:T(1,128)}, f32[1,32]{1,0:T(1,128)}, f32[32,256]{1,0:T(8,128)}, f32[1,32]{1,0:T(1,128)}, f32[12,1,32]{2,1,0:T(1,128)}, /*index=5*...) custom-call(f32[8,200,128]{2,1,0:T(8,128)S(1)} %all-to-all-done.crit, ...), custom_call_target="tpu_custom_call" | custom-call | tf_op jit(solution)/shard_map/finish/pallas_call | solution.py:890
  (6 shorter events, 0.1 us)
Async XLA Ops:
  17.6 17.3 %copy-start.1 = (f32[1,2,256,256]{3,2,1,0:T(8,128)S(1)}, f32[1,2,256,256]{3,2,1,0:T(8,128)}, u32[]{:S(2)}) copy-start(f32[1,2,256,256]{3,2,1,0:T(8,128)} %param.51) | copy-start | bytes 1572868
  17.6 17.3 %copy-start.2 = (f32[1,17,4096]{2,0,1:T(1,128)S(1)}, f32[1,17,4096]{2,0,1:T(1,128)}, u32[]{:S(2)}) copy-start(f32[1,17,4096]{2,0,1:T(1,128)} %param.31) | copy-start | bytes 835588
  17.6 17.3 %copy-start.3 = (f32[1,256,256]{2,1,0:T(8,128)S(1)}, f32[1,256,256]{2,1,0:T(8,128)}, u32[]{:S(2)}) copy-start(f32[1,256,256]{2,1,0:T(8,128)} %param.45) | copy-start | bytes 786436
  17.6 17.3 %copy-start.4 = (f32[1,6,4096]{2,0,1:T(1,128)S(1)}, f32[1,6,4096]{2,0,1:T(1,128)}, u32[]{:S(2)}) copy-start(f32[1,6,4096]{2,0,1:T(1,128)} %param.36) | copy-start | bytes 294916
  17.6 17.3 %copy-start.5 = (f32[112,256]{1,0:T(8,128)S(1)}, f32[112,256]{1,0:T(8,128)}, u32[]{:S(2)}) copy-start(f32[112,256]{1,0:T(8,128)} %get-tuple-element.39.small) | copy-start | bytes 344068
  17.6 42.4 %all-to-all-start = ((f32[8,200,128]{2,1,0:T(8,128)}), f32[8,200,128]{2,1,0:T(8,128)S(1)}, u32[]{:S(2)}, u32[]{:S(2)}) async-start(f32[8,200,128]{2,1,0:T(8,128)} %get-tuple-element.38), calls=%async_computation | async-start | bytes 1638400 | tf_op jit(solution)/shard_map/all_to_all | solution.py:833
  46.3 1.6 %collective-permute-start = (f32[4,96,128]{2,1,0:T(8,128)S(1)}, f32[4,96,128]{2,1,0:T(8,128)S(1)}, u32[]{:S(2)}, u32[]{:S(2)}) collective-permute-start(f32[4,96,128]{2,1,0:T(8,128)S(1)} %get-tuple-element.41), channel_id=1, source_target_pairs={{0,1},{1,0},{2,3},{3,2},{4,5},{5,4},{6,7},{7,6},{8,9},{9,8},{10,11... | collective-permute-start | bytes 589832 | tf_op jit(solution)/shard_map/ppermute | solution.py:876
  48.0 15.2 %collective-permute-start.1 = (f32[2,96,128]{2,1,0:T(8,128)S(1)}, f32[2,96,128]{2,1,0:T(8,128)S(1)}, u32[]{:S(2)}, u32[]{:S(2)}) collective-permute-start(f32[2,96,128]{2,1,0:T(8,128)S(1)} %dynamic-slice_bitcast_fusion), channel_id=1, source_target_pairs={{0,2},{1,3},{2,0},{3,1},{4,6},{5,7},{6,4},{7,5},{8,10},{9,11},{10,... | collective-permute-start | bytes 294920 | tf_op jit(solution)/shard_map/ppermute | solution.py:883
  60.1 3.6 %collective-permute-start.2 = (f32[1,128]{1,0:T(1,128)S(1)}, f32[1,128]{1,0:T(1,128)S(1)}, u32[]{:S(2)}, u32[]{:S(2)}) collective-permute-start(f32[1,128]{1,0:T(1,128)S(1)} %bitcast.70), channel_id=1, source_target_pairs={{0,8},{8,0},{16,24},{24,16},{1,9},{9,1},{17,25},{25,17},{2,10},{10... | collective-permute-start | bytes 1544 | tf_op jit(solution)/shard_map/ppermute | solution.py:886
  63.7 6.0 %copy-start = (f32[1,4096]{1,0:T(1,128)S(1)}, f32[1,4096]{1,0:T(1,128)}, u32[]{:S(2)}) copy-start(f32[1,4096]{1,0:T(1,128)} %param.42) | copy-start | bytes 49156
  63.7 6.0 %collective-permute-start.3 = (f32[1,96,128]{2,1,0:T(8,128)S(1)}, f32[1,96,128]{2,1,0:T(8,128)S(1)}, u32[]{:S(2)}, u32[]{:S(2)}) collective-permute-start(f32[1,96,128]{2,1,0:T(8,128)S(1)} %get-tuple-element.61), channel_id=1, source_target_pairs={{0,4},{1,5},{2,6},{3,7},{4,0},{5,1},{6,2},{7,3},{8,12},{9,13},{10,... | collective-permute-start | bytes 147464 | tf_op jit(solution)/shard_map/ppermute | solution.py:883
  65.3 4.4 %collective-permute-start.4 = (f32[1,128]{1,0:T(1,128)S(1)}, f32[1,128]{1,0:T(1,128)S(1)}, u32[]{:S(2)}, u32[]{:S(2)}) collective-permute-start(f32[1,128]{1,0:T(1,128)S(1)} %bitcast_maximum_fusion.refs_2_), channel_id=1, source_target_pairs={{0,16},{8,24},{16,0},{24,8},{1,17},{9,25},{17,1},{25,9},{2,18},{10... | collective-permute-start | bytes 1544 | tf_op jit(solution)/shard_map/ppermute | solution.py:886

commit v5 on v4

--- a/solution.py
+++ b/solution.py
@@ -74,6 +74,26 @@
     return dot_t(left[0], right[0]) + dot_t(left[0], right[1]) + dot_t(left[1], right[0])
 
 
+def store_three(ref, value):
+    rows = value.shape[0]
+    for k, part in enumerate(split_three(value)):
+        ref[k * rows : (k + 1) * rows, :] = part.astype(BF16)
+
+
+def split_rest(value):
+    high, low = split(value)
+    rest = (value - high.astype(F32) - low.astype(F32)).astype(BF16)
+    return high, low, rest
+
+
+def dot6(weight, value):
+    rows = weight.shape[0] // 3
+    first = dot(weight, value[0])
+    second = dot(weight[: 2 * rows], value[1])
+    third = first[2 * rows :] + second[rows:] + dot(weight[:rows], value[2])
+    return first[:rows] + ((first[rows : 2 * rows] + second[:rows]) + third)
+
+
 def wide(column, blocks):
     return jnp.concatenate([column] * blocks, axis=1)
 
@@ -81,6 +101,22 @@
 def stack_join(value):
     high, low = split_wide(value)
     return jnp.concatenate([high, low, high], axis=0).astype(BF16)
+
+
+def split_three(value):
+    high, rest = split_wide(value)
+    middle, low = split_wide(rest)
+    return high, middle, low
+
+
+def stack_join_three(value):
+    high, middle, low = split_three(value)
+    return jnp.concatenate([high, middle, low, high, middle, high], axis=0).astype(BF16)
+
+
+def stack_weight_three(value):
+    high, middle, low = split_three(value)
+    return jnp.transpose(jnp.concatenate([high, high, high, middle, middle, low], axis=0)).astype(BF16)
 
 
 def stack_weight(value):
@@ -464,6 +500,12 @@
         send[p, at : at + 8, :] = sums
 
 
+def halvings(peers):
+    bits = list(range(1, (peers - 1).bit_length()))
+    turn = len(bits) // 2
+    return bits, bits[turn:] + bits[:turn]
+
+
 def actor_kernel(
     peers,
     core_ref,
@@ -479,7 +521,6 @@
     one,
     two,
     back,
-    head,
     head_back,
     entry,
     bias_two,
@@ -492,6 +533,9 @@
     acc_side,
     acc_out,
     acc_row,
+    actor_first,
+    actor_second,
+    actor_head,
 ):
     count = jnp.max(count_ref[...].astype(F32)).astype(jnp.int32)
     alpha = jnp.exp(temper_ref[...])
@@ -500,10 +544,10 @@
     width = blocks * LANES
     given = columns(small[REST_ROW : REST_ROW + 8, :])
     final = small[HEAD_ROW : HEAD_ROW + HEAD, :]
-    store_split(two, 0, 0.5 * actor_w2[...])
+    store_three(actor_second, 0.5 * actor_w2[...])
     store_split(back, 0, jnp.transpose(0.5 * actor_w2[...]))
     bias_two[0] = given[0]
-    one[0] = stack_weight(0.5 * small[0:JOIN, :])
+    actor_first[...] = stack_weight_three(0.5 * small[0:JOIN, :])
     for k in range(2):
         first = (1 + k) * JOIN
         one[1 + k] = stack_weight(0.5 * small[first : first + JOIN, :])
@@ -512,7 +556,7 @@
         bias_two[1 + k] = given[1 + k]
         last[k] = given[3 + k]
         store_split(back, 1 + k, back_weights(critic_w2[k], last[k]))
-    store_split(head, 0, final)
+    store_three(actor_head, final)
     head_back[...] = stack_weight(0.5 * final)
     wide_bias[...] = small[BIAS_ROW : BIAS_ROW + HEAD, 0:LANES]
     critic_b3 = [small[BIAS_ROW + k : BIAS_ROW + k + 1, LANES : LANES + 1] for k in range(2)]
@@ -533,18 +577,18 @@
         fill_join(join.at[lane], states, noise_now, first)
         noise = join[lane, 16:24, :]
         tail = jnp.where(inside, 0.0, noise)
-        given = stack_join(jnp.concatenate([join[lane, 0:16, :], tail], axis=0))
-        half = dot(one[0], given)
+        given = stack_join_three(jnp.concatenate([join[lane, 0:16, :], tail], axis=0))
+        half = dot(actor_first[...], given)
         yield "vpu", 160
         hidden, slope_one = activate_slope(half)
-        hidden_one = split(hidden)
-        yield "mxu", 192
-        half = dot3_joint(pair(two, 0), hidden_one)
+        hidden_one = split_rest(hidden)
+        yield "mxu", 384
+        half = dot6(actor_second[...], hidden_one)
         yield "vpu", 170
         hidden, slope_two = activate_slope(half + wide(bias_two[0], blocks))
-        hidden_two = split(hidden)
-        yield "mxu", 128
-        out = dot3_joint(pair(head, 0), hidden_two)
+        hidden_two = split_rest(hidden)
+        yield "mxu", 192
+        out = dot6(actor_head[...], hidden_two)
         yield "vpu", 100
         action, logp, spread, bend = squash(out + wide(wide_bias[...], blocks), noise)
         acc_row[0:1, :] += known["mask"] * (logp + ENTROPY_AIM)
@@ -637,9 +681,12 @@
     )
     acc_side[...] = joined
     core = core_ref[0]
+    orders = halvings(peers)
     for side, part in ((keep, core), (give, 1 - core)):
         for q in range(peers // 2):
-            mine = pl.ds(pl.multiple_of((2 * q + part) * share, 8), share)
+            chips = [sum(((q >> j) & 1) << (bit - 1) for j, bit in enumerate(order)) for order in orders]
+            chip = chips[0] + part * (chips[1] - chips[0])
+            mine = pl.ds(pl.multiple_of((2 * chip + part) * share, 8), share)
             side[q, 0:share, :] = acc_two[mine, 0:LANES]
             side[q, share : 2 * share, :] = acc_two[mine, LANES : 2 * LANES]
             side[q, 2 * share : 3 * share, :] = acc_side[mine, :]
@@ -840,7 +887,6 @@
             pltpu.VMEM((3, HID, 3 * JOIN), BF16),
             pltpu.VMEM((3, 2, HID, HID), BF16),
             pltpu.VMEM((3, 2, HID, HID), BF16),
-            pltpu.VMEM((1, 2, HEAD, HID), BF16),
             pltpu.VMEM((HID, 3 * HEAD), BF16),
             pltpu.VMEM((2, 2, 16, HID), BF16),
             pltpu.VMEM((3, HID, LANES), F32),
@@ -853,6 +899,9 @@
             pltpu.VMEM((HID, LANES), F32),
             pltpu.VMEM((HEAD, LANES), F32),
             pltpu.VMEM((8, ACTOR_BLOCKS * LANES), F32),
+            pltpu.VMEM((HID, 6 * JOIN), BF16),
+            pltpu.VMEM((3 * HID, HID), BF16),
+            pltpu.VMEM((3 * HEAD, HID), BF16),
         ],
         compiler_params=pltpu.CompilerParams(vmem_limit_bytes=ACTOR_LIMIT),
         cost_estimate=pl.CostEstimate(flops=20 * 10**9, bytes_accessed=4 * 10**6, transcendentals=10**7),
@@ -872,18 +921,21 @@
     best_in = best
     agents = lax.axis_size("seed")
     spans = (agents - 1).bit_length()
-    bits = (peers - 1).bit_length()
+    orders = halvings(peers)
     actor_in = lax.ppermute(given, "dp", [(k, k ^ 1) for k in range(peers)])
-    for bit in range(1, max(bits, 1 + spans)):
-        if bit < bits:
+    for step in range(max(len(orders[0]), spans)):
+        if step < len(orders[0]):
             both = (kept + actor_in).reshape(-1, 2, actor_rows, LANES)
-            mine = (me >> bit) & 1
+            first, second = orders[0][step], orders[1][step]
+            mine = jnp.where(me % 2 == 0, me >> first, me >> second) & 1
             kept = lax.dynamic_index_in_dim(both, mine, 1, False)
             given = lax.dynamic_index_in_dim(both, 1 - mine, 1, False)
-            actor_in = lax.ppermute(given, "dp", [(k, k ^ (1 << bit)) for k in range(peers)])
-        if bit <= spans:
+            pairs = [(k, k ^ (1 << (second if k % 2 else first))) for k in range(peers)]
+            actor_in = lax.ppermute(given, "dp", pairs)
+        if step < spans:
             best = jnp.maximum(best, best_in)
-            best_in = lax.ppermute(best, "seed", [(k, k ^ (1 << (bit - 1))) for k in range(agents)])
+            far = 1 << (spans - 1 - step)
+            best_in = lax.ppermute(best, "seed", [(k, k ^ far) for k in range(agents)])
         actor_in, best_in = lax.optimization_barrier((actor_in, best_in))
     actor_parts, bests = (kept[0], actor_in[0]), (best, best_in)
     shape = jax.ShapeDtypeStruct

time: 70.9 us -> 73.2 us (1.032)
  Pallas kernels: 27.8 us -> 29 us
    pallas_call x1, Pallas kernels: 11.3 us -> 12.6 us  [shards(): pl.pallas_call(functools.partial(actor_kernel, peers), out_shape=(jax.Sha...]
  transfers between devices with their start and end apart: 6 -> 6, of which waited for: 4 -> 4; matrix products, arithmetic and copies ran while one was open for 0% -> 0% of each run, Pallas kernels for 16% -> 17%
where the time goes in v5:
time: 73.2 us; the launch traced here: 72.9 us
  starting transfers between devices  34.7 us (47%)
  Pallas kernels  29 us (40%)
  waiting for transfers between devices  6.87 us (9%)
  between operations  2.2 us (3%)
    all_to_all x1, starting transfers between devices, shards(): lax.all_to_all(critic_send, 'dp', split_axis=0, concat_axis=0, tiled=True)  17.2 us
    pallas_call x1, Pallas kernels, shards(): pl.pallas_call(functools.partial(critic_kernel, peers), out_shape=(jax.Sh...  15.6 us
    ppermute x2, starting transfers between devices, shards(): actor_in = lax.ppermute(given, 'dp', pairs)  14.7 us
    pallas_call x1, Pallas kernels, shards(): pl.pallas_call(functools.partial(actor_kernel, peers), out_shape=(jax.Sha...  12.6 us
    ppermute x2, waiting for transfers between devices, shards(): best_in = lax.ppermute(best, 'seed', [(k, k ^ far) for k in range(agents)])  3.89 us
    ppermute x2, starting transfers between devices, shards(): best_in = lax.ppermute(best, 'seed', [(k, k ^ far) for k in range(agents)])  2.24 us
    ppermute x2, waiting for transfers between devices, shards(): actor_in = lax.ppermute(given, 'dp', pairs)  1.91 us
  transfers between devices with their start and end apart: 6, of which 4 were waited for; matrix products, arithmetic and copies ran while one was open for 0% of the time, Pallas kernels for 17%

profile of v5, /device:TPU:0, one launch (start us, length us, event | category | flops | bytes accessed | tf_op | source)
XLA Modules:
  0.0 72.9 jit_solution(17338855078177328105)
XLA Ops:
  1.9 15.6 %critic.1 = (f32[8,200,128]{2,1,0:T(8,128)}, f32[112,256]{1,0:T(8,128)}) custom-call(s32[1,1]{1,0:T(1,128)S(6)} %copy.50.refs_0_.count_ref, f32[1,1]{1,0:T(1,128)} %bitcast.57.refs_1_, f32[1,12]{1,0:T(1,128)} %refs_2_.1, f32[1,2]{1,0:T(1,128)} %refs_3_.1, f32[1,2]{1,0:T(1,128)} %refs_4_.1, f32[17,1,256]{2,1,0:T(1,128)} %bitcast.80, f32[1,256]{1,0:T(1,128)} %refs_6_.1, ...), custom_call_target="tpu_custom_call" | custom-call | flops 20000000000 | bytes 4000000 | tf_op jit(solution)/shard_map/critic/pallas_call | solution.py:847
  17.6 0.0 copy-start.1
  17.6 0.0 copy-start.2
  17.6 0.0 copy-start.3
  17.6 0.0 copy-start.4
  17.6 0.0 copy-start.5
  17.6 17.2 %all-to-all-start = ((f32[8,200,128]{2,1,0:T(8,128)}), f32[8,200,128]{2,1,0:T(8,128)S(1)}, u32[]{:S(2)}, u32[]{:S(2)}) async-start(f32[8,200,128]{2,1,0:T(8,128)} %get-tuple-element.38), calls=%async_computation | async-start | bytes 1638400 | tf_op jit(solution)/shard_map/all_to_all | solution.py:880
  34.9 0.0 copy-done.1
  34.9 0.0 copy-done.2
  34.9 0.0 copy-done.3
  34.9 0.0 copy-done.4
  34.9 0.0 copy-done.5
  34.9 12.6 %actor.1 = (f32[4,96,128]{2,1,0:T(8,128)S(1)}, f32[4,96,128]{2,1,0:T(8,128)S(1)}) custom-call(s32[1]{0:T(128)} %bitcast.26.core_ref, s32[1,1]{1,0:T(1,128)S(6)} %copy.50.refs_0_.count_ref, f32[1,1]{1,0:T(1,128)} %bitcast.58.temper_ref, f32[544,128]{1,0:T(8,128)S(1)} %bitcast.64, f32[192,128]{1,0:T(8,128)S(1)} %bitcast.67, f32[112,256]{1,0:T(8,128)S(1)} %copy-done.5, ...), custom_call_target="tpu_custom_call" | custom-call | flops 20000000000 | bytes 4000000 | tf_op jit(solution)/shard_map/actor/pallas_call | solution.py:881
  47.5 0.6 collective-permute-start
  48.1 1.1 %collective-permute-done = f32[4,96,128]{2,1,0:T(8,128)S(1)} collective-permute-done((f32[4,96,128]{2,1,0:T(8,128)S(1)}, f32[4,96,128]{2,1,0:T(8,128)S(1)}, u32[]{:S(2)}, u32[]{:S(2)}) %collective-permute-start) | collective-permute-done | bytes 196640 | tf_op jit(solution)/shard_map/ppermute | solution.py:925
  49.2 13.1 %collective-permute-start.1 = (f32[2,96,128]{2,1,0:T(8,128)S(1)}, f32[2,96,128]{2,1,0:T(8,128)S(1)}, u32[]{:S(2)}, u32[]{:S(2)}) collective-permute-start(f32[2,96,128]{2,1,0:T(8,128)S(1)} %dynamic-slice_bitcast_fusion), channel_id=1, source_target_pairs={{0,2},{1,5},{2,0},{3,7},{4,6},{5,1},{6,4},{7,3},{8,10},{9,13},{10,... | collective-permute-start | bytes 294920 | tf_op jit(solution)/shard_map/ppermute | solution.py:934
  62.4 0.0 all-to-all-done.critic_in
  62.4 0.7 collective-permute-start.2
  63.1 1.9 %collective-permute-done.1 = f32[2,96,128]{2,1,0:T(8,128)S(1)} collective-permute-done((f32[2,96,128]{2,1,0:T(8,128)S(1)}, f32[2,96,128]{2,1,0:T(8,128)S(1)}, u32[]{:S(2)}, u32[]{:S(2)}) %collective-permute-start.1) | collective-permute-done | bytes 98336 | tf_op jit(solution)/shard_map/ppermute | solution.py:934
  65.0 1.9 %collective-permute-done.2 = f32[1,128]{1,0:T(1,128)S(1)} collective-permute-done((f32[1,128]{1,0:T(1,128)S(1)}, f32[1,128]{1,0:T(1,128)S(1)}, u32[]{:S(2)}, u32[]{:S(2)}) %collective-permute-start.2) | collective-permute-done | bytes 544 | tf_op jit(solution)/shard_map/ppermute | solution.py:938
  66.9 0.0 copy-start
  66.9 1.5 %collective-permute-start.3 = (f32[1,96,128]{2,1,0:T(8,128)S(1)}, f32[1,96,128]{2,1,0:T(8,128)S(1)}, u32[]{:S(2)}, u32[]{:S(2)}) collective-permute-start(f32[1,96,128]{2,1,0:T(8,128)S(1)} %get-tuple-element.61), channel_id=1, source_target_pairs={{0,4},{1,3},{2,6},{3,1},{4,0},{5,7},{6,2},{7,5},{8,12},{9,11},{10,... | collective-permute-start | bytes 147464 | tf_op jit(solution)/shard_map/ppermute | solution.py:934
  68.5 1.6 %collective-permute-start.4 = (f32[1,128]{1,0:T(1,128)S(1)}, f32[1,128]{1,0:T(1,128)S(1)}, u32[]{:S(2)}, u32[]{:S(2)}) collective-permute-start(f32[1,128]{1,0:T(1,128)S(1)} %bitcast_maximum_fusion.refs_2_), channel_id=1, source_target_pairs={{0,8},{8,0},{16,24},{24,16},{1,9},{9,1},{17,25},{25,17},{2,10},{10... | collective-permute-start | bytes 1544 | tf_op jit(solution)/shard_map/ppermute | solution.py:938
  70.1 2.0 %collective-permute-done.4.refs_3_ = f32[1,128]{1,0:T(1,128)S(1)} collective-permute-done((f32[1,128]{1,0:T(1,128)S(1)}, f32[1,128]{1,0:T(1,128)S(1)}, u32[]{:S(2)}, u32[]{:S(2)}) %collective-permute-start.4) | collective-permute-done | bytes 544 | tf_op jit(solution)/shard_map/ppermute | solution.py:938
  72.0 0.0 collective-permute-done.3
  72.0 0.0 copy-done
  72.0 0.8 %finish.1 = (f32[17,1,32]{2,1,0:T(1,128)}, f32[1,32]{1,0:T(1,128)}, f32[32,256]{1,0:T(8,128)}, f32[1,32]{1,0:T(1,128)}, f32[12,1,32]{2,1,0:T(1,128)}, /*index=5*...) custom-call(f32[8,200,128]{2,1,0:T(8,128)S(1)} %all-to-all-done.crit, ...), custom_call_target="tpu_custom_call" | custom-call | tf_op jit(solution)/shard_map/finish/pallas_call | solution.py:942
  (6 shorter events, 0.1 us)
Async XLA Ops:
  17.6 17.3 %copy-start.1 = (f32[1,2,256,256]{3,2,1,0:T(8,128)S(1)}, f32[1,2,256,256]{3,2,1,0:T(8,128)}, u32[]{:S(2)}) copy-start(f32[1,2,256,256]{3,2,1,0:T(8,128)} %param.51) | copy-start | bytes 1572868
  17.6 17.3 %copy-start.2 = (f32[1,17,4096]{2,0,1:T(1,128)S(1)}, f32[1,17,4096]{2,0,1:T(1,128)}, u32[]{:S(2)}) copy-start(f32[1,17,4096]{2,0,1:T(1,128)} %param.31) | copy-start | bytes 835588
  17.6 17.3 %copy-start.3 = (f32[1,256,256]{2,1,0:T(8,128)S(1)}, f32[1,256,256]{2,1,0:T(8,128)}, u32[]{:S(2)}) copy-start(f32[1,256,256]{2,1,0:T(8,128)} %param.45) | copy-start | bytes 786436
  17.6 17.3 %copy-start.4 = (f32[1,6,4096]{2,0,1:T(1,128)S(1)}, f32[1,6,4096]{2,0,1:T(1,128)}, u32[]{:S(2)}) copy-start(f32[1,6,4096]{2,0,1:T(1,128)} %param.36) | copy-start | bytes 294916
  17.6 17.3 %copy-start.5 = (f32[112,256]{1,0:T(8,128)S(1)}, f32[112,256]{1,0:T(8,128)}, u32[]{:S(2)}) copy-start(f32[112,256]{1,0:T(8,128)} %get-tuple-element.39.small) | copy-start | bytes 344068
  17.6 44.7 %all-to-all-start = ((f32[8,200,128]{2,1,0:T(8,128)}), f32[8,200,128]{2,1,0:T(8,128)S(1)}, u32[]{:S(2)}, u32[]{:S(2)}) async-start(f32[8,200,128]{2,1,0:T(8,128)} %get-tuple-element.38), calls=%async_computation | async-start | bytes 1638400 | tf_op jit(solution)/shard_map/all_to_all | solution.py:880
  47.5 1.6 %collective-permute-start = (f32[4,96,128]{2,1,0:T(8,128)S(1)}, f32[4,96,128]{2,1,0:T(8,128)S(1)}, u32[]{:S(2)}, u32[]{:S(2)}) collective-permute-start(f32[4,96,128]{2,1,0:T(8,128)S(1)} %get-tuple-element.41), channel_id=1, source_target_pairs={{0,1},{1,0},{2,3},{3,2},{4,5},{5,4},{6,7},{7,6},{8,9},{9,8},{10,11... | collective-permute-start | bytes 589832 | tf_op jit(solution)/shard_map/ppermute | solution.py:925
  49.2 15.7 %collective-permute-start.1 = (f32[2,96,128]{2,1,0:T(8,128)S(1)}, f32[2,96,128]{2,1,0:T(8,128)S(1)}, u32[]{:S(2)}, u32[]{:S(2)}) collective-permute-start(f32[2,96,128]{2,1,0:T(8,128)S(1)} %dynamic-slice_bitcast_fusion), channel_id=1, source_target_pairs={{0,2},{1,5},{2,0},{3,7},{4,6},{5,1},{6,4},{7,3},{8,10},{9,13},{10,... | collective-permute-start | bytes 294920 | tf_op jit(solution)/shard_map/ppermute | solution.py:934
  62.4 4.5 %collective-permute-start.2 = (f32[1,128]{1,0:T(1,128)S(1)}, f32[1,128]{1,0:T(1,128)S(1)}, u32[]{:S(2)}, u32[]{:S(2)}) collective-permute-start(f32[1,128]{1,0:T(1,128)S(1)} %bitcast.70), channel_id=1, source_target_pairs={{0,16},{8,24},{16,0},{24,8},{1,17},{9,25},{17,1},{25,9},{2,18},{10... | collective-permute-start | bytes 1544 | tf_op jit(solution)/shard_map/ppermute | solution.py:938
  66.9 5.1 %copy-start = (f32[1,4096]{1,0:T(1,128)S(1)}, f32[1,4096]{1,0:T(1,128)}, u32[]{:S(2)}) copy-start(f32[1,4096]{1,0:T(1,128)} %param.42) | copy-start | bytes 49156
  66.9 5.1 %collective-permute-start.3 = (f32[1,96,128]{2,1,0:T(8,128)S(1)}, f32[1,96,128]{2,1,0:T(8,128)S(1)}, u32[]{:S(2)}, u32[]{:S(2)}) collective-permute-start(f32[1,96,128]{2,1,0:T(8,128)S(1)} %get-tuple-element.61), channel_id=1, source_target_pairs={{0,4},{1,3},{2,6},{3,1},{4,0},{5,7},{6,2},{7,5},{8,12},{9,11},{10,... | collective-permute-start | bytes 147464 | tf_op jit(solution)/shard_map/ppermute | solution.py:934
  68.5 3.5 %collective-permute-start.4 = (f32[1,128]{1,0:T(1,128)S(1)}, f32[1,128]{1,0:T(1,128)S(1)}, u32[]{:S(2)}, u32[]{:S(2)}) collective-permute-start(f32[1,128]{1,0:T(1,128)S(1)} %bitcast_maximum_fusion.refs_2_), channel_id=1, source_target_pairs={{0,8},{8,0},{16,24},{24,16},{1,9},{9,1},{17,25},{25,17},{2,10},{10... | collective-permute-start | bytes 1544 | tf_op jit(solution)/shard_map/ppermute | solution.py:938

commit v6 on v5

--- a/solution.py
+++ b/solution.py
@@ -32,7 +32,7 @@
 BIAS_ROW = REST_ROW + 8
 SMALL = BIAS_ROW + 16
 HEAD = 16
-CRITIC_BLOCKS, CRITIC_STREAMS, CRITIC_LAG = 4, 4, 2000
+CRITIC_BLOCKS, CRITIC_STREAMS, CRITIC_LAG = 4, 4, 2600
 ACTOR_BLOCKS, ACTOR_STREAMS = 8, 2
 SOURCES = 29
 CRITIC_LIMIT = 56 * 1024 * 1024
@@ -92,6 +92,11 @@
     second = dot(weight[: 2 * rows], value[1])
     third = first[2 * rows :] + second[rows:] + dot(weight[:rows], value[2])
     return first[:rows] + ((first[rows : 2 * rows] + second[:rows]) + third)
+
+
+def sum_parts(value):
+    rows = value.shape[0] // 2
+    return value[:rows] + value[rows:]
 
 
 def wide(column, blocks):
@@ -614,11 +619,11 @@
         yield "vpu", 90
         grad_one = split(half * slope_one)
         yield "mxu", 128
-        acc_head[...] += dot_t(hidden_two[0], outs[:32]) + dot_t(hidden_two[1], outs[:32])
+        acc_head[...] += sum_parts(dot_t(jnp.concatenate(hidden_two[:2], axis=0), outs[:32]))
         yield "mxu", 192
         acc_two[...] += dot3_t(grad_two, hidden_one)
         yield "mxu", 128
-        acc_one[...] += dot_t(grad_one[0], given[:48]) + dot_t(grad_one[1], given[:48])
+        acc_one[...] += sum_parts(dot_t(jnp.concatenate(grad_one, axis=0), given[:48]))
 
     def critic(first, known, k):
         yield None, "fresh"

time: 73.2 us -> 73 us (level)
  waiting for transfers between devices: 6.87 us -> 4.56 us
  starting transfers between devices: 34.7 us -> 36.9 us
    ppermute x2, starting transfers between devices: 2.24 us -> 15.1 us  [shards(): best_in = lax.ppermute(best, 'seed', [(k, k ^ far) for k in range(agents)])]
    ppermute x2, starting transfers between devices: 14.7 us -> 4.04 us  [shards(): actor_in = lax.ppermute(given, 'dp', pairs)]
    ppermute x2, waiting for transfers between devices: 1.91 us -> 0.01 us  [shards(): actor_in = lax.ppermute(given, 'dp', pairs)]
  transfers between devices with their start and end apart: 6 -> 6, of which waited for: 4 -> 3; matrix products, arithmetic and copies ran while one was open for 0% -> 0% of each run, Pallas kernels for 17% -> 17%
where the time goes in v6:
time: 73 us; the launch traced here: 72.8 us
  starting transfers between devices  36.9 us (51%)
  Pallas kernels  29 us (40%)
  waiting for transfers between devices  4.56 us (6%)
  between operations  2.2 us (3%)
    all_to_all x1, starting transfers between devices, shards(): lax.all_to_all(critic_send, 'dp', split_axis=0, concat_axis=0, tiled=True)  17.2 us
    pallas_call x1, Pallas kernels, shards(): pl.pallas_call(functools.partial(critic_kernel, peers), out_shape=(jax.Sh...  15.6 us
    ppermute x2, starting transfers between devices, shards(): best_in = lax.ppermute(best, 'seed', [(k, k ^ far) for k in range(agents)])  15.1 us
    pallas_call x1, Pallas kernels, shards(): pl.pallas_call(functools.partial(actor_kernel, peers), out_shape=(jax.Sha...  12.6 us
    ppermute x2, starting transfers between devices, shards(): actor_in = lax.ppermute(given, 'dp', pairs)  4.04 us
    ppermute x2, waiting for transfers between devices, shards(): best_in = lax.ppermute(best, 'seed', [(k, k ^ far) for k in range(agents)])  3.48 us
  transfers between devices with their start and end apart: 6, of which 3 were waited for; matrix products, arithmetic and copies ran while one was open for 0% of the time, Pallas kernels for 17%

profile of v6, /device:TPU:0, one launch (start us, length us, event | category | flops | bytes accessed | tf_op | source)
XLA Modules:
  0.0 72.8 jit_solution(16915728313128526206)
XLA Ops:
  1.9 15.6 %critic.1 = (f32[8,200,128]{2,1,0:T(8,128)}, f32[112,256]{1,0:T(8,128)}) custom-call(s32[1,1]{1,0:T(1,128)S(6)} %copy.50.refs_0_.count_ref, f32[1,1]{1,0:T(1,128)} %bitcast.57.refs_1_, f32[1,12]{1,0:T(1,128)} %refs_2_.1, f32[1,2]{1,0:T(1,128)} %refs_3_.1, f32[1,2]{1,0:T(1,128)} %refs_4_.1, f32[17,1,256]{2,1,0:T(1,128)} %bitcast.80, f32[1,256]{1,0:T(1,128)} %refs_6_.1, ...), custom_call_target="tpu_custom_call" | custom-call | flops 20000000000 | bytes 4000000 | tf_op jit(solution)/shard_map/critic/pallas_call | solution.py:852
  17.5 0.0 copy-start.1
  17.6 0.0 copy-start.2
  17.6 0.0 copy-start.3
  17.6 0.0 copy-start.4
  17.6 0.0 copy-start.5
  17.6 17.2 %all-to-all-start = ((f32[8,200,128]{2,1,0:T(8,128)}), f32[8,200,128]{2,1,0:T(8,128)S(1)}, u32[]{:S(2)}, u32[]{:S(2)}) async-start(f32[8,200,128]{2,1,0:T(8,128)} %get-tuple-element.38), calls=%async_computation | async-start | bytes 1638400 | tf_op jit(solution)/shard_map/all_to_all | solution.py:885
  34.8 0.0 copy-done.1
  34.8 0.0 copy-done.2
  34.8 0.0 copy-done.3
  34.8 0.0 copy-done.4
  34.8 0.0 copy-done.5
  34.8 12.6 %actor.1 = (f32[4,96,128]{2,1,0:T(8,128)S(1)}, f32[4,96,128]{2,1,0:T(8,128)S(1)}) custom-call(s32[1]{0:T(128)} %bitcast.26.core_ref, s32[1,1]{1,0:T(1,128)S(6)} %copy.50.refs_0_.count_ref, f32[1,1]{1,0:T(1,128)} %bitcast.58.temper_ref, f32[544,128]{1,0:T(8,128)S(1)} %bitcast.64, f32[192,128]{1,0:T(8,128)S(1)} %bitcast.67, f32[112,256]{1,0:T(8,128)S(1)} %copy-done.5, ...), custom_call_target="tpu_custom_call" | custom-call | flops 20000000000 | bytes 4000000 | tf_op jit(solution)/shard_map/actor/pallas_call | solution.py:886
  47.4 0.6 collective-permute-start
  48.0 1.1 %collective-permute-done = f32[4,96,128]{2,1,0:T(8,128)S(1)} collective-permute-done((f32[4,96,128]{2,1,0:T(8,128)S(1)}, f32[4,96,128]{2,1,0:T(8,128)S(1)}, u32[]{:S(2)}, u32[]{:S(2)}) %collective-permute-start) | collective-permute-done | bytes 196640 | tf_op jit(solution)/shard_map/ppermute | solution.py:930
  49.1 2.0 %collective-permute-start.1 = (f32[2,96,128]{2,1,0:T(8,128)S(1)}, f32[2,96,128]{2,1,0:T(8,128)S(1)}, u32[]{:S(2)}, u32[]{:S(2)}) collective-permute-start(f32[2,96,128]{2,1,0:T(8,128)S(1)} %dynamic-slice_bitcast_fusion), channel_id=1, source_target_pairs={{0,2},{1,5},{2,0},{3,7},{4,6},{5,1},{6,4},{7,3},{8,10},{9,13},{10,... | collective-permute-start | bytes 294920 | tf_op jit(solution)/shard_map/ppermute | solution.py:939
  51.1 0.0 all-to-all-done.critic_in
  51.1 13.6 %collective-permute-start.2 = (f32[1,128]{1,0:T(1,128)S(1)}, f32[1,128]{1,0:T(1,128)S(1)}, u32[]{:S(2)}, u32[]{:S(2)}) collective-permute-start(f32[1,128]{1,0:T(1,128)S(1)} %bitcast.70), channel_id=1, source_target_pairs={{0,16},{8,24},{16,0},{24,8},{1,17},{9,25},{17,1},{25,9},{2,18},{10... | collective-permute-start | bytes 1544 | tf_op jit(solution)/shard_map/ppermute | solution.py:943
  64.7 0.0 collective-permute-done.1
  64.7 1.5 %collective-permute-done.2 = f32[1,128]{1,0:T(1,128)S(1)} collective-permute-done((f32[1,128]{1,0:T(1,128)S(1)}, f32[1,128]{1,0:T(1,128)S(1)}, u32[]{:S(2)}, u32[]{:S(2)}) %collective-permute-start.2) | collective-permute-done | bytes 544 | tf_op jit(solution)/shard_map/ppermute | solution.py:943
  66.2 0.0 copy-start
  66.2 2.1 %collective-permute-start.3 = (f32[1,96,128]{2,1,0:T(8,128)S(1)}, f32[1,96,128]{2,1,0:T(8,128)S(1)}, u32[]{:S(2)}, u32[]{:S(2)}) collective-permute-start(f32[1,96,128]{2,1,0:T(8,128)S(1)} %get-tuple-element.61), channel_id=1, source_target_pairs={{0,4},{1,3},{2,6},{3,1},{4,0},{5,7},{6,2},{7,5},{8,12},{9,11},{10,... | collective-permute-start | bytes 147464 | tf_op jit(solution)/shard_map/ppermute | solution.py:939
  68.3 1.6 %collective-permute-start.4 = (f32[1,128]{1,0:T(1,128)S(1)}, f32[1,128]{1,0:T(1,128)S(1)}, u32[]{:S(2)}, u32[]{:S(2)}) collective-permute-start(f32[1,128]{1,0:T(1,128)S(1)} %bitcast_maximum_fusion.refs_2_), channel_id=1, source_target_pairs={{0,8},{8,0},{16,24},{24,16},{1,9},{9,1},{17,25},{25,17},{2,10},{10... | collective-permute-start | bytes 1544 | tf_op jit(solution)/shard_map/ppermute | solution.py:943
  69.9 2.0 %collective-permute-done.4.refs_3_ = f32[1,128]{1,0:T(1,128)S(1)} collective-permute-done((f32[1,128]{1,0:T(1,128)S(1)}, f32[1,128]{1,0:T(1,128)S(1)}, u32[]{:S(2)}, u32[]{:S(2)}) %collective-permute-start.4) | collective-permute-done | bytes 544 | tf_op jit(solution)/shard_map/ppermute | solution.py:943
  71.9 0.0 collective-permute-done.3
  71.9 0.0 copy-done
  71.9 0.8 %finish.1 = (f32[17,1,32]{2,1,0:T(1,128)}, f32[1,32]{1,0:T(1,128)}, f32[32,256]{1,0:T(8,128)}, f32[1,32]{1,0:T(1,128)}, f32[12,1,32]{2,1,0:T(1,128)}, /*index=5*...) custom-call(f32[8,200,128]{2,1,0:T(8,128)S(1)} %all-to-all-done.crit, ...), custom_call_target="tpu_custom_call" | custom-call | tf_op jit(solution)/shard_map/finish/pallas_call | solution.py:947
  (6 shorter events, 0.1 us)
Async XLA Ops:
  17.5 17.3 %copy-start.1 = (f32[1,2,256,256]{3,2,1,0:T(8,128)S(1)}, f32[1,2,256,256]{3,2,1,0:T(8,128)}, u32[]{:S(2)}) copy-start(f32[1,2,256,256]{3,2,1,0:T(8,128)} %param.51) | copy-start | bytes 1572868
  17.6 17.3 %copy-start.2 = (f32[1,17,4096]{2,0,1:T(1,128)S(1)}, f32[1,17,4096]{2,0,1:T(1,128)}, u32[]{:S(2)}) copy-start(f32[1,17,4096]{2,0,1:T(1,128)} %param.31) | copy-start | bytes 835588
  17.6 17.3 %copy-start.3 = (f32[1,256,256]{2,1,0:T(8,128)S(1)}, f32[1,256,256]{2,1,0:T(8,128)}, u32[]{:S(2)}) copy-start(f32[1,256,256]{2,1,0:T(8,128)} %param.45) | copy-start | bytes 786436
  17.6 17.3 %copy-start.4 = (f32[1,6,4096]{2,0,1:T(1,128)S(1)}, f32[1,6,4096]{2,0,1:T(1,128)}, u32[]{:S(2)}) copy-start(f32[1,6,4096]{2,0,1:T(1,128)} %param.36) | copy-start | bytes 294916
  17.6 17.3 %copy-start.5 = (f32[112,256]{1,0:T(8,128)S(1)}, f32[112,256]{1,0:T(8,128)}, u32[]{:S(2)}) copy-start(f32[112,256]{1,0:T(8,128)} %get-tuple-element.39.small) | copy-start | bytes 344068
  17.6 33.5 %all-to-all-start = ((f32[8,200,128]{2,1,0:T(8,128)}), f32[8,200,128]{2,1,0:T(8,128)S(1)}, u32[]{:S(2)}, u32[]{:S(2)}) async-start(f32[8,200,128]{2,1,0:T(8,128)} %get-tuple-element.38), calls=%async_computation | async-start | bytes 1638400 | tf_op jit(solution)/shard_map/all_to_all | solution.py:885
  47.4 1.6 %collective-permute-start = (f32[4,96,128]{2,1,0:T(8,128)S(1)}, f32[4,96,128]{2,1,0:T(8,128)S(1)}, u32[]{:S(2)}, u32[]{:S(2)}) collective-permute-start(f32[4,96,128]{2,1,0:T(8,128)S(1)} %get-tuple-element.41), channel_id=1, source_target_pairs={{0,1},{1,0},{2,3},{3,2},{4,5},{5,4},{6,7},{7,6},{8,9},{9,8},{10,11... | collective-permute-start | bytes 589832 | tf_op jit(solution)/shard_map/ppermute | solution.py:930
  49.1 15.5 %collective-permute-start.1 = (f32[2,96,128]{2,1,0:T(8,128)S(1)}, f32[2,96,128]{2,1,0:T(8,128)S(1)}, u32[]{:S(2)}, u32[]{:S(2)}) collective-permute-start(f32[2,96,128]{2,1,0:T(8,128)S(1)} %dynamic-slice_bitcast_fusion), channel_id=1, source_target_pairs={{0,2},{1,5},{2,0},{3,7},{4,6},{5,1},{6,4},{7,3},{8,10},{9,13},{10,... | collective-permute-start | bytes 294920 | tf_op jit(solution)/shard_map/ppermute | solution.py:939
  51.1 15.1 %collective-permute-start.2 = (f32[1,128]{1,0:T(1,128)S(1)}, f32[1,128]{1,0:T(1,128)S(1)}, u32[]{:S(2)}, u32[]{:S(2)}) collective-permute-start(f32[1,128]{1,0:T(1,128)S(1)} %bitcast.70), channel_id=1, source_target_pairs={{0,16},{8,24},{16,0},{24,8},{1,17},{9,25},{17,1},{25,9},{2,18},{10... | collective-permute-start | bytes 1544 | tf_op jit(solution)/shard_map/ppermute | solution.py:943
  66.2 5.7 %copy-start = (f32[1,4096]{1,0:T(1,128)S(1)}, f32[1,4096]{1,0:T(1,128)}, u32[]{:S(2)}) copy-start(f32[1,4096]{1,0:T(1,128)} %param.42) | copy-start | bytes 49156
  66.2 5.6 %collective-permute-start.3 = (f32[1,96,128]{2,1,0:T(8,128)S(1)}, f32[1,96,128]{2,1,0:T(8,128)S(1)}, u32[]{:S(2)}, u32[]{:S(2)}) collective-permute-start(f32[1,96,128]{2,1,0:T(8,128)S(1)} %get-tuple-element.61), channel_id=1, source_target_pairs={{0,4},{1,3},{2,6},{3,1},{4,0},{5,7},{6,2},{7,5},{8,12},{9,11},{10,... | collective-permute-start | bytes 147464 | tf_op jit(solution)/shard_map/ppermute | solution.py:939
  68.3 3.5 %collective-permute-start.4 = (f32[1,128]{1,0:T(1,128)S(1)}, f32[1,128]{1,0:T(1,128)S(1)}, u32[]{:S(2)}, u32[]{:S(2)}) collective-permute-start(f32[1,128]{1,0:T(1,128)S(1)} %bitcast_maximum_fusion.refs_2_), channel_id=1, source_target_pairs={{0,8},{8,0},{16,24},{24,16},{1,9},{9,1},{17,25},{25,17},{2,10},{10... | collective-permute-start | bytes 1544 | tf_op jit(solution)/shard_map/ppermute | solution.py:943
